TPU v7x, 32 devices: a whole 2x2x4 slice. The times are simulated.
32 devices in a mesh: groups: 2 (over y), wide: 4 (over x, core), narrow: 4 (over z).
Axes of the slice: x: 2, y: 2, z: 4, core: 2. Of those that a mesh axis runs over, the one named last changes fastest.
Arguments:
- spectra: bfloat16 [2, 32, 640, 2, 1281], P(None, ('groups', 'wide'), 'narrow'), parts along dimension 1, may hold values from -6 to 6
- legendre: bfloat16 [320, 1281, 128], P('narrow'), may hold values from -0.15625 to 0.15625
- pair_of_slot: int32 [640], replicated, may hold values from 0 to 639, each once
- lat_owner: int32 [128], replicated, may hold values from 0 to 3, as said below
- region_of_lon: int32 [2048], replicated, may hold values from 0 to 63, never falling along the last dimension, each value on 1 to 48 neighbouring positions
Outputs:
- peak: float32 [4, 128, 64], P('groups', 'narrow', 'wide'), parts along dimension 0
- peak_slope: float32 [4, 128, 64], P('groups', 'narrow', 'wide'), parts along dimension 0
There are 2 independent parts, one for each index of `groups`. A program takes and returns all parts, laid end to end along the dimension named above; an argument that names none is the same for every part. Nothing has to cross between parts.
Inputs may be any that keep to these rules, and one draw needn't show every extreme that they name: `lat_owner`: each index of narrow owns exactly 32 latitudes. `region_of_lon`: regions never fall along the longitudes and every region has at least one longitude. `pair_of_slot`: a permutation.
All inputs are finite; a program needn't handle non-finite values.
Results may differ from a plain program's by a relative error of at most 0.0003.
Values sent between devices are 32-bit elements; how exact they have to be, the bound alone decides.
No kernel may reach another device: no remote copies, remote signals or barrier semaphores. Data moves between devices by JAX's collectives and lax.ppermute only.
A program may use at most 192 MiB of HBM per device.

v0:
```python
import functools
import math

import jax
import jax.numpy as jnp
from jax import lax
from jax.experimental import pallas as pl
from jax.experimental.pallas import tpu as pltpu
from jax.sharding import PartitionSpec as P

REG_DEV = 16
WIDEST_REGION = 48
LANES = 128
PAIRS_UNIT = 8
NB = 32
VMEM = 56 * 2**20
CHUNKS = (1, 2, 3, 2, 2)
STAGES = ((0, 1, 2), (3,), (4,))
F32 = jnp.float32
BF16 = jnp.bfloat16


def synthesize(operand, waves, start, width, top):
    columns = start + jnp.arange(width, dtype=jnp.int32)
    phase = waves[:, None] * columns[None, :] % (4 * top)
    angle = phase.astype(F32) * (2.0 * math.pi / (4 * top))
    cosine = jnp.cos(angle)
    sine = jnp.sin(angle)
    rate = (waves.astype(F32) / top)[:, None]
    upper = jnp.concatenate([cosine, -rate * sine], axis=1)
    lower = jnp.concatenate([-sine, -rate * cosine], axis=1)
    table = jnp.concatenate([upper, lower], axis=0) * top ** (-0.5)
    return jnp.dot(operand, table, precision=lax.Precision.HIGHEST)


def synthesize_all(operand, waves, lon, top):
    width = min(512, lon)
    starts = jnp.arange(lon // width, dtype=jnp.int32) * width
    blocks = lax.map(lambda begin: synthesize(operand, waves, begin, width, top), starts)
    blocks = blocks.reshape(blocks.shape[0], blocks.shape[1], 2, width)
    value = jnp.transpose(blocks[:, :, 0], (1, 0, 2)).reshape(operand.shape[0], lon)
    slope = jnp.transpose(blocks[:, :, 1], (1, 0, 2)).reshape(operand.shape[0], lon)
    return value, slope


def region_peak(values, region_of_lon, wanted):
    hits = region_of_lon[:, None] == wanted[None, :]
    masked = jnp.where(hits[None, None], values[..., None], -1e30)
    return masked.max(axis=2)


def plain(spectra, legendre, pair_of_slot, lat_owner, region_of_lon):
    members, steps_here, slot_count, _, length = spectra.shape
    top = length - 1
    lon = region_of_lon.shape[0]
    half_count = legendre.shape[0]
    lat_half = legendre.shape[2] // 2
    here = lax.axis_index("narrow")
    paired = lax.dynamic_slice_in_dim(pair_of_slot, here * slot_count, slot_count)
    position = jnp.arange(length, dtype=jnp.int32)[None, :]
    first_len = (top - paired)[:, None]
    leading = position < first_len
    offset = jnp.where(leading, position, position - first_len)
    even_term = offset % 2 == 0
    masks = jnp.stack(
        [leading & even_term, leading & ~even_term, ~leading & even_term, ~leading & ~even_term],
        axis=1,
    ).astype(BF16)
    ordered = jnp.transpose(spectra, (2, 0, 1, 3, 4))
    masked = masks[:, :, None, None, None, :] * ordered[:, None]
    masked = masked.reshape(half_count, 2, -1, length)
    table = legendre.reshape(half_count, length, 2, lat_half)
    sums = jnp.einsum("abrl,albj->abrj", masked, table, preferred_element_type=F32)
    sums = sums.reshape(slot_count, 4, members, steps_here, 2, lat_half)
    north_lead = sums[:, 0] + sums[:, 1]
    south_lead = sums[:, 0] - sums[:, 1]
    north_tail = sums[:, 2] + sums[:, 3]
    south_tail = sums[:, 2] - sums[:, 3]
    lead = jnp.concatenate([north_lead, jnp.flip(south_lead, axis=-1)], axis=-1)
    tail = jnp.concatenate([north_tail, jnp.flip(south_tail, axis=-1)], axis=-1)
    waved = jnp.stack([lead, tail], axis=1).reshape(2 * slot_count, members, steps_here, 2, -1)
    order = jnp.argsort(lat_owner, stable=True)
    waved = jnp.take(waved, order, axis=4)
    arrived = lax.all_to_all(waved, "narrow", split_axis=4, concat_axis=0, tiled=True)
    waves = jnp.stack([pair_of_slot, top - 1 - pair_of_slot], axis=1).reshape(-1)
    lat_here = arrived.shape[4]
    operand = jnp.transpose(arrived, (1, 2, 4, 3, 0)).reshape(members * steps_here * lat_here, -1)
    value, slope = synthesize_all(operand, waves, lon, top)
    value = value.reshape(members, steps_here, lat_here, lon).max(axis=1)
    slope = jnp.abs(slope).reshape(members, steps_here, lat_here, lon).max(axis=1)
    wide_count = lax.axis_size("wide")
    mine_start = lax.axis_index("wide") * REG_DEV
    wanted = jnp.arange(REG_DEV * wide_count, dtype=jnp.int32)
    peaks = region_peak(value, region_of_lon, wanted)
    slopes = region_peak(slope, region_of_lon, wanted)
    peaks, slopes = lax.pmax((peaks, slopes), "wide")
    peak = lax.dynamic_slice_in_dim(peaks, mine_start, REG_DEV, 2)
    peak_slope = lax.dynamic_slice_in_dim(slopes, mine_start, REG_DEV, 2)
    return peak, peak_slope


def iota(shape, axis):
    return lax.broadcasted_iota(jnp.int32, shape, axis)


def latitude_lanes(owner, here, parts):
    square = (LANES, LANES)
    row = jnp.broadcast_to(owner.astype(F32), square)
    column = row.T
    first, second = iota(square, 0), iota(square, 1)
    ahead = (column < row) | ((column == row) & (first < second))
    place = jnp.sum(jnp.where(ahead, 1.0, 0.0), axis=0, keepdims=True)
    place = jnp.broadcast_to(place, square).T
    half = LANES // 2
    lane_of = jnp.where(first < half, first, half + LANES - 1 - first).astype(F32)
    share = LANES // parts
    rows = []
    for step in range(parts):
        owner_index = lax.rem(here + step, parts)
        target = (owner_index * share + second % share).astype(F32)
        rows.append(jnp.sum(jnp.where(place == target, lane_of, 0.0), axis=0, keepdims=True))
    return jnp.concatenate(rows, axis=0).astype(jnp.int32)


def legendre_kernel(first_unit, parts, pair_ref, here_ref, owner_ref, s_ref, l_ref, *refs):
    outs, (lanes_ref, table, sums) = refs[:parts], refs[parts:]
    members, steps, slots, _, length = s_ref.shape
    top = length - 1
    times = members * steps
    rows = 2 * times
    unit = pl.program_id(0)
    here = here_ref[0]

    @pl.when(unit == 0)
    def _():
        lanes_ref[...] = latitude_lanes(owner_ref[...], here, parts)

    def turn(i, carry):
        at = pl.multiple_of(i * LANES, LANES)
        table[:, pl.ds(at, LANES), :] = jnp.swapaxes(l_ref[pl.ds(at, LANES)], 0, 1)
        return carry

    lax.fori_loop(0, top // LANES, turn, 0)

    spot = iota((rows, top), 1)
    even = jnp.where(spot % 2 == 0, 1.0, 0.0).astype(BF16)
    base = (here * pl.num_programs(0) * 0) + here * (pair_ref.shape[0] // parts) + (first_unit + unit) * slots
    low = iota((rows, LANES), 1) < LANES // 2
    for pair in range(slots // 2):
        parts_of, last, signs = [], [], []
        for side in range(2):
            slot = 2 * pair + side
            whole = s_ref[:, :, slot].reshape(rows, length)
            x = whole[:, :top]
            last.append(whole[:, top:].astype(F32))
            first_len = top - pair_ref[base + slot]
            lead = x * jnp.where(spot < first_len, 1.0, 0.0).astype(BF16)
            tail = x - lead
            lead_even = lead * even
            tail_even = tail * even
            parts_of += [lead_even, lead - lead_even, tail_even, tail - tail_even]
            signs.append(jnp.where(first_len % 2 == 0, 1.0, -1.0).astype(F32))
        product = jnp.dot(jnp.concatenate(parts_of, axis=0), table[pair], preferred_element_type=F32)
        end = l_ref[top, pair : pair + 1, :].astype(F32)
        for side in range(2):
            at = 4 * side * rows
            lead_even, lead_odd, tail_even, tail_odd = (
                product[at + i * rows : at + (i + 1) * rows] for i in range(4)
            )
            tail_even = tail_even + last[side] * end
            found = (
                (lead_even + lead_odd, lead_even - lead_odd),
                (tail_even + tail_odd, (tail_even - tail_odd) * signs[side]),
            )
            for which, (north, south) in enumerate(found):
                if side == 0:
                    both = jnp.where(low, north, pltpu.roll(south, LANES // 2, 1))
                else:
                    both = jnp.where(low, pltpu.roll(north, LANES // 2, 1), south)
                wave = 2 * (2 * pair + side) + which
                sums[wave * rows : (wave + 1) * rows, :] = both

    waves = 2 * slots
    share = LANES // parts
    per = LANES // share
    group = iota((waves, LANES), 1) // share
    for step in range(parts):
        index = jnp.broadcast_to(lanes_ref[step : step + 1, :], (waves, LANES))
        for part in range(2):
            for block in range(times // per):
                built = None
                for place in range(per):
                    at = block * per + place
                    step_of, member = at // members, at % members
                    row = (member * steps + step_of) * 2 + part
                    source = sums[pl.ds(row, waves, stride=rows), :]
                    moved = jnp.take_along_axis(source, index, axis=1, mode="promise_in_bounds")
                    built = moved if place == 0 else jnp.where(group == place, moved, built)
                outs[step][part, :, block * LANES : (block + 1) * LANES] = built


def legendre_sums(spectra, turned, pair_of_slot, here, owner, first_unit, units, parts):
    members, steps, _, _, length = spectra.shape
    slots = 2 * PAIRS_UNIT
    waves = 2 * slots
    width = members * steps * LANES // parts
    out = jax.ShapeDtypeStruct((2, units * waves, width), F32)
    return pl.pallas_call(
        functools.partial(legendre_kernel, first_unit, parts),
        grid_spec=pltpu.PrefetchScalarGridSpec(
            num_scalar_prefetch=2,
            grid=(units,),
            in_specs=[
                pl.BlockSpec((1, LANES), lambda u, *_: (0, 0)),
                pl.BlockSpec(
                    (members, steps, slots, 2, length), lambda u, *_: (0, 0, first_unit + u, 0, 0)
                ),
                pl.BlockSpec((length, PAIRS_UNIT, LANES), lambda u, *_: (0, first_unit + u, 0)),
            ],
            out_specs=[pl.BlockSpec((2, waves, width), lambda u, *_: (0, u, 0))] * parts,
            scratch_shapes=[
                pltpu.VMEM((parts, LANES), jnp.int32),
                pltpu.VMEM((PAIRS_UNIT, length - 1, LANES), BF16),
                pltpu.VMEM((waves * 2 * members * steps, LANES), F32),
            ],
        ),
        out_shape=[out] * parts,
        compiler_params=pltpu.CompilerParams(vmem_limit_bytes=VMEM),
        name="legendre",
    )(pair_of_slot, here, owner, spectra, turned)


def split(x):
    high = x.astype(BF16)
    return high, (x - high.astype(F32)).astype(BF16)


def synthesis_kernel(counts, fresh, closing, shape, *refs):
    lon, members, regions, wide = shape
    refs = list(refs)
    if closing:
        starts_ref, here_ref = refs.pop(0), refs.pop(0)
    base_ref, coef_ref = refs.pop(0), refs.pop(0)
    pieces = [refs.pop(0) for _ in counts]
    if not fresh:
        cos_in, sin_in = refs.pop(0), refs.pop(0)
    if closing:
        outs = [refs.pop(0) for _ in range(wide)]
    else:
        cos_out, sin_out = refs.pop(0), refs.pop(0)
    w_cos_h, w_cos_l, w_sin_h, w_sin_l, t_cos_h, t_cos_l, t_sin_h, t_sin_l = refs[:8]
    step = pl.program_id(0)
    block = t_cos_h.shape[0]
    width = pieces[0].shape[2]

    @pl.when(step == 0)
    def _():
        at = 0
        for piece, count in zip(pieces, counts):
            span = slice(at, at + count)
            coef = coef_ref[span, :]
            c, s, rate = coef[:, 0:1], coef[:, 1:2], coef[:, 2:3]
            real, imag = piece[0], piece[1]
            p0 = real * c - imag * s
            p1 = real * s + imag * c
            for index, value in enumerate((p0, rate * p1)):
                cols = slice(index * width, (index + 1) * width)
                w_cos_h[span, cols], w_cos_l[span, cols] = split(value)
            for index, value in enumerate((p1, rate * p0)):
                cols = slice(index * width, (index + 1) * width)
                w_sin_h[span, cols], w_sin_l[span, cols] = split(value)
            at += count

    coarse = lon // 2 // NB

    def fill(a, carry):
        row = step * (block // NB) + a
        ca = base_ref[pl.ds(row, 1), :]
        sa = base_ref[pl.ds(coarse + row, 1), :]
        cb = base_ref[2 * coarse : 2 * coarse + NB, :]
        sb = base_ref[2 * coarse + NB : 2 * coarse + 2 * NB, :]
        at = pl.ds(pl.multiple_of(a * NB, NB), NB)
        t_cos_h[at, :], t_cos_l[at, :] = split(ca * cb - sa * sb)
        t_sin_h[at, :], t_sin_l[at, :] = split(sa * cb + ca * sb)
        return carry

    lax.fori_loop(0, block // NB, fill, 0)

    def product(table_h, table_l, weight_h, weight_l):
        dot = functools.partial(jnp.dot, preferred_element_type=F32)
        return (
            dot(table_h[...], weight_h[...])
            + dot(table_l[...], weight_h[...])
            + dot(table_h[...], weight_l[...])
        )

    even = product(t_cos_h, t_cos_l, w_cos_h, w_cos_l)
    odd = product(t_sin_h, t_sin_l, w_sin_h, w_sin_l)
    if not fresh:
        even = even + cos_in[...]
        odd = odd + sin_in[...]
    if not closing:
        cos_out[...] = even
        sin_out[...] = odd
        return

    value_ref, slope_ref, found_v, found_s = refs[8:]
    half = lon // 2

    def narrowed(x):
        return functools.reduce(
            jnp.maximum, [x[:, i : i + LANES] for i in range(0, width, LANES)]
        )

    a, d = even[:, :width], even[:, width:]
    b, c = odd[:, :width], odd[:, width:]
    below = pl.ds(pl.multiple_of(step * block, block), block)
    above = pl.ds(pl.multiple_of(half + step * block, block), block)
    value_ref[below, :] = narrowed(a + b)
    value_ref[above, :] = narrowed(a - b)
    slope_ref[below, :] = narrowed(jnp.abs(c - d))
    slope_ref[above, :] = narrowed(jnp.abs(c + d))

    @pl.when(step == pl.num_programs(0) - 1)
    def _():
        window = (WIDEST_REGION + 15) // 8 * 8
        rows = iota((window, LANES), 0)

        def best(low, high):
            at = pl.multiple_of(jnp.minimum(low // 8 * 8, lon - window), 8)
            inside = (rows >= low - at) & (rows < high - at)
            v = jnp.where(inside, value_ref[pl.ds(at, window), :], -3e38)
            s = jnp.where(inside, slope_ref[pl.ds(at, window), :], -3e38)
            return jnp.max(v, axis=0, keepdims=True), jnp.max(s, axis=0, keepdims=True)

        def one(region, carry):
            begin, end = starts_ref[region], starts_ref[region + 1]
            upper = end > half
            low = jnp.where(upper, jnp.maximum(begin, half), half - end)
            high = jnp.where(upper, end, half - begin)
            v, s = best(low, high)
            found_v[pl.ds(region, 1), :] = v
            found_s[pl.ds(region, 1), :] = s
            return carry

        lax.fori_loop(0, regions, one, 0, unroll=8)
        centre = starts_ref[regions + 1]
        v, s = best(0, half - starts_ref[centre])
        at = pl.ds(centre, 1)
        found_v[at, :] = jnp.maximum(found_v[at, :], v)
        found_s[at, :] = jnp.maximum(found_s[at, :], s)
        values, slopes = found_v[...], found_s[...]
        span = LANES
        while span > LANES // 2:
            span //= 2
            values = jnp.maximum(values, pltpu.roll(values, span, 1))
            slopes = jnp.maximum(slopes, pltpu.roll(slopes, span, 1))
        found_v[...] = jnp.where(iota(values.shape, 1) < LANES // 2, values, slopes)
        for offset in range(wide):
            owner = lax.rem(here_ref[0] + offset, wide)
            start = pl.multiple_of(owner * REG_DEV, REG_DEV)
            outs[offset][...] = found_v[pl.ds(start, REG_DEV), :]


def synthesis(base, coef, pieces, held, closing, lon, members, regions, wide, starts, here):
    block = min(512, lon // 2)
    depth = base.shape[1]
    counts = tuple(piece.shape[1] for piece in pieces)
    width = pieces[0].shape[2]
    fresh = held is None
    prefetch = (starts, here) if closing else ()
    whole = lambda x: pl.BlockSpec(x.shape, lambda i, *_: (0,) * x.ndim)
    strip = pl.BlockSpec((block, 2 * width), lambda i, *_: (i, 0))
    operands = [base, coef, *pieces] + ([] if fresh else list(held))
    in_specs = [whole(x) for x in (base, coef, *pieces)] + ([] if fresh else [strip] * 2)
    scratch = [pltpu.VMEM((depth, 2 * width), BF16)] * 4 + [pltpu.VMEM((block, depth), BF16)] * 4
    if closing:
        out_shape = [jax.ShapeDtypeStruct((REG_DEV, LANES), F32)] * wide
        out_specs = [pl.BlockSpec((REG_DEV, LANES), lambda i, *_: (0, 0))] * wide
        scratch += [pltpu.VMEM((lon, LANES), F32)] * 2 + [pltpu.VMEM((regions, LANES), F32)] * 2
    else:
        out_shape = [jax.ShapeDtypeStruct((lon // 2, 2 * width), F32)] * 2
        out_specs = [strip] * 2
    return pl.pallas_call(
        functools.partial(
            synthesis_kernel, counts, fresh, closing, (lon, members, regions, wide)
        ),
        grid_spec=pltpu.PrefetchScalarGridSpec(
            num_scalar_prefetch=len(prefetch),
            grid=(lon // 2 // block,),
            in_specs=in_specs,
            out_specs=out_specs,
            scratch_shapes=scratch,
        ),
        out_shape=out_shape,
        compiler_params=pltpu.CompilerParams(vmem_limit_bytes=VMEM),
        name="synthesis",
    )(*prefetch, *operands)


def shift(x, axis, count, step):
    return lax.ppermute(x, axis, [(i, (i + step) % count) for i in range(count)])


def turns(numbers, full):
    angle = (numbers % full).astype(F32) * (2.0 * math.pi / full)
    return jnp.cos(angle), jnp.sin(angle)


def kernels(spectra, legendre, pair_of_slot, lat_owner, region_of_lon):
    members, steps, slot_count, _, length = spectra.shape
    top = length - 1
    lon = region_of_lon.shape[0]
    parts = lax.axis_size("narrow")
    wide = lax.axis_size("wide")
    regions = REG_DEV * wide
    here = lax.axis_index("narrow")
    here_wide = lax.axis_index("wide")
    here_ref = here.reshape(1)
    owner = lat_owner.reshape(1, -1)
    turned = jnp.transpose(legendre, (1, 0, 2))

    chunks, first = [], 0
    for units in CHUNKS:
        sums = legendre_sums(
            spectra, turned, pair_of_slot, here_ref, owner, first, units, parts
        )
        chunks.append([sums[0]] + [shift(sums[i], "narrow", parts, i) for i in range(1, parts)])
        final, first = sums[0], first + units
    pair_of_slot, region_of_lon, final = lax.optimization_barrier(
        (pair_of_slot, region_of_lon, final)
    )
    chunks[-1][0] = final

    waves_of = jnp.stack([pair_of_slot, top - 1 - pair_of_slot], axis=1).reshape(parts, -1)
    source = lax.rem(here - jnp.arange(parts, dtype=jnp.int32) + parts, parts)
    waves_of = waves_of[source]
    edges = jnp.arange(regions + 1, dtype=jnp.int32)
    starts = jnp.sum((region_of_lon[None, :] < edges[:, None]).astype(jnp.int32), axis=1)
    starts = jnp.concatenate([starts, region_of_lon[lon // 2 - 1 : lon // 2]])

    per_unit = 4 * PAIRS_UNIT
    bounds = [0]
    for units in CHUNKS:
        bounds.append(bounds[-1] + units * per_unit)
    order = []
    for stage in STAGES:
        for chunk in stage:
            order.append(waves_of[:, bounds[chunk] : bounds[chunk + 1]].reshape(-1))
    waves = jnp.concatenate(order)
    full = 8 * top
    coarse = 2 * NB * jnp.arange(lon // 2 // NB, dtype=jnp.int32)
    fine = 2 * jnp.arange(NB, dtype=jnp.int32) + 1
    ca, sa = turns(coarse[:, None] * waves[None, :], full)
    cb, sb = turns(fine[:, None] * waves[None, :], full)
    base = jnp.concatenate([ca, sa, cb, sb], axis=0)
    c, s = turns((lon - 1) * waves, full)
    scale = top ** (-0.5)
    coef = jnp.stack([c * scale, s * scale, waves.astype(F32) / top] + [c] * 5, axis=1)

    held, at = None, 0
    for number, stage in enumerate(STAGES):
        pieces = [piece for chunk in stage for piece in chunks[chunk]]
        depth = sum(piece.shape[1] for piece in pieces)
        held = synthesis(
            base[:, at : at + depth],
            coef[at : at + depth],
            pieces,
            held,
            number == len(STAGES) - 1,
            lon,
            members,
            regions,
            wide,
            starts,
            here_wide.reshape(1),
        )
        at += depth

    best = held[0]
    for offset in range(1, wide):
        best = jnp.maximum(best, shift(held[offset], "wide", wide, offset))
    best = best.reshape(REG_DEV, 2, members, LANES // 2 // members)
    peak = jnp.transpose(best[:, 0], (1, 2, 0))
    peak_slope = jnp.transpose(best[:, 1], (1, 2, 0))
    return peak, peak_slope


def per_device(spectra, legendre, pair_of_slot, lat_owner, region_of_lon):
    members, steps, _, _, length = spectra.shape
    pairs, _, lanes = legendre.shape
    share = lat_owner.shape[0] // lax.axis_size("narrow")
    fits = (
        pairs == PAIRS_UNIT * sum(CHUNKS)
        and lanes == LANES
        and lat_owner.shape[0] == LANES
        and 2 * members * share == LANES
        and members * steps * share % LANES == 0
        and (length - 1) % LANES == 0
        and region_of_lon.shape[0] % 1024 == 0
    )
    run = kernels if fits else plain
    return run(spectra, legendre, pair_of_slot, lat_owner, region_of_lon)


def solution(mesh):
    in_specs = (
        P(None, ("groups", "wide"), "narrow", None, None),
        P("narrow", None, None),
        P(),
        P(),
        P(),
    )
    out_specs = (P("groups", "narrow", "wide"), P("groups", "narrow", "wide"))
    return jax.shard_map(
        per_device, mesh=mesh, in_specs=in_specs, out_specs=out_specs, check_vma=False
    )
```

profile of v0, /device:TPU:1, one launch (start us, length us, event | category | flops | bytes accessed | tf_op | source)
XLA Modules:
  0.0 133.3 jit_solution(1303341799198182915)
XLA Ops:
  0.6 8.7 %legendre.8 = (f32[2,64,256]{2,1,0:T(8,128)}, f32[2,64,256]{2,1,0:T(8,128)}, f32[2,64,256]{2,1,0:T(8,128)}, f32[2,64,256]{2,1,0:T(8,128)}) custom-call(s32[640]{0:T(1024)} %pair_ref.9, s32[1]{0:T(128)} %bitcast.here_ref, s32[1,128]{1,0:T(1,128)} %bitcast.23, bf16[2,4,160,2,1281]{4,3,2,1,0:T(2,128)(2,1)} %s_ref.9, bf16[1281,80,128]{2,1,0:T(8,128)(2,1)} %bitcast.16), custom_call_target="tpu_custom_call" | custom-call | tf_op jit(solution)/shard_map/legendre/pallas_call | solution.py:208
  9.4 3.1 %collective-permute-start.10 = (f32[2,64,256]{2,1,0:T(8,128)}, f32[2,64,256]{2,1,0:T(8,128)S(1)}, u32[]{:S(2)}, u32[]{:S(2)}) collective-permute-start(f32[2,64,256]{2,1,0:T(8,128)} %get-tuple-element.50), channel_id=1, source_target_pairs={{0,2},{1,3},{2,0},{3,1},{4,6},{5,7},{6,4},{7,5},{8,10},{9,11},{10,... | collective-permute-start | bytes 393224 | tf_op jit(solution)/shard_map/ppermute | solution.py:402
  12.5 1.1 collective-permute-start.11
  13.6 6.1 %legendre.7 = (f32[2,32,256]{2,1,0:T(8,128)}, f32[2,32,256]{2,1,0:T(8,128)}, f32[2,32,256]{2,1,0:T(8,128)}, f32[2,32,256]{2,1,0:T(8,128)}) custom-call(s32[640]{0:T(1024)} %pair_ref.9, s32[1]{0:T(128)} %bitcast.here_ref, s32[1,128]{1,0:T(1,128)} %bitcast.24, bf16[2,4,160,2,1281]{4,3,2,1,0:T(2,128)(2,1)} %s_ref.9, bf16[1281,80,128]{2,1,0:T(8,128)(2,1)} %bitcast.17), custom_call_target="tpu_custom_call" | custom-call | tf_op jit(solution)/shard_map/legendre/pallas_call | solution.py:208
  20.1 1.0 collective-permute-start.7
  21.1 2.4 %collective-permute-start.8 = (f32[2,32,256]{2,1,0:T(8,128)}, f32[2,32,256]{2,1,0:T(8,128)S(1)}, u32[]{:S(2)}, u32[]{:S(2)}) collective-permute-start(f32[2,32,256]{2,1,0:T(8,128)} %get-tuple-element.47), channel_id=1, source_target_pairs={{0,3},{1,0},{2,1},{3,2},{4,7},{5,4},{6,5},{7,6},{8,11},{9,8},{10,9... | collective-permute-start | bytes 196616 | tf_op jit(solution)/shard_map/ppermute | solution.py:402
  23.5 8.8 %legendre.5 = (f32[2,64,256]{2,1,0:T(8,128)}, f32[2,64,256]{2,1,0:T(8,128)}, f32[2,64,256]{2,1,0:T(8,128)}, f32[2,64,256]{2,1,0:T(8,128)}) custom-call(s32[640]{0:T(1024)} %pair_ref.9, s32[1]{0:T(128)} %bitcast.here_ref, s32[1,128]{1,0:T(1,128)} %bitcast.25, bf16[2,4,160,2,1281]{4,3,2,1,0:T(2,128)(2,1)} %s_ref.9, bf16[1281,80,128]{2,1,0:T(8,128)(2,1)} %bitcast.18), custom_call_target="tpu_custom_call" | custom-call | tf_op jit(solution)/shard_map/legendre/pallas_call | solution.py:208
  34.7 1.4 %fusion.11 = (f32[32,1280]{1,0:T(8,128)S(1)}, f32[32,1280]{1,0:T(8,128)S(1)}, f32[32,1280]{1,0:T(8,128)S(1)}, f32[32,1280]{1,0:T(8,128)S(1)}) fusion(s32[1280]{0:T(1024)S(1)} %constant_dynamic-update-slice_fusion.6, s32[32]{0:T(128)S(1)} %get-tuple-element.83, s32[32]{0:T(128)S(1)} %get-tuple-element.82), kind=kLoop, calls=%fused_computation.21 | loop fusion | flops 737280 | bytes 660736 | tf_op jit(solution)/shard_map/cos | solution.py:407
  36.2 11.3 %legendre.9 = (f32[2,96,256]{2,1,0:T(8,128)}, f32[2,96,256]{2,1,0:T(8,128)}, f32[2,96,256]{2,1,0:T(8,128)}, f32[2,96,256]{2,1,0:T(8,128)}) custom-call(s32[640]{0:T(1024)} %pair_ref.9, s32[1]{0:T(128)} %bitcast.here_ref, s32[1,128]{1,0:T(1,128)} %bitcast.26, bf16[2,4,160,2,1281]{4,3,2,1,0:T(2,128)(2,1)} %s_ref.9, bf16[1281,80,128]{2,1,0:T(8,128)(2,1)} %bitcast.19), custom_call_target="tpu_custom_call" | custom-call | tf_op jit(solution)/shard_map/legendre/pallas_call | solution.py:208
  47.6 8.9 %legendre.6 = (f32[2,64,256]{2,1,0:T(8,128)}, f32[2,64,256]{2,1,0:T(8,128)}, f32[2,64,256]{2,1,0:T(8,128)}, f32[2,64,256]{2,1,0:T(8,128)}) custom-call(s32[640]{0:T(1024)} %pair_ref.9, s32[1]{0:T(128)} %bitcast.here_ref, s32[1,128]{1,0:T(1,128)} %bitcast.27, bf16[2,4,160,2,1281]{4,3,2,1,0:T(2,128)(2,1)} %s_ref.9, bf16[1281,80,128]{2,1,0:T(8,128)(2,1)} %bitcast.20), custom_call_target="tpu_custom_call" | custom-call | tf_op jit(solution)/shard_map/legendre/pallas_call | solution.py:208
  56.6 1.0 collective-permute-start.13
  57.6 2.4 %collective-permute-start.14 = (f32[2,96,256]{2,1,0:T(8,128)S(1)}, f32[2,96,256]{2,1,0:T(8,128)S(1)}, u32[]{:S(2)}, u32[]{:S(2)}) collective-permute-start(f32[2,96,256]{2,1,0:T(8,128)S(1)} %copy-done.17), channel_id=1, source_target_pairs={{0,3},{1,0},{2,1},{3,2},{4,7},{5,4},{6,5},{7,6},{8,11},{9,8},{10,9... | collective-permute-start | bytes 589832 | tf_op jit(solution)/shard_map/ppermute | solution.py:402
  60.3 1.4 %collective-permute-start.3 = (f32[2,64,256]{2,1,0:T(8,128)}, f32[2,64,256]{2,1,0:T(8,128)S(1)}, u32[]{:S(2)}, u32[]{:S(2)}) collective-permute-start(f32[2,64,256]{2,1,0:T(8,128)} %get-tuple-element.41), channel_id=1, source_target_pairs={{0,1},{1,2},{2,3},{3,0},{4,5},{5,6},{6,7},{7,4},{8,9},{9,10},{10,1... | collective-permute-start | bytes 393224 | tf_op jit(solution)/shard_map/ppermute | solution.py:402
  61.7 0.7 pad_maximum_fusion.3
  63.2 10.5 %collective-permute-done.9.refs_7_ = f32[2,64,256]{2,1,0:T(8,128)S(1)} collective-permute-done((f32[2,64,256]{2,1,0:T(8,128)S(1)}, f32[2,64,256]{2,1,0:T(8,128)S(1)}, u32[]{:S(2)}, u32[]{:S(2)}) %collective-permute-start.9) | collective-permute-done | bytes 131104 | tf_op jit(solution)/shard_map/ppermute | solution.py:402
  73.7 3.7 %collective-permute-start.4 = (f32[2,64,256]{2,1,0:T(8,128)}, f32[2,64,256]{2,1,0:T(8,128)S(1)}, u32[]{:S(2)}, u32[]{:S(2)}) collective-permute-start(f32[2,64,256]{2,1,0:T(8,128)} %get-tuple-element.42), channel_id=1, source_target_pairs={{0,2},{1,3},{2,0},{3,1},{4,6},{5,7},{6,4},{7,5},{8,10},{9,11},{10,... | collective-permute-start | bytes 393224 | tf_op jit(solution)/shard_map/ppermute | solution.py:402
  77.9 1.1 collective-permute-start
  78.9 3.2 %collective-permute-start.1 = (f32[2,64,256]{2,1,0:T(8,128)S(1)}, f32[2,64,256]{2,1,0:T(8,128)S(1)}, u32[]{:S(2)}, u32[]{:S(2)}) collective-permute-start(f32[2,64,256]{2,1,0:T(8,128)S(1)} %copy-done.21), channel_id=1, source_target_pairs={{0,2},{1,3},{2,0},{3,1},{4,6},{5,7},{6,4},{7,5},{8,10},{9,11},{10,... | collective-permute-start | bytes 393224 | tf_op jit(solution)/shard_map/ppermute | solution.py:402
  82.1 1.2 collective-permute-start.2
  83.3 1.3 pad_add_fusion.1.refs_0_
  84.6 0.9 copy.32.refs_1_
  85.5 0.8 copy.31.refs_1_
  86.3 0.8 copy.30.refs_3_
  87.1 0.8 pad_maximum_fusion.refs_0_
  87.9 10.3 %synthesis.3 = (f32[1024,512]{1,0:T(8,128)}, f32[1024,512]{1,0:T(8,128)}) custom-call(f32[128,768]{1,0:T(8,128)} %pad_maximum_fusion.refs_0_, f32[768,8]{1,0:T(8,128)} %copy.32.refs_1_, f32[2,32,256]{2,1,0:T(8,128)} %get-tuple-element.44.refs_2_, f32[2,32,256]{2,1,0:T(8,128)} %copy-done.13, f32[2,32,256]{2,1,0:T(8,128)} %copy-done.14, ...), custom_call_target="tpu_custom_call" | custom-call | tf_op jit(solution)/shard_map/synthesis/pallas_call | solution.py:384
  98.3 0.6 copy-done.10
  99.0 5.7 %synthesis.4 = (f32[1024,512]{1,0:T(8,128)}, f32[1024,512]{1,0:T(8,128)}) custom-call(f32[128,256]{1,0:T(8,128)} %get-tuple-element.66.refs_0_, f32[256,8]{1,0:T(8,128)} %copy.31.refs_1_, f32[2,64,256]{2,1,0:T(8,128)} %get-tuple-element.40.refs_2_, f32[2,64,256]{2,1,0:T(8,128)} %copy-done.6, f32[2,64,256]{2,1,0:T(8,128)} %copy-done.10, ...), custom_call_target="tpu_custom_call" | custom-call | tf_op jit(solution)/shard_map/synthesis/pallas_call | solution.py:384
  105.5 7.1 %synthesis.5 = (f32[16,128]{1,0:T(8,128)}, f32[16,128]{1,0:T(8,128)}, f32[16,128]{1,0:T(8,128)}, f32[16,128]{1,0:T(8,128)}) custom-call(s32[66]{0:T(128)} %pad_add_fusion.1.refs_0_, s32[1]{0:T(128)} %bitcast.3.refs_1_, f32[128,256]{1,0:T(8,128)} %get-tuple-element.67.refs_2_, f32[256,8]{1,0:T(8,128)} %copy.30.refs_3_, ...), custom_call_target="tpu_custom_call" | custom-call | tf_op jit(solution)/shard_map/synthesis/pallas_call | solution.py:384
  112.6 15.2 %collective-permute-start.15 = (f32[16,128]{1,0:T(8,128)}, f32[16,128]{1,0:T(8,128)S(1)}, u32[]{:S(2)}, u32[]{:S(2)}) collective-permute-start(f32[16,128]{1,0:T(8,128)} %get-tuple-element.61), channel_id=1, source_target_pairs={{0,4},{4,8},{8,12},{12,0},{1,5},{5,9},{9,13},{13,1},{2,6},{6,10},{... | collective-permute-start | bytes 24584 | tf_op jit(solution)/shard_map/ppermute | solution.py:402
  128.8 1.7 %collective-permute-done.16 = f32[16,128]{1,0:T(8,128)S(1)} collective-permute-done((f32[16,128]{1,0:T(8,128)}, f32[16,128]{1,0:T(8,128)S(1)}, u32[]{:S(2)}, u32[]{:S(2)}) %collective-permute-start.16) | collective-permute-done | bytes 8224 | tf_op jit(solution)/shard_map/ppermute | solution.py:402
  130.5 0.8 collective-permute-done.17
  131.3 0.7 maximum_maximum_fusion
  (114 shorter events, 7.6 us)
Async XLA Ops:
  9.4 50.6 %collective-permute-start.10 = (f32[2,64,256]{2,1,0:T(8,128)}, f32[2,64,256]{2,1,0:T(8,128)S(1)}, u32[]{:S(2)}, u32[]{:S(2)}) collective-permute-start(f32[2,64,256]{2,1,0:T(8,128)} %get-tuple-element.50), channel_id=1, source_target_pairs={{0,2},{1,3},{2,0},{3,1},{4,6},{5,7},{6,4},{7,5},{8,10},{9,11},{10,... | collective-permute-start | bytes 393224 | tf_op jit(solution)/shard_map/ppermute | solution.py:402
  12.5 47.8 %collective-permute-start.11 = (f32[2,64,256]{2,1,0:T(8,128)}, f32[2,64,256]{2,1,0:T(8,128)S(1)}, u32[]{:S(2)}, u32[]{:S(2)}) collective-permute-start(f32[2,64,256]{2,1,0:T(8,128)} %get-tuple-element.51), channel_id=1, source_target_pairs={{0,3},{1,0},{2,1},{3,2},{4,7},{5,4},{6,5},{7,6},{8,11},{9,8},{10,9... | collective-permute-start | bytes 393224 | tf_op jit(solution)/shard_map/ppermute | solution.py:402
  19.7 36.8 %collective-permute-start.6 = (f32[2,32,256]{2,1,0:T(8,128)}, f32[2,32,256]{2,1,0:T(8,128)S(1)}, u32[]{:S(2)}, u32[]{:S(2)}) collective-permute-start(f32[2,32,256]{2,1,0:T(8,128)} %get-tuple-element.45), channel_id=1, source_target_pairs={{0,1},{1,2},{2,3},{3,0},{4,5},{5,6},{6,7},{7,4},{8,9},{9,10},{10,1... | collective-permute-start | bytes 196616 | tf_op jit(solution)/shard_map/ppermute | solution.py:402
  20.1 36.5 %collective-permute-start.7 = (f32[2,32,256]{2,1,0:T(8,128)}, f32[2,32,256]{2,1,0:T(8,128)S(1)}, u32[]{:S(2)}, u32[]{:S(2)}) collective-permute-start(f32[2,32,256]{2,1,0:T(8,128)} %get-tuple-element.46), channel_id=1, source_target_pairs={{0,2},{1,3},{2,0},{3,1},{4,6},{5,7},{6,4},{7,5},{8,10},{9,11},{10,... | collective-permute-start | bytes 196616 | tf_op jit(solution)/shard_map/ppermute | solution.py:402
  21.1 11.1 %copy-start = (s32[640]{0:T(1024)S(1)}, s32[640]{0:T(1024)}, u32[]{:S(2)}) copy-start(s32[640]{0:T(1024)} %pair_ref.9) | copy-start | bytes 7684
  21.1 36.5 %collective-permute-start.8 = (f32[2,32,256]{2,1,0:T(8,128)}, f32[2,32,256]{2,1,0:T(8,128)S(1)}, u32[]{:S(2)}, u32[]{:S(2)}) collective-permute-start(f32[2,32,256]{2,1,0:T(8,128)} %get-tuple-element.47), channel_id=1, source_target_pairs={{0,3},{1,0},{2,1},{3,2},{4,7},{5,4},{6,5},{7,6},{8,11},{9,8},{10,9... | collective-permute-start | bytes 196616 | tf_op jit(solution)/shard_map/ppermute | solution.py:402
  47.5 10.1 %copy-start.17 = (f32[2,96,256]{2,1,0:T(8,128)S(1)}, f32[2,96,256]{2,1,0:T(8,128)}, u32[]{:S(2)}) copy-start(f32[2,96,256]{2,1,0:T(8,128)} %get-tuple-element.55) | copy-start | bytes 589828
  47.5 12.5 %copy-start.23 = (f32[2,64,256]{2,1,0:T(8,128)S(1)}, f32[2,64,256]{2,1,0:T(8,128)}, u32[]{:S(2)}) copy-start(f32[2,64,256]{2,1,0:T(8,128)} %get-tuple-element.49) | copy-start | bytes 393220
  47.5 14.9 %copy-start.16 = (s32[2048]{0:T(1024)S(1)}, s32[2048]{0:T(1024)}, u32[]{:S(2)}) copy-start(s32[2048]{0:T(1024)} %param.9) | copy-start | bytes 24580
  47.5 30.3 %copy-start.22 = (f32[2,64,256]{2,1,0:T(8,128)S(1)}, f32[2,64,256]{2,1,0:T(8,128)}, u32[]{:S(2)}) copy-start(f32[2,64,256]{2,1,0:T(8,128)} %get-tuple-element.37) | copy-start | bytes 393220
  47.6 31.4 %copy-start.21 = (f32[2,64,256]{2,1,0:T(8,128)S(1)}, f32[2,64,256]{2,1,0:T(8,128)}, u32[]{:S(2)}) copy-start(f32[2,64,256]{2,1,0:T(8,128)} %get-tuple-element.38) | copy-start | bytes 393220
  47.6 34.5 %copy-start.20 = (f32[2,64,256]{2,1,0:T(8,128)S(1)}, f32[2,64,256]{2,1,0:T(8,128)}, u32[]{:S(2)}) copy-start(f32[2,64,256]{2,1,0:T(8,128)} %get-tuple-element.39) | copy-start | bytes 393220
  56.5 31.4 %copy-start.13 = (f32[2,32,256]{2,1,0:T(8,128)}, f32[2,32,256]{2,1,0:T(8,128)S(1)}, u32[]{:S(2)}) copy-start(f32[2,32,256]{2,1,0:T(8,128)S(1)} %collective-permute-done.6.refs_3_) | copy-start | bytes 196612
  56.5 21.4 %collective-permute-start.12 = (f32[2,96,256]{2,1,0:T(8,128)S(1)}, f32[2,96,256]{2,1,0:T(8,128)S(1)}, u32[]{:S(2)}, u32[]{:S(2)}) collective-permute-start(f32[2,96,256]{2,1,0:T(8,128)S(1)} %copy-done.19), channel_id=1, source_target_pairs={{0,1},{1,2},{2,3},{3,0},{4,5},{5,6},{6,7},{7,4},{8,9},{9,10},{10,1... | collective-permute-start | bytes 589832 | tf_op jit(solution)/shard_map/ppermute | solution.py:402
  56.6 31.3 %copy-start.14 = (f32[2,32,256]{2,1,0:T(8,128)}, f32[2,32,256]{2,1,0:T(8,128)S(1)}, u32[]{:S(2)}) copy-start(f32[2,32,256]{2,1,0:T(8,128)S(1)} %collective-permute-done.7.refs_4_) | copy-start | bytes 196612
  56.6 22.3 %collective-permute-start.13 = (f32[2,96,256]{2,1,0:T(8,128)S(1)}, f32[2,96,256]{2,1,0:T(8,128)S(1)}, u32[]{:S(2)}, u32[]{:S(2)}) collective-permute-start(f32[2,96,256]{2,1,0:T(8,128)S(1)} %copy-done.18), channel_id=1, source_target_pairs={{0,2},{1,3},{2,0},{3,1},{4,6},{5,7},{6,4},{7,5},{8,10},{9,11},{10,... | collective-permute-start | bytes 589832 | tf_op jit(solution)/shard_map/ppermute | solution.py:402
  57.6 30.3 %copy-start.15 = (f32[2,32,256]{2,1,0:T(8,128)}, f32[2,32,256]{2,1,0:T(8,128)S(1)}, u32[]{:S(2)}) copy-start(f32[2,32,256]{2,1,0:T(8,128)S(1)} %collective-permute-done.8.refs_5_) | copy-start | bytes 196612
  57.6 24.5 %collective-permute-start.14 = (f32[2,96,256]{2,1,0:T(8,128)S(1)}, f32[2,96,256]{2,1,0:T(8,128)S(1)}, u32[]{:S(2)}, u32[]{:S(2)}) collective-permute-start(f32[2,96,256]{2,1,0:T(8,128)S(1)} %copy-done.17), channel_id=1, source_target_pairs={{0,3},{1,0},{2,1},{3,2},{4,7},{5,4},{6,5},{7,6},{8,11},{9,8},{10,9... | collective-permute-start | bytes 589832 | tf_op jit(solution)/shard_map/ppermute | solution.py:402
  60.0 27.9 %copy-start.4 = (f32[2,64,256]{2,1,0:T(8,128)}, f32[2,64,256]{2,1,0:T(8,128)S(1)}, u32[]{:S(2)}) copy-start(f32[2,64,256]{2,1,0:T(8,128)S(1)} %collective-permute-done.10.refs_8_) | copy-start | bytes 393220
  60.0 13.7 %collective-permute-start.9 = (f32[2,64,256]{2,1,0:T(8,128)S(1)}, f32[2,64,256]{2,1,0:T(8,128)S(1)}, u32[]{:S(2)}, u32[]{:S(2)}) collective-permute-start(f32[2,64,256]{2,1,0:T(8,128)S(1)} %copy-done.23), channel_id=1, source_target_pairs={{0,1},{1,2},{2,3},{3,0},{4,5},{5,6},{6,7},{7,4},{8,9},{9,10},{10,1... | collective-permute-start | bytes 393224 | tf_op jit(solution)/shard_map/ppermute | solution.py:402
  60.3 27.6 %copy-start.5 = (f32[2,64,256]{2,1,0:T(8,128)}, f32[2,64,256]{2,1,0:T(8,128)S(1)}, u32[]{:S(2)}) copy-start(f32[2,64,256]{2,1,0:T(8,128)S(1)} %collective-permute-done.11.refs_9_) | copy-start | bytes 393220
  60.3 17.1 %collective-permute-start.3 = (f32[2,64,256]{2,1,0:T(8,128)}, f32[2,64,256]{2,1,0:T(8,128)S(1)}, u32[]{:S(2)}, u32[]{:S(2)}) collective-permute-start(f32[2,64,256]{2,1,0:T(8,128)} %get-tuple-element.41), channel_id=1, source_target_pairs={{0,1},{1,2},{2,3},{3,0},{4,5},{5,6},{6,7},{7,4},{8,9},{9,10},{10,1... | collective-permute-start | bytes 393224 | tf_op jit(solution)/shard_map/ppermute | solution.py:402
  73.7 14.2 %copy-start.8 = (f32[2,64,256]{2,1,0:T(8,128)}, f32[2,64,256]{2,1,0:T(8,128)S(1)}, u32[]{:S(2)}) copy-start(f32[2,64,256]{2,1,0:T(8,128)S(1)} %collective-permute-done.9.refs_7_) | copy-start | bytes 393220
  73.7 24.6 %collective-permute-start.4 = (f32[2,64,256]{2,1,0:T(8,128)}, f32[2,64,256]{2,1,0:T(8,128)S(1)}, u32[]{:S(2)}, u32[]{:S(2)}) collective-permute-start(f32[2,64,256]{2,1,0:T(8,128)} %get-tuple-element.42), channel_id=1, source_target_pairs={{0,2},{1,3},{2,0},{3,1},{4,6},{5,7},{6,4},{7,5},{8,10},{9,11},{10,... | collective-permute-start | bytes 393224 | tf_op jit(solution)/shard_map/ppermute | solution.py:402
  77.4 20.9 %copy-start.6 = (f32[2,64,256]{2,1,0:T(8,128)}, f32[2,64,256]{2,1,0:T(8,128)S(1)}, u32[]{:S(2)}) copy-start(f32[2,64,256]{2,1,0:T(8,128)S(1)} %collective-permute-done.3.refs_3_) | copy-start | bytes 393220
  77.4 20.9 %collective-permute-start.5 = (f32[2,64,256]{2,1,0:T(8,128)}, f32[2,64,256]{2,1,0:T(8,128)S(1)}, u32[]{:S(2)}, u32[]{:S(2)}) collective-permute-start(f32[2,64,256]{2,1,0:T(8,128)} %get-tuple-element.43), channel_id=1, source_target_pairs={{0,3},{1,0},{2,1},{3,2},{4,7},{5,4},{6,5},{7,6},{8,11},{9,8},{10,9... | collective-permute-start | bytes 393224 | tf_op jit(solution)/shard_map/ppermute | solution.py:402
  77.9 26.9 %collective-permute-start = (f32[2,64,256]{2,1,0:T(8,128)S(1)}, f32[2,64,256]{2,1,0:T(8,128)S(1)}, u32[]{:S(2)}, u32[]{:S(2)}) collective-permute-start(f32[2,64,256]{2,1,0:T(8,128)S(1)} %copy-done.22), channel_id=1, source_target_pairs={{0,1},{1,2},{2,3},{3,0},{4,5},{5,6},{6,7},{7,4},{8,9},{9,10},{10,1... | collective-permute-start | bytes 393224 | tf_op jit(solution)/shard_map/ppermute | solution.py:402
  78.9 25.8 %collective-permute-start.1 = (f32[2,64,256]{2,1,0:T(8,128)S(1)}, f32[2,64,256]{2,1,0:T(8,128)S(1)}, u32[]{:S(2)}, u32[]{:S(2)}) collective-permute-start(f32[2,64,256]{2,1,0:T(8,128)S(1)} %copy-done.21), channel_id=1, source_target_pairs={{0,2},{1,3},{2,0},{3,1},{4,6},{5,7},{6,4},{7,5},{8,10},{9,11},{10,... | collective-permute-start | bytes 393224 | tf_op jit(solution)/shard_map/ppermute | solution.py:402
  82.1 22.7 %collective-permute-start.2 = (f32[2,64,256]{2,1,0:T(8,128)S(1)}, f32[2,64,256]{2,1,0:T(8,128)S(1)}, u32[]{:S(2)}, u32[]{:S(2)}) collective-permute-start(f32[2,64,256]{2,1,0:T(8,128)S(1)} %copy-done.20), channel_id=1, source_target_pairs={{0,3},{1,0},{2,1},{3,2},{4,7},{5,4},{6,5},{7,6},{8,11},{9,8},{10,9... | collective-permute-start | bytes 393224 | tf_op jit(solution)/shard_map/ppermute | solution.py:402
  112.6 16.2 %collective-permute-start.15 = (f32[16,128]{1,0:T(8,128)}, f32[16,128]{1,0:T(8,128)S(1)}, u32[]{:S(2)}, u32[]{:S(2)}) collective-permute-start(f32[16,128]{1,0:T(8,128)} %get-tuple-element.61), channel_id=1, source_target_pairs={{0,4},{4,8},{8,12},{12,0},{1,5},{5,9},{9,13},{13,1},{2,6},{6,10},{... | collective-permute-start | bytes 24584 | tf_op jit(solution)/shard_map/ppermute | solution.py:402
  127.7 2.7 %collective-permute-start.16 = (f32[16,128]{1,0:T(8,128)}, f32[16,128]{1,0:T(8,128)S(1)}, u32[]{:S(2)}, u32[]{:S(2)}) collective-permute-start(f32[16,128]{1,0:T(8,128)} %get-tuple-element.62), channel_id=1, source_target_pairs={{0,8},{4,12},{8,0},{12,4},{1,9},{5,13},{9,1},{13,5},{2,10},{6,14},... | collective-permute-start | bytes 24584 | tf_op jit(solution)/shard_map/ppermute | solution.py:402
  128.0 3.3 %collective-permute-start.17 = (f32[16,128]{1,0:T(8,128)}, f32[16,128]{1,0:T(8,128)S(1)}, u32[]{:S(2)}, u32[]{:S(2)}) collective-permute-start(f32[16,128]{1,0:T(8,128)} %get-tuple-element.63), channel_id=1, source_target_pairs={{0,12},{4,0},{8,4},{12,8},{1,13},{5,1},{9,5},{13,9},{2,14},{6,2},{... | collective-permute-start | bytes 24584 | tf_op jit(solution)/shard_map/ppermute | solution.py:402
  (10 other events, 46.3 us)
where the time goes:
time: 134 us; the launch traced here: 133 us
  Pallas kernels  67 us (50%)
  starting transfers between devices  38.4 us (29%)
  waiting for transfers between devices  13.6 us (10%)
  local copies, waits for them, and re-layouts  8.05 us (6%)
  other arithmetic  5.29 us (4%)
    pallas_call x5, Pallas kernels, legendre_sums(): pl.pallas_call(functools.partial(legendre_kernel, first_unit, parts), gri...  43.8 us
    ppermute x18, starting transfers between devices, shift(): lax.ppermute(x, axis, [(i, (i + step) % count) for i in range(count)])  38.4 us
    pallas_call x3, Pallas kernels, synthesis(): pl.pallas_call(functools.partial(synthesis_kernel, counts, fresh, closing...  23.2 us
    ppermute x18, waiting for transfers between devices, shift(): lax.ppermute(x, axis, [(i, (i + step) % count) for i in range(count)])  13.6 us
    unnamed x61, local copies, waits for them, and re-layouts  5.2 us
  transfers between devices with their start and end apart: 18, of which 4 were waited for; matrix products, arithmetic and copies ran while one was open for 7% of the time, Pallas kernels for 38%

commit v1 on v0

--- a/solution.py
+++ b/solution.py
@@ -13,9 +13,12 @@
 LANES = 128
 PAIRS_UNIT = 8
 NB = 32
-VMEM = 56 * 2**20
-CHUNKS = (1, 2, 3, 2, 2)
-STAGES = ((0, 1, 2), (3,), (4,))
+CUTS = 5
+LEGENDRE_VMEM = 107 * 2**19
+SYNTHESIS_VMEM = 28 * 2**20
+TURN = 128
+CHUNKS = (2, 2, 2, 2, 2)
+GROUPS = ((0, 1), (2, 3), (4,))
 F32 = jnp.float32
 BF16 = jnp.bfloat16
 
@@ -116,74 +119,119 @@
     share = LANES // parts
     rows = []
     for step in range(parts):
-        owner_index = lax.rem(here + step, parts)
+        owner_index = lax.bitwise_xor(here, jnp.int32(step))
         target = (owner_index * share + second % share).astype(F32)
         rows.append(jnp.sum(jnp.where(place == target, lane_of, 0.0), axis=0, keepdims=True))
     return jnp.concatenate(rows, axis=0).astype(jnp.int32)
 
 
-def legendre_kernel(first_unit, parts, pair_ref, here_ref, owner_ref, s_ref, l_ref, *refs):
-    outs, (lanes_ref, table, sums) = refs[:parts], refs[parts:]
-    members, steps, slots, _, length = s_ref.shape
+def legendre_kernel(first_unit, units, parts, known, pair_ref, here_ref, owner_ref, s_hbm, l_hbm, *refs):
+    if known:
+        lanes_ref, outs, refs = owner_ref, refs[:parts], refs[parts:]
+    else:
+        lanes_ref, outs, refs = refs[parts], refs[:parts], refs[parts + 1 :]
+    s_buf, l_buf, table, total, sums, ends, s_sem, l_sem = refs
+    _, members, steps, slots, _, length = s_buf.shape
     top = length - 1
     times = members * steps
     rows = 2 * times
+    pairs = slots // 2
     unit = pl.program_id(0)
     here = here_ref[0]
+    cuts = l_sem.shape[1]
+    depth = top // cuts
+
+    def copies(which):
+        side = lax.rem(which, 2)
+        at = pl.multiple_of((first_unit + which) * slots, slots)
+        found = [
+            pltpu.make_async_copy(
+                s_hbm.at[:, :, pl.ds(at, slots)], s_buf.at[side], s_sem.at[side]
+            )
+        ]
+        at = pl.multiple_of((first_unit + which) * pairs, pairs)
+        for cut in range(cuts):
+            span = pl.ds(cut * depth, depth if cut < cuts - 1 else length - cut * depth)
+            found.append(
+                pltpu.make_async_copy(
+                    l_hbm.at[span, pl.ds(at, pairs)], l_buf.at[side, span], l_sem.at[side, cut]
+                )
+            )
+        return found
 
     @pl.when(unit == 0)
     def _():
-        lanes_ref[...] = latitude_lanes(owner_ref[...], here, parts)
-
-    def turn(i, carry):
-        at = pl.multiple_of(i * LANES, LANES)
-        table[:, pl.ds(at, LANES), :] = jnp.swapaxes(l_ref[pl.ds(at, LANES)], 0, 1)
-        return carry
-
-    lax.fori_loop(0, top // LANES, turn, 0)
+        for copy in copies(jnp.int32(0)):
+            copy.start()
+        if not known:
+            lanes_ref[...] = latitude_lanes(owner_ref[...], here, parts)
+
+    @pl.when(unit + 1 < units)
+    def _():
+        for copy in copies(unit + 1):
+            copy.start()
+
+    side = lax.rem(unit, 2)
+    arriving = copies(unit)
+    arriving[0].wait()
 
     spot = iota((rows, top), 1)
     even = jnp.where(spot % 2 == 0, 1.0, 0.0).astype(BF16)
-    base = (here * pl.num_programs(0) * 0) + here * (pair_ref.shape[0] // parts) + (first_unit + unit) * slots
-    low = iota((rows, LANES), 1) < LANES // 2
-    for pair in range(slots // 2):
-        parts_of, last, signs = [], [], []
-        for side in range(2):
-            slot = 2 * pair + side
-            whole = s_ref[:, :, slot].reshape(rows, length)
-            x = whole[:, :top]
-            last.append(whole[:, top:].astype(F32))
+    base = here * (pair_ref.shape[0] // parts) + (first_unit + unit) * slots
+    for cut in range(cuts):
+        arriving[1 + cut].wait()
+        for at in range(cut * depth, (cut + 1) * depth, TURN):
+            table[:, at : at + TURN, :] = jnp.swapaxes(l_buf[side, at : at + TURN], 0, 1)
+
+    for pair in range(pairs):
+        masked = []
+        for slot in (2 * pair, 2 * pair + 1):
+            x = s_buf[side, :, :, slot].reshape(rows, length)[:, :top]
             first_len = top - pair_ref[base + slot]
             lead = x * jnp.where(spot < first_len, 1.0, 0.0).astype(BF16)
             tail = x - lead
             lead_even = lead * even
             tail_even = tail * even
-            parts_of += [lead_even, lead - lead_even, tail_even, tail - tail_even]
-            signs.append(jnp.where(first_len % 2 == 0, 1.0, -1.0).astype(F32))
-        product = jnp.dot(jnp.concatenate(parts_of, axis=0), table[pair], preferred_element_type=F32)
-        end = l_ref[top, pair : pair + 1, :].astype(F32)
-        for side in range(2):
-            at = 4 * side * rows
+            masked += [lead_even, lead - lead_even, tail_even, tail - tail_even]
+        total[pair] = jnp.dot(
+            jnp.concatenate(masked, axis=0), table[pair], preferred_element_type=F32
+        )
+
+    low = iota((rows, LANES), 1) < LANES // 2
+
+    ends[...] = l_buf[side, top].astype(F32)
+
+    def combine(pair, carry):
+        end = ends[pl.ds(pair, 1), :]
+        for odd_slot in range(2):
+            slot = 2 * pair + odd_slot
+            sign = jnp.where((top - pair_ref[base + slot]) % 2 == 0, 1.0, -1.0).astype(F32)
+            last = s_buf[side, :, :, slot, :, top:].reshape(rows, 1).astype(F32)
+            at = 4 * odd_slot * rows
             lead_even, lead_odd, tail_even, tail_odd = (
-                product[at + i * rows : at + (i + 1) * rows] for i in range(4)
+                total[pair, at + i * rows : at + (i + 1) * rows, :] for i in range(4)
             )
-            tail_even = tail_even + last[side] * end
+            tail_even = tail_even + last * end
             found = (
                 (lead_even + lead_odd, lead_even - lead_odd),
-                (tail_even + tail_odd, (tail_even - tail_odd) * signs[side]),
+                (tail_even + tail_odd, (tail_even - tail_odd) * sign),
             )
             for which, (north, south) in enumerate(found):
-                if side == 0:
+                if odd_slot:
+                    both = jnp.where(low, pltpu.roll(north, LANES // 2, 1), south)
+                else:
                     both = jnp.where(low, north, pltpu.roll(south, LANES // 2, 1))
-                else:
-                    both = jnp.where(low, pltpu.roll(north, LANES // 2, 1), south)
-                wave = 2 * (2 * pair + side) + which
-                sums[wave * rows : (wave + 1) * rows, :] = both
+                at = pl.multiple_of((2 * slot + which) * rows, rows)
+                sums[pl.ds(at, rows), :] = both
+        return carry
+
+    [combine(i, 0) for i in range(pairs)]
 
     waves = 2 * slots
     share = LANES // parts
     per = LANES // share
     group = iota((waves, LANES), 1) // share
+    mine = pl.ds(pl.multiple_of(unit * waves, waves), waves)
     for step in range(parts):
         index = jnp.broadcast_to(lanes_ref[step : step + 1, :], (waves, LANES))
         for part in range(2):
@@ -196,36 +244,46 @@
                     source = sums[pl.ds(row, waves, stride=rows), :]
                     moved = jnp.take_along_axis(source, index, axis=1, mode="promise_in_bounds")
                     built = moved if place == 0 else jnp.where(group == place, moved, built)
-                outs[step][part, :, block * LANES : (block + 1) * LANES] = built
+                outs[step][part, mine, block * LANES : (block + 1) * LANES] = built
 
 
 def legendre_sums(spectra, turned, pair_of_slot, here, owner, first_unit, units, parts):
     members, steps, _, _, length = spectra.shape
     slots = 2 * PAIRS_UNIT
     waves = 2 * slots
-    width = members * steps * LANES // parts
-    out = jax.ShapeDtypeStruct((2, units * waves, width), F32)
+    times = members * steps
+    width = times * LANES // parts
+    known = first_unit > 0
+    out = [jax.ShapeDtypeStruct((2, units * waves, width), F32)] * parts
+    if not known:
+        out = out + [jax.ShapeDtypeStruct((parts, LANES), jnp.int32)]
+    here_spec = pl.BlockSpec(memory_space=pltpu.VMEM)
+    away = pl.BlockSpec(memory_space=pltpu.HBM)
     return pl.pallas_call(
-        functools.partial(legendre_kernel, first_unit, parts),
+        functools.partial(legendre_kernel, first_unit, units, parts, known),
         grid_spec=pltpu.PrefetchScalarGridSpec(
             num_scalar_prefetch=2,
             grid=(units,),
-            in_specs=[
-                pl.BlockSpec((1, LANES), lambda u, *_: (0, 0)),
-                pl.BlockSpec(
-                    (members, steps, slots, 2, length), lambda u, *_: (0, 0, first_unit + u, 0, 0)
-                ),
-                pl.BlockSpec((length, PAIRS_UNIT, LANES), lambda u, *_: (0, first_unit + u, 0)),
-            ],
-            out_specs=[pl.BlockSpec((2, waves, width), lambda u, *_: (0, u, 0))] * parts,
+            in_specs=[here_spec, away, away],
+            out_specs=[here_spec] * len(out),
             scratch_shapes=[
-                pltpu.VMEM((parts, LANES), jnp.int32),
+                pltpu.VMEM((2, members, steps, slots, 2, length), BF16),
+                pltpu.VMEM((2, length, PAIRS_UNIT, LANES), BF16),
                 pltpu.VMEM((PAIRS_UNIT, length - 1, LANES), BF16),
-                pltpu.VMEM((waves * 2 * members * steps, LANES), F32),
+                pltpu.VMEM((PAIRS_UNIT, 16 * times, LANES), F32),
+                pltpu.VMEM((waves * 2 * times, LANES), F32),
+                pltpu.VMEM((PAIRS_UNIT, LANES), F32),
+                pltpu.SemaphoreType.DMA((2,)),
+                pltpu.SemaphoreType.DMA((2, CUTS)),
             ],
         ),
-        out_shape=[out] * parts,
-        compiler_params=pltpu.CompilerParams(vmem_limit_bytes=VMEM),
+        out_shape=out,
+        compiler_params=pltpu.CompilerParams(vmem_limit_bytes=LEGENDRE_VMEM),
+        cost_estimate=pl.CostEstimate(
+            flops=units * PAIRS_UNIT * 2 * LANES * LANES * length,
+            bytes_accessed=units * PAIRS_UNIT * (LANES + 2 * 2 * times) * length * 2,
+            transcendentals=0,
+        ),
         name="legendre",
     )(pair_of_slot, here, owner, spectra, turned)
 
@@ -235,12 +293,26 @@
     return high, (x - high.astype(F32)).astype(BF16)
 
 
+def turns(numbers, full):
+    quarter = full // 4
+    turned = (numbers + quarter // 2) // quarter
+    x = (numbers - turned * quarter).astype(F32) * (2.0 * math.pi / full)
+    y = x * x
+    sine = x * (1.0 + y * (-1 / 6 + y * (1 / 120 + y * (-1 / 5040 + y * (1 / 362880)))))
+    cosine = 1.0 + y * (-1 / 2 + y * (1 / 24 + y * (-1 / 720 + y * (1 / 40320 - y * (1 / 3628800)))))
+    odd = turned % 2 == 1
+    c, s = jnp.where(odd, sine, cosine), jnp.where(odd, cosine, sine)
+    c = jnp.where((turned == 1) | (turned == 2), -c, c)
+    s = jnp.where((turned == 2) | (turned == 3), -s, s)
+    return c, s
+
+
 def synthesis_kernel(counts, fresh, closing, shape, *refs):
-    lon, members, regions, wide = shape
+    lon, top, regions, wide = shape
     refs = list(refs)
     if closing:
         starts_ref, here_ref = refs.pop(0), refs.pop(0)
-    base_ref, coef_ref = refs.pop(0), refs.pop(0)
+    waves_ref = refs.pop(0)
     pieces = [refs.pop(0) for _ in counts]
     if not fresh:
         cos_in, sin_in = refs.pop(0), refs.pop(0)
@@ -248,17 +320,32 @@
         outs = [refs.pop(0) for _ in range(wide)]
     else:
         cos_out, sin_out = refs.pop(0), refs.pop(0)
-    w_cos_h, w_cos_l, w_sin_h, w_sin_l, t_cos_h, t_cos_l, t_sin_h, t_sin_l = refs[:8]
+    base_ref, w_cos_h, w_cos_l, w_sin_h, w_sin_l, t_cos_h, t_cos_l, t_sin_h, t_sin_l = refs[:9]
     step = pl.program_id(0)
-    block = t_cos_h.shape[0]
+    block, depth = t_cos_h.shape
     width = pieces[0].shape[2]
+    coarse = lon // 2 // NB
+    full = 8 * top
 
     @pl.when(step == 0)
     def _():
+        waves = waves_ref[...]
+        at = 0
+        for factor, shift_by, count in ((2 * NB, 0, coarse), (2, 1, NB)):
+            number = factor * iota((count, depth), 0) + shift_by
+            c, s = turns(number * waves % full, full)
+            base_ref[at : at + count, :] = c
+            base_ref[at + count : at + 2 * count, :] = s
+            at += 2 * count
+        c, s = turns((lon - 1) * waves % full, full)
+        rate = waves.astype(F32) * (1.0 / top)
+        scale = top ** (-0.5)
+        kind = iota((8, depth), 0)
+        turn = jnp.where(kind == 0, c * scale, jnp.where(kind == 1, s * scale, rate))
         at = 0
         for piece, count in zip(pieces, counts):
             span = slice(at, at + count)
-            coef = coef_ref[span, :]
+            coef = turn[:, span].T
             c, s, rate = coef[:, 0:1], coef[:, 1:2], coef[:, 2:3]
             real, imag = piece[0], piece[1]
             p0 = real * c - imag * s
@@ -271,8 +358,6 @@
                 w_sin_h[span, cols], w_sin_l[span, cols] = split(value)
             at += count
 
-    coarse = lon // 2 // NB
-
     def fill(a, carry):
         row = step * (block // NB) + a
         ca = base_ref[pl.ds(row, 1), :]
@@ -296,15 +381,16 @@
 
     even = product(t_cos_h, t_cos_l, w_cos_h, w_cos_l)
     odd = product(t_sin_h, t_sin_l, w_sin_h, w_sin_l)
+    here_rows = pl.ds(pl.multiple_of(step * block, block), block)
     if not fresh:
-        even = even + cos_in[...]
-        odd = odd + sin_in[...]
+        even = even + cos_in[here_rows, :]
+        odd = odd + sin_in[here_rows, :]
     if not closing:
-        cos_out[...] = even
-        sin_out[...] = odd
+        cos_out[here_rows, :] = even
+        sin_out[here_rows, :] = odd
         return
 
-    value_ref, slope_ref, found_v, found_s = refs[8:]
+    value_ref, slope_ref, found_v, found_s = refs[9:]
     half = lon // 2
 
     def narrowed(x):
@@ -362,28 +448,26 @@
             outs[offset][...] = found_v[pl.ds(start, REG_DEV), :]
 
 
-def synthesis(base, coef, pieces, held, closing, lon, members, regions, wide, starts, here):
+def synthesis(waves, pieces, held, closing, lon, top, regions, wide, starts, here):
     block = min(512, lon // 2)
-    depth = base.shape[1]
+    depth = waves.shape[1]
     counts = tuple(piece.shape[1] for piece in pieces)
     width = pieces[0].shape[2]
     fresh = held is None
     prefetch = (starts, here) if closing else ()
-    whole = lambda x: pl.BlockSpec(x.shape, lambda i, *_: (0,) * x.ndim)
-    strip = pl.BlockSpec((block, 2 * width), lambda i, *_: (i, 0))
-    operands = [base, coef, *pieces] + ([] if fresh else list(held))
-    in_specs = [whole(x) for x in (base, coef, *pieces)] + ([] if fresh else [strip] * 2)
-    scratch = [pltpu.VMEM((depth, 2 * width), BF16)] * 4 + [pltpu.VMEM((block, depth), BF16)] * 4
+    operands = [waves, *pieces] + ([] if fresh else list(held))
+    in_specs = [pl.BlockSpec(memory_space=pltpu.VMEM)] * len(operands)
+    scratch = [pltpu.VMEM((2 * (lon // 2 // NB + NB), depth), F32)]
+    scratch += [pltpu.VMEM((depth, 2 * width), BF16)] * 4 + [pltpu.VMEM((block, depth), BF16)] * 4
     if closing:
         out_shape = [jax.ShapeDtypeStruct((REG_DEV, LANES), F32)] * wide
-        out_specs = [pl.BlockSpec((REG_DEV, LANES), lambda i, *_: (0, 0))] * wide
         scratch += [pltpu.VMEM((lon, LANES), F32)] * 2 + [pltpu.VMEM((regions, LANES), F32)] * 2
     else:
         out_shape = [jax.ShapeDtypeStruct((lon // 2, 2 * width), F32)] * 2
-        out_specs = [strip] * 2
+    out_specs = [pl.BlockSpec(memory_space=pltpu.VMEM)] * len(out_shape)
     return pl.pallas_call(
         functools.partial(
-            synthesis_kernel, counts, fresh, closing, (lon, members, regions, wide)
+            synthesis_kernel, counts, fresh, closing, (lon, top, regions, wide)
         ),
         grid_spec=pltpu.PrefetchScalarGridSpec(
             num_scalar_prefetch=len(prefetch),
@@ -393,7 +477,10 @@
             scratch_shapes=scratch,
         ),
         out_shape=out_shape,
-        compiler_params=pltpu.CompilerParams(vmem_limit_bytes=VMEM),
+        compiler_params=pltpu.CompilerParams(vmem_limit_bytes=SYNTHESIS_VMEM),
+        cost_estimate=pl.CostEstimate(
+            flops=6 * depth * lon * 2 * width, bytes_accessed=16 * lon * width, transcendentals=0
+        ),
         name="synthesis",
     )(*prefetch, *operands)
 
@@ -402,9 +489,18 @@
     return lax.ppermute(x, axis, [(i, (i + step) % count) for i in range(count)])
 
 
-def turns(numbers, full):
-    angle = (numbers % full).astype(F32) * (2.0 * math.pi / full)
-    return jnp.cos(angle), jnp.sin(angle)
+def swap(x, axis, count, step):
+    return lax.ppermute(x, axis, [(i, i ^ step) for i in range(count)])
+
+
+def final_kernel(*refs):
+    *found, peak_ref, slope_ref = refs
+    best = functools.reduce(jnp.maximum, [x[...] for x in found])
+    members, _, share = peak_ref.shape
+    for member in range(members):
+        peak_ref[member] = best[:, member * share : (member + 1) * share]
+        at = LANES // 2 + member * share
+        slope_ref[member] = best[:, at : at + share]
 
 
 def kernels(spectra, legendre, pair_of_slot, lat_owner, region_of_lon):
@@ -419,22 +515,35 @@
     here_ref = here.reshape(1)
     owner = lat_owner.reshape(1, -1)
     turned = jnp.transpose(legendre, (1, 0, 2))
-
-    chunks, first = [], 0
-    for units in CHUNKS:
+    tied = lax.optimization_barrier
+
+    kept, beside, near, far, first = [], [], [], [], 0
+    for number, units in enumerate(CHUNKS):
+        if number >= 1:
+            here_ref, kept[-1] = tied((here_ref, kept[-1]))
+        if number == 2:
+            pair_here, region_of_lon, kept[-1] = tied((pair_of_slot, region_of_lon, kept[-1]))
+        if number >= 2:
+            here_ref, far[number - 2] = tied((here_ref, far[number - 2]))
+        if number >= 3:
+            ready = [g for g, group in enumerate(GROUPS) if group[-1] == number - 2]
+            for g in ready:
+                here_ref, near[g] = tied((here_ref, near[g]))
         sums = legendre_sums(
             spectra, turned, pair_of_slot, here_ref, owner, first, units, parts
         )
-        chunks.append([sums[0]] + [shift(sums[i], "narrow", parts, i) for i in range(1, parts)])
-        final, first = sums[0], first + units
-    pair_of_slot, region_of_lon, final = lax.optimization_barrier(
-        (pair_of_slot, region_of_lon, final)
-    )
-    chunks[-1][0] = final
-
-    waves_of = jnp.stack([pair_of_slot, top - 1 - pair_of_slot], axis=1).reshape(parts, -1)
-    source = lax.rem(here - jnp.arange(parts, dtype=jnp.int32) + parts, parts)
-    waves_of = waves_of[source]
+        if number == 0:
+            owner = sums[parts]
+        kept.append(sums[0])
+        beside.append(sums[1])
+        far.append([swap(sums[i], "narrow", parts, i) for i in range(2, parts)])
+        for group in GROUPS:
+            if group[-1] == number:
+                near.append(swap(jnp.concatenate([beside[i] for i in group], axis=1), "narrow", parts, 1))
+        first += units
+
+    waves_of = jnp.stack([pair_here, top - 1 - pair_here], axis=1).reshape(parts, -1)
+    waves_of = waves_of[lax.bitwise_xor(here, jnp.arange(parts, dtype=jnp.int32))]
     edges = jnp.arange(regions + 1, dtype=jnp.int32)
     starts = jnp.sum((region_of_lon[None, :] < edges[:, None]).astype(jnp.int32), axis=1)
     starts = jnp.concatenate([starts, region_of_lon[lon // 2 - 1 : lon // 2]])
@@ -443,55 +552,52 @@
     bounds = [0]
     for units in CHUNKS:
         bounds.append(bounds[-1] + units * per_unit)
-    order = []
-    for stage in STAGES:
-        for chunk in stage:
-            order.append(waves_of[:, bounds[chunk] : bounds[chunk + 1]].reshape(-1))
-    waves = jnp.concatenate(order)
-    full = 8 * top
-    coarse = 2 * NB * jnp.arange(lon // 2 // NB, dtype=jnp.int32)
-    fine = 2 * jnp.arange(NB, dtype=jnp.int32) + 1
-    ca, sa = turns(coarse[:, None] * waves[None, :], full)
-    cb, sb = turns(fine[:, None] * waves[None, :], full)
-    base = jnp.concatenate([ca, sa, cb, sb], axis=0)
-    c, s = turns((lon - 1) * waves, full)
-    scale = top ** (-0.5)
-    coef = jnp.stack([c * scale, s * scale, waves.astype(F32) / top] + [c] * 5, axis=1)
-
-    held, at = None, 0
-    for number, stage in enumerate(STAGES):
-        pieces = [piece for chunk in stage for piece in chunks[chunk]]
-        depth = sum(piece.shape[1] for piece in pieces)
+
+    def piece(array, source, chunks):
+        return array, [waves_of[source, bounds[i] : bounds[i + 1]] for i in chunks]
+
+    late = len(CHUNKS) - 1
+    own = [piece(kept[i], 0, (i,)) for i in range(late + 1)]
+    swapped = [piece(near[g], 1, group) for g, group in enumerate(GROUPS)]
+    across = [
+        [piece(array, 2 + i, (chunk,)) for i, array in enumerate(far[chunk])]
+        for chunk in range(late + 1)
+    ]
+    stages = (
+        own[: late - 1] + swapped[:-2] + sum(across[: late - 1], []),
+        own[late - 1 :] + swapped[-2:-1] + across[late - 1],
+        swapped[-1:] + across[late],
+    )
+    held = None
+    for number, stage in enumerate(stages):
+        waves = jnp.concatenate([w for _, found in stage for w in found])
         held = synthesis(
-            base[:, at : at + depth],
-            coef[at : at + depth],
-            pieces,
+            waves.reshape(1, -1),
+            [array for array, _ in stage],
             held,
-            number == len(STAGES) - 1,
+            number == len(stages) - 1,
             lon,
-            members,
+            top,
             regions,
             wide,
             starts,
             here_wide.reshape(1),
         )
-        at += depth
-
-    best = held[0]
-    for offset in range(1, wide):
-        best = jnp.maximum(best, shift(held[offset], "wide", wide, offset))
-    best = best.reshape(REG_DEV, 2, members, LANES // 2 // members)
-    peak = jnp.transpose(best[:, 0], (1, 2, 0))
-    peak_slope = jnp.transpose(best[:, 1], (1, 2, 0))
-    return peak, peak_slope
+
+    found = [held[0]] + [shift(held[i], "wide", wide, i) for i in range(1, wide)]
+    out = jax.ShapeDtypeStruct((members, REG_DEV, LANES // 2 // members), F32)
+    peak, peak_slope = pl.pallas_call(final_kernel, out_shape=[out] * 2, name="final")(*found)
+    return jnp.transpose(peak, (0, 2, 1)), jnp.transpose(peak_slope, (0, 2, 1))
 
 
 def per_device(spectra, legendre, pair_of_slot, lat_owner, region_of_lon):
     members, steps, _, _, length = spectra.shape
     pairs, _, lanes = legendre.shape
     share = lat_owner.shape[0] // lax.axis_size("narrow")
+    parts = lax.axis_size("narrow")
     fits = (
-        pairs == PAIRS_UNIT * sum(CHUNKS)
+        parts & (parts - 1) == 0
+        and pairs == PAIRS_UNIT * sum(CHUNKS)
         and lanes == LANES
         and lat_owner.shape[0] == LANES
         and 2 * members * share == LANES

time: 134 us -> 97.5 us (0.73)
  starting transfers between devices: 38.4 us -> 22.7 us
  waiting for transfers between devices: 13.6 us -> 2.93 us
  other arithmetic: 5.29 us -> 1.02 us
  local copies, waits for them, and re-layouts: 8.05 us -> 4.33 us
  Pallas kernels: 67 us -> 65.4 us
    ppermute x18 -> x3, starting transfers between devices: 38.4 us -> 5.6 us  [shift(): lax.ppermute(x, axis, [(i, (i + step) % count) for i in range(count)])]
    ppermute x0 -> x13, starting transfers between devices: none -> 17.1 us  [swap(): return lax.ppermute(x, axis, [(i, i ^ step) for i in range(count)])]
    ppermute x18 -> x3, waiting for transfers between devices: 13.6 us -> 2.9 us  [shift(): lax.ppermute(x, axis, [(i, (i + step) % count) for i in range(count)])]
    pallas_call x3, Pallas kernels: 23.2 us -> 19 us  [synthesis(): pl.pallas_call(functools.partial(synthesis_kernel, counts, fresh, closing...]
    unnamed x61 -> x18, local copies, waits for them, and re-layouts: 5.2 us -> 2.53 us
    pallas_call x5 -> x6, Pallas kernels: 43.8 us -> 46.4 us  [the longest x5 45 us: legendre_sums(): pl.pallas_call(functools.partial(legendre_kernel, first_unit, units, part...]
    cos x1 -> x0, other arithmetic: 1.39 us -> none  [turns(): return (jnp.cos(angle), jnp.sin(angle))]
  transfers between devices with their start and end apart: 18 -> 16, of which waited for: 4 -> 3; matrix products, arithmetic and copies ran while one was open for 7% -> 3% of each run, Pallas kernels for 38% -> 52%
where the time goes in v1:
time: 97.5 us; the launch traced here: 97.2 us
  Pallas kernels  65.4 us (67%)
  starting transfers between devices  22.7 us (23%)
  local copies, waits for them, and re-layouts  4.33 us (4%)
  waiting for transfers between devices  2.93 us (3%)
  other arithmetic  1.02 us (1%)
    pallas_call x5, Pallas kernels, legendre_sums(): pl.pallas_call(functools.partial(legendre_kernel, first_unit, units, part...  45 us
    pallas_call x3, Pallas kernels, synthesis(): pl.pallas_call(functools.partial(synthesis_kernel, counts, fresh, closing...  19 us
    ppermute x13, starting transfers between devices, swap(): return lax.ppermute(x, axis, [(i, i ^ step) for i in range(count)])  17.1 us
    ppermute x3, starting transfers between devices, shift(): lax.ppermute(x, axis, [(i, (i + step) % count) for i in range(count)])  5.6 us
    ppermute x3, waiting for transfers between devices, shift(): lax.ppermute(x, axis, [(i, (i + step) % count) for i in range(count)])  2.9 us
    unnamed x18, local copies, waits for them, and re-layouts  2.53 us
  transfers between devices with their start and end apart: 16, of which 3 were waited for; matrix products, arithmetic and copies ran while one was open for 3% of the time, Pallas kernels for 52%

profile of v1, /device:TPU:1, one launch (start us, length us, event | category | flops | bytes accessed | tf_op | source)
XLA Modules:
  0.0 97.2 jit_solution(8693217970819292606)
XLA Ops:
  0.6 0.7 copy-done
  1.3 0.7 copy-done.3
  2.0 8.4 %legendre.5 = (f32[2,64,256]{2,1,0:T(8,128)S(1)}, f32[2,64,256]{2,1,0:T(8,128)S(1)}, f32[2,64,256]{2,1,0:T(8,128)S(1)}, f32[2,64,256]{2,1,0:T(8,128)}, s32[4,128]{1,0:T(4,128)S(1)}) custom-call(s32[640]{0:T(1024)S(1)} %copy-done, s32[1]{0:T(128)} %bitcast.here_ref, s32[1,128]{1,0:T(1,128)S(1)} %bitcast.50, bf16[2,4,160,2,1281]{4,3,2,1,0:T(2,128)(2,1)} %s_hbm.9, ...), custom_call_target="tpu_custom_call" | custom-call | flops 671612928 | bytes 6558720 | tf_op jit(solution)/shard_map/legendre/pallas_call | solution.py:262
  10.4 3.2 %collective-permute-start = (f32[2,64,256]{2,1,0:T(8,128)S(1)}, f32[2,64,256]{2,1,0:T(8,128)S(1)}, u32[]{:S(2)}, u32[]{:S(2)}) collective-permute-start(f32[2,64,256]{2,1,0:T(8,128)S(1)} %get-tuple-element.63), channel_id=1, source_target_pairs={{0,2},{1,3},{2,0},{3,1},{4,6},{5,7},{6,4},{7,5},{8,10},{9,11},{10,... | collective-permute-start | bytes 393224 | tf_op jit(solution)/shard_map/ppermute | solution.py:493
  13.6 1.1 %collective-permute-start.1 = (f32[2,64,256]{2,1,0:T(8,128)}, f32[2,64,256]{2,1,0:T(8,128)S(1)}, u32[]{:S(2)}, u32[]{:S(2)}) collective-permute-start(f32[2,64,256]{2,1,0:T(8,128)} %get-tuple-element.64), channel_id=1, source_target_pairs={{0,3},{1,2},{2,1},{3,0},{4,7},{5,6},{6,5},{7,4},{8,11},{9,10},{10,... | collective-permute-start | bytes 393224 | tf_op jit(solution)/shard_map/ppermute | solution.py:493
  14.7 9.1 %legendre.6 = (f32[2,64,256]{2,1,0:T(8,128)S(1)}, f32[2,64,256]{2,1,0:T(8,128)S(1)}, f32[2,64,256]{2,1,0:T(8,128)S(1)}, f32[2,64,256]{2,1,0:T(8,128)}) custom-call(s32[640]{0:T(1024)S(1)} %copy-done, s32[1]{0:T(128)} %bitcast.here_ref, s32[4,128]{1,0:T(4,128)S(1)} %get-tuple-element.57.owner_ref, bf16[2,4,160,2,1281]{4,3,2,1,0:T(2,128)(2,1)} %s_hbm.9, ...), custom_call_target="tpu_custom_call" | custom-call | flops 671612928 | bytes 6558720 | tf_op jit(solution)/shard_map/legendre/pallas_call | solution.py:262
  23.8 1.4 %collective-permute-start.2 = (f32[2,64,256]{2,1,0:T(8,128)S(1)}, f32[2,64,256]{2,1,0:T(8,128)S(1)}, u32[]{:S(2)}, u32[]{:S(2)}) collective-permute-start(f32[2,64,256]{2,1,0:T(8,128)S(1)} %get-tuple-element.68), channel_id=1, source_target_pairs={{0,2},{1,3},{2,0},{3,1},{4,6},{5,7},{6,4},{7,5},{8,10},{9,11},{10,... | collective-permute-start | bytes 393224 | tf_op jit(solution)/shard_map/ppermute | solution.py:493
  25.2 0.9 collective-permute-start.3
  26.2 0.4 collective-permute-start.4
  27.0 0.6 gather_fusion
  27.9 0.6 slice.63
  28.7 9.1 %legendre.7 = (f32[2,64,256]{2,1,0:T(8,128)S(1)}, f32[2,64,256]{2,1,0:T(8,128)S(1)}, f32[2,64,256]{2,1,0:T(8,128)S(1)}, f32[2,64,256]{2,1,0:T(8,128)}) custom-call(s32[640]{0:T(1024)S(1)} %copy-done.1, s32[1]{0:T(128)} %bitcast.here_ref, s32[4,128]{1,0:T(4,128)S(1)} %get-tuple-element.57.owner_ref, bf16[2,4,160,2,1281]{4,3,2,1,0:T(2,128)(2,1)} %s_hbm.9, ...), custom_call_target="tpu_custom_call" | custom-call | flops 671612928 | bytes 6558720 | tf_op jit(solution)/shard_map/legendre/pallas_call | solution.py:262
  37.8 2.4 %collective-permute-start.5 = (f32[2,64,256]{2,1,0:T(8,128)S(1)}, f32[2,64,256]{2,1,0:T(8,128)S(1)}, u32[]{:S(2)}, u32[]{:S(2)}) collective-permute-start(f32[2,64,256]{2,1,0:T(8,128)S(1)} %get-tuple-element.76), channel_id=1, source_target_pairs={{0,2},{1,3},{2,0},{3,1},{4,6},{5,7},{6,4},{7,5},{8,10},{9,11},{10,... | collective-permute-start | bytes 393224 | tf_op jit(solution)/shard_map/ppermute | solution.py:493
  40.2 0.9 collective-permute-start.6
  41.1 0.7 pad_add_fusion.2.refs_0_
  41.8 9.1 %legendre.8 = (f32[2,64,256]{2,1,0:T(8,128)S(1)}, f32[2,64,256]{2,1,0:T(8,128)S(1)}, f32[2,64,256]{2,1,0:T(8,128)S(1)}, f32[2,64,256]{2,1,0:T(8,128)}) custom-call(s32[640]{0:T(1024)S(1)} %copy-done.1, s32[1]{0:T(128)} %bitcast.here_ref, s32[4,128]{1,0:T(4,128)S(1)} %get-tuple-element.57.owner_ref, bf16[2,4,160,2,1281]{4,3,2,1,0:T(2,128)(2,1)} %s_hbm.9, ...), custom_call_target="tpu_custom_call" | custom-call | flops 671612928 | bytes 6558720 | tf_op jit(solution)/shard_map/legendre/pallas_call | solution.py:262
  50.9 1.9 %collective-permute-start.11 = (f32[2,64,256]{2,1,0:T(8,128)S(1)}, f32[2,64,256]{2,1,0:T(8,128)S(1)}, u32[]{:S(2)}, u32[]{:S(2)}) collective-permute-start(f32[2,64,256]{2,1,0:T(8,128)S(1)} %get-tuple-element.86), channel_id=1, source_target_pairs={{0,2},{1,3},{2,0},{3,1},{4,6},{5,7},{6,4},{7,5},{8,10},{9,11},{10,... | collective-permute-start | bytes 393224 | tf_op jit(solution)/shard_map/ppermute | solution.py:493
  52.8 1.1 %collective-permute-start.12 = (f32[2,64,256]{2,1,0:T(8,128)}, f32[2,64,256]{2,1,0:T(8,128)S(1)}, u32[]{:S(2)}, u32[]{:S(2)}) collective-permute-start(f32[2,64,256]{2,1,0:T(8,128)} %get-tuple-element.87), channel_id=1, source_target_pairs={{0,3},{1,2},{2,1},{3,0},{4,7},{5,6},{6,5},{7,4},{8,11},{9,10},{10,... | collective-permute-start | bytes 393224 | tf_op jit(solution)/shard_map/ppermute | solution.py:493
  54.0 9.3 %legendre.9 = (f32[2,64,256]{2,1,0:T(8,128)S(1)}, f32[2,64,256]{2,1,0:T(8,128)S(1)}, f32[2,64,256]{2,1,0:T(8,128)S(1)}, f32[2,64,256]{2,1,0:T(8,128)}) custom-call(s32[640]{0:T(1024)S(1)} %copy-done.1, s32[1]{0:T(128)} %bitcast.here_ref, s32[4,128]{1,0:T(4,128)S(1)} %get-tuple-element.57.owner_ref, bf16[2,4,160,2,1281]{4,3,2,1,0:T(2,128)(2,1)} %s_hbm.9, ...), custom_call_target="tpu_custom_call" | custom-call | flops 671612928 | bytes 6558720 | tf_op jit(solution)/shard_map/legendre/pallas_call | solution.py:262
  63.3 1.5 %collective-permute-start.7 = (f32[2,64,256]{2,1,0:T(8,128)S(1)}, f32[2,64,256]{2,1,0:T(8,128)S(1)}, u32[]{:S(2)}, u32[]{:S(2)}) collective-permute-start(f32[2,64,256]{2,1,0:T(8,128)S(1)} %get-tuple-element.79), channel_id=1, source_target_pairs={{0,1},{1,0},{2,3},{3,2},{4,5},{5,4},{6,7},{7,6},{8,9},{9,8},{10,11... | collective-permute-start | bytes 393224 | tf_op jit(solution)/shard_map/ppermute | solution.py:493
  64.8 1.0 %collective-permute-start.8 = (f32[2,64,256]{2,1,0:T(8,128)S(1)}, f32[2,64,256]{2,1,0:T(8,128)S(1)}, u32[]{:S(2)}, u32[]{:S(2)}) collective-permute-start(f32[2,64,256]{2,1,0:T(8,128)S(1)} %get-tuple-element.80), channel_id=1, source_target_pairs={{0,2},{1,3},{2,0},{3,1},{4,6},{5,7},{6,4},{7,5},{8,10},{9,11},{10,... | collective-permute-start | bytes 393224 | tf_op jit(solution)/shard_map/ppermute | solution.py:493
  65.8 8.6 %synthesis.3 = (f32[1024,512]{1,0:T(8,128)S(1)}, f32[1024,512]{1,0:T(8,128)S(1)}) custom-call(s32[1,704]{1,0:T(1,128)S(1)} %reshape.48.refs_0_, f32[2,64,256]{2,1,0:T(8,128)S(1)} %get-tuple-element.88.refs_1_, f32[2,64,256]{2,1,0:T(8,128)S(1)} %get-tuple-element.89.refs_2_, f32[2,64,256]{2,1,0:T(8,128)S(1)} %get-tuple-element.90.refs_3_, ...), custom_call_target="tpu_custom_call" | custom-call | flops 4429185024 | bytes 8388608 | tf_op jit(solution)/shard_map/synthesis/pallas_call | solution.py:468
  74.5 1.2 %collective-permute-start.9 = (f32[2,64,256]{2,1,0:T(8,128)S(1)}, f32[2,64,256]{2,1,0:T(8,128)S(1)}, u32[]{:S(2)}, u32[]{:S(2)}) collective-permute-start(f32[2,64,256]{2,1,0:T(8,128)S(1)} %copy-done.8), channel_id=1, source_target_pairs={{0,3},{1,2},{2,1},{3,0},{4,7},{5,6},{6,5},{7,4},{8,11},{9,10},{10,... | collective-permute-start | bytes 393224 | tf_op jit(solution)/shard_map/ppermute | solution.py:493
  75.7 5.4 %synthesis.4 = (f32[1024,512]{1,0:T(8,128)S(1)}, f32[1024,512]{1,0:T(8,128)S(1)}) custom-call(s32[1,384]{1,0:T(1,128)S(1)} %reshape.47.refs_0_, f32[2,64,256]{2,1,0:T(8,128)S(1)} %get-tuple-element.82.refs_1_, f32[2,64,256]{2,1,0:T(8,128)S(1)} %get-tuple-element.83.refs_2_, f32[2,128,256]{2,1,0:T(8,128)S(1)} %collective-permute-done.10.refs_3_, ...), custom_call_target="tpu_custom_call" | custom-call | flops 2415919104 | bytes 8388608 | tf_op jit(solution)/shard_map/synthesis/pallas_call | solution.py:468
  81.1 5.0 %synthesis.5 = (f32[16,128]{1,0:T(8,128)S(1)}, f32[16,128]{1,0:T(8,128)S(1)}, f32[16,128]{1,0:T(8,128)S(1)}, f32[16,128]{1,0:T(8,128)S(1)}) custom-call(s32[66]{0:T(128)S(1)} %pad_add_fusion.2.refs_0_, s32[1]{0:T(128)} %bitcast.3.refs_1_, s32[1,192]{1,0:T(1,128)S(1)} %bitcast.49, f32[2,64,256]{2,1,0:T(8,128)S(1)} %collective-permute-done.7.refs_3_, ...), custom_call_target="tpu_custom_call" | custom-call | flops 1207959552 | bytes 8388608 | tf_op jit(solution)/shard_map/synthesis/pallas_call | solution.py:468
  86.1 0.6 copy-done.2
  86.7 5.2 %collective-permute-start.13 = (f32[16,128]{1,0:T(8,128)S(1)}, f32[16,128]{1,0:T(8,128)S(1)}, u32[]{:S(2)}, u32[]{:S(2)}) collective-permute-start(f32[16,128]{1,0:T(8,128)S(1)} %get-tuple-element.103), channel_id=1, source_target_pairs={{0,4},{4,8},{8,12},{12,0},{1,5},{5,9},{9,13},{13,1},{2,6},{6,10},{... | collective-permute-start | bytes 24584 | tf_op jit(solution)/shard_map/ppermute | solution.py:489
  92.3 0.4 collective-permute-done.13.refs_1_
  92.7 1.7 %collective-permute-done.14.refs_2_ = f32[16,128]{1,0:T(8,128)S(1)} collective-permute-done((f32[16,128]{1,0:T(8,128)S(1)}, f32[16,128]{1,0:T(8,128)S(1)}, u32[]{:S(2)}, u32[]{:S(2)}) %collective-permute-start.14) | collective-permute-done | bytes 8224 | tf_op jit(solution)/shard_map/ppermute | solution.py:489
  94.4 0.8 collective-permute-done.15.refs_3_
  95.2 0.6 copy-done.7
  95.8 1.4 %final.1 = (f32[2,16,32]{2,1,0:T(8,128)}, f32[2,16,32]{2,1,0:T(8,128)}) custom-call(f32[16,128]{1,0:T(8,128)} %copy-done.2, f32[16,128]{1,0:T(8,128)} %copy-done.5, f32[16,128]{1,0:T(8,128)} %copy-done.6, f32[16,128]{1,0:T(8,128)} %copy-done.7), custom_call_target="tpu_custom_call" | custom-call | tf_op jit(solution)/shard_map/final/pallas_call | solution.py:589
  (48 shorter events, 1.5 us)
Async XLA Ops:
  0.6 0.7 copy-start
  1.3 0.7 copy-start.3
  10.4 18.3 %collective-permute-start = (f32[2,64,256]{2,1,0:T(8,128)S(1)}, f32[2,64,256]{2,1,0:T(8,128)S(1)}, u32[]{:S(2)}, u32[]{:S(2)}) collective-permute-start(f32[2,64,256]{2,1,0:T(8,128)S(1)} %get-tuple-element.63), channel_id=1, source_target_pairs={{0,2},{1,3},{2,0},{3,1},{4,6},{5,7},{6,4},{7,5},{8,10},{9,11},{10,... | collective-permute-start | bytes 393224 | tf_op jit(solution)/shard_map/ppermute | solution.py:493
  13.6 15.1 %collective-permute-start.1 = (f32[2,64,256]{2,1,0:T(8,128)}, f32[2,64,256]{2,1,0:T(8,128)S(1)}, u32[]{:S(2)}, u32[]{:S(2)}) collective-permute-start(f32[2,64,256]{2,1,0:T(8,128)} %get-tuple-element.64), channel_id=1, source_target_pairs={{0,3},{1,2},{2,1},{3,0},{4,7},{5,6},{6,5},{7,4},{8,11},{9,10},{10,... | collective-permute-start | bytes 393224 | tf_op jit(solution)/shard_map/ppermute | solution.py:493
  14.7 13.0 %copy-start.4 = (s32[2048]{0:T(1024)S(1)}, s32[2048]{0:T(1024)}, u32[]{:S(2)}) copy-start(s32[2048]{0:T(1024)} %param.9) | copy-start | bytes 24580
  14.7 14.0 %copy-start.1 = (s32[640]{0:T(1024)S(1)}, s32[640]{0:T(1024)}, u32[]{:S(2)}) copy-start(s32[640]{0:T(1024)} %pair_ref.9) | copy-start | bytes 7684
  23.8 18.0 %collective-permute-start.2 = (f32[2,64,256]{2,1,0:T(8,128)S(1)}, f32[2,64,256]{2,1,0:T(8,128)S(1)}, u32[]{:S(2)}, u32[]{:S(2)}) collective-permute-start(f32[2,64,256]{2,1,0:T(8,128)S(1)} %get-tuple-element.68), channel_id=1, source_target_pairs={{0,2},{1,3},{2,0},{3,1},{4,6},{5,7},{6,4},{7,5},{8,10},{9,11},{10,... | collective-permute-start | bytes 393224 | tf_op jit(solution)/shard_map/ppermute | solution.py:493
  25.2 16.6 %collective-permute-start.3 = (f32[2,64,256]{2,1,0:T(8,128)}, f32[2,64,256]{2,1,0:T(8,128)S(1)}, u32[]{:S(2)}, u32[]{:S(2)}) collective-permute-start(f32[2,64,256]{2,1,0:T(8,128)} %get-tuple-element.69), channel_id=1, source_target_pairs={{0,3},{1,2},{2,1},{3,0},{4,7},{5,6},{6,5},{7,4},{8,11},{9,10},{10,... | collective-permute-start | bytes 393224 | tf_op jit(solution)/shard_map/ppermute | solution.py:493
  26.2 15.6 %collective-permute-start.4 = (f32[2,128,256]{2,1,0:T(8,128)S(1)}, f32[2,128,256]{2,1,0:T(8,128)S(1)}, u32[]{:S(2)}, u32[]{:S(2)}) collective-permute-start(f32[2,128,256]{2,1,0:T(8,128)S(1)} %pad_maximum_fusion), channel_id=1, source_target_pairs={{0,1},{1,0},{2,3},{3,2},{4,5},{5,4},{6,7},{7,6},{8,9},{9,8},{10,11... | collective-permute-start | bytes 786440 | tf_op jit(solution)/shard_map/ppermute | solution.py:493
  37.8 13.1 %collective-permute-start.5 = (f32[2,64,256]{2,1,0:T(8,128)S(1)}, f32[2,64,256]{2,1,0:T(8,128)S(1)}, u32[]{:S(2)}, u32[]{:S(2)}) collective-permute-start(f32[2,64,256]{2,1,0:T(8,128)S(1)} %get-tuple-element.76), channel_id=1, source_target_pairs={{0,2},{1,3},{2,0},{3,1},{4,6},{5,7},{6,4},{7,5},{8,10},{9,11},{10,... | collective-permute-start | bytes 393224 | tf_op jit(solution)/shard_map/ppermute | solution.py:493
  40.2 10.7 %collective-permute-start.6 = (f32[2,64,256]{2,1,0:T(8,128)}, f32[2,64,256]{2,1,0:T(8,128)S(1)}, u32[]{:S(2)}, u32[]{:S(2)}) collective-permute-start(f32[2,64,256]{2,1,0:T(8,128)} %get-tuple-element.77), channel_id=1, source_target_pairs={{0,3},{1,2},{2,1},{3,0},{4,7},{5,6},{6,5},{7,4},{8,11},{9,10},{10,... | collective-permute-start | bytes 393224 | tf_op jit(solution)/shard_map/ppermute | solution.py:493
  50.9 23.5 %collective-permute-start.11 = (f32[2,64,256]{2,1,0:T(8,128)S(1)}, f32[2,64,256]{2,1,0:T(8,128)S(1)}, u32[]{:S(2)}, u32[]{:S(2)}) collective-permute-start(f32[2,64,256]{2,1,0:T(8,128)S(1)} %get-tuple-element.86), channel_id=1, source_target_pairs={{0,2},{1,3},{2,0},{3,1},{4,6},{5,7},{6,4},{7,5},{8,10},{9,11},{10,... | collective-permute-start | bytes 393224 | tf_op jit(solution)/shard_map/ppermute | solution.py:493
  52.8 22.9 %collective-permute-start.12 = (f32[2,64,256]{2,1,0:T(8,128)}, f32[2,64,256]{2,1,0:T(8,128)S(1)}, u32[]{:S(2)}, u32[]{:S(2)}) collective-permute-start(f32[2,64,256]{2,1,0:T(8,128)} %get-tuple-element.87), channel_id=1, source_target_pairs={{0,3},{1,2},{2,1},{3,0},{4,7},{5,6},{6,5},{7,4},{8,11},{9,10},{10,... | collective-permute-start | bytes 393224 | tf_op jit(solution)/shard_map/ppermute | solution.py:493
  53.9 21.7 %collective-permute-start.10 = (f32[2,128,256]{2,1,0:T(8,128)S(1)}, f32[2,128,256]{2,1,0:T(8,128)S(1)}, u32[]{:S(2)}, u32[]{:S(2)}) collective-permute-start(f32[2,128,256]{2,1,0:T(8,128)S(1)} %pad_maximum_fusion.1), channel_id=1, source_target_pairs={{0,1},{1,0},{2,3},{3,2},{4,5},{5,4},{6,7},{7,6},{8,9},{9,8},{10,11... | collective-permute-start | bytes 786440 | tf_op jit(solution)/shard_map/ppermute | solution.py:493
  63.3 17.8 %collective-permute-start.7 = (f32[2,64,256]{2,1,0:T(8,128)S(1)}, f32[2,64,256]{2,1,0:T(8,128)S(1)}, u32[]{:S(2)}, u32[]{:S(2)}) collective-permute-start(f32[2,64,256]{2,1,0:T(8,128)S(1)} %get-tuple-element.79), channel_id=1, source_target_pairs={{0,1},{1,0},{2,3},{3,2},{4,5},{5,4},{6,7},{7,6},{8,9},{9,8},{10,11... | collective-permute-start | bytes 393224 | tf_op jit(solution)/shard_map/ppermute | solution.py:493
  64.8 9.6 %copy-start.8 = (f32[2,64,256]{2,1,0:T(8,128)S(1)}, f32[2,64,256]{2,1,0:T(8,128)}, u32[]{:S(2)}) copy-start(f32[2,64,256]{2,1,0:T(8,128)} %get-tuple-element.81) | copy-start | bytes 393220
  64.8 16.3 %collective-permute-start.8 = (f32[2,64,256]{2,1,0:T(8,128)S(1)}, f32[2,64,256]{2,1,0:T(8,128)S(1)}, u32[]{:S(2)}, u32[]{:S(2)}) collective-permute-start(f32[2,64,256]{2,1,0:T(8,128)S(1)} %get-tuple-element.80), channel_id=1, source_target_pairs={{0,2},{1,3},{2,0},{3,1},{4,6},{5,7},{6,4},{7,5},{8,10},{9,11},{10,... | collective-permute-start | bytes 393224 | tf_op jit(solution)/shard_map/ppermute | solution.py:493
  74.5 6.6 %collective-permute-start.9 = (f32[2,64,256]{2,1,0:T(8,128)S(1)}, f32[2,64,256]{2,1,0:T(8,128)S(1)}, u32[]{:S(2)}, u32[]{:S(2)}) collective-permute-start(f32[2,64,256]{2,1,0:T(8,128)S(1)} %copy-done.8), channel_id=1, source_target_pairs={{0,3},{1,2},{2,1},{3,0},{4,7},{5,6},{6,5},{7,4},{8,11},{9,10},{10,... | collective-permute-start | bytes 393224 | tf_op jit(solution)/shard_map/ppermute | solution.py:493
  86.1 0.6 copy-start.2
  86.7 6.0 %collective-permute-start.13 = (f32[16,128]{1,0:T(8,128)S(1)}, f32[16,128]{1,0:T(8,128)S(1)}, u32[]{:S(2)}, u32[]{:S(2)}) collective-permute-start(f32[16,128]{1,0:T(8,128)S(1)} %get-tuple-element.103), channel_id=1, source_target_pairs={{0,4},{4,8},{8,12},{12,0},{1,5},{5,9},{9,13},{13,1},{2,6},{6,10},{... | collective-permute-start | bytes 24584 | tf_op jit(solution)/shard_map/ppermute | solution.py:489
  91.9 2.5 %collective-permute-start.14 = (f32[16,128]{1,0:T(8,128)S(1)}, f32[16,128]{1,0:T(8,128)S(1)}, u32[]{:S(2)}, u32[]{:S(2)}) collective-permute-start(f32[16,128]{1,0:T(8,128)S(1)} %get-tuple-element.104), channel_id=1, source_target_pairs={{0,8},{4,12},{8,0},{12,4},{1,9},{5,13},{9,1},{13,5},{2,10},{6,14},... | collective-permute-start | bytes 24584 | tf_op jit(solution)/shard_map/ppermute | solution.py:489
  92.1 3.1 %collective-permute-start.15 = (f32[16,128]{1,0:T(8,128)S(1)}, f32[16,128]{1,0:T(8,128)S(1)}, u32[]{:S(2)}, u32[]{:S(2)}) collective-permute-start(f32[16,128]{1,0:T(8,128)S(1)} %get-tuple-element.105), channel_id=1, source_target_pairs={{0,12},{4,0},{8,4},{12,8},{1,13},{5,1},{9,5},{13,9},{2,14},{6,2},{... | collective-permute-start | bytes 24584 | tf_op jit(solution)/shard_map/ppermute | solution.py:489
  92.7 2.5 %copy-start.5 = (f32[16,128]{1,0:T(8,128)}, f32[16,128]{1,0:T(8,128)S(1)}, u32[]{:S(2)}) copy-start(f32[16,128]{1,0:T(8,128)S(1)} %collective-permute-done.13.refs_1_) | copy-start | bytes 24580
  94.4 0.8 copy-start.6
  95.2 0.6 copy-start.7

commit v2 on v1

--- a/solution.py
+++ b/solution.py
@@ -15,10 +15,11 @@
 NB = 32
 CUTS = 5
 LEGENDRE_VMEM = 107 * 2**19
-SYNTHESIS_VMEM = 28 * 2**20
+SYNTHESIS_VMEM = 24 * 2**20
+TABLES_VMEM = 12 * 2**20
 TURN = 128
-CHUNKS = (2, 2, 2, 2, 2)
-GROUPS = ((0, 1), (2, 3), (4,))
+CHUNKS = (2, 3, 3, 2)
+GROUPS = ((0, 1, 2), (3,))
 F32 = jnp.float32
 BF16 = jnp.bfloat16
 
@@ -176,7 +177,7 @@
     arriving[0].wait()
 
     spot = iota((rows, top), 1)
-    even = jnp.where(spot % 2 == 0, 1.0, 0.0).astype(BF16)
+    sign = jnp.where(spot % 2 == 0, 1.0, -1.0).astype(BF16)
     base = here * (pair_ref.shape[0] // parts) + (first_unit + unit) * slots
     for cut in range(cuts):
         arriving[1 + cut].wait()
@@ -190,9 +191,7 @@
             first_len = top - pair_ref[base + slot]
             lead = x * jnp.where(spot < first_len, 1.0, 0.0).astype(BF16)
             tail = x - lead
-            lead_even = lead * even
-            tail_even = tail * even
-            masked += [lead_even, lead - lead_even, tail_even, tail - tail_even]
+            masked += [lead, lead * sign, tail, tail * sign]
         total[pair] = jnp.dot(
             jnp.concatenate(masked, axis=0), table[pair], preferred_element_type=F32
         )
@@ -205,16 +204,15 @@
         end = ends[pl.ds(pair, 1), :]
         for odd_slot in range(2):
             slot = 2 * pair + odd_slot
-            sign = jnp.where((top - pair_ref[base + slot]) % 2 == 0, 1.0, -1.0).astype(F32)
-            last = s_buf[side, :, :, slot, :, top:].reshape(rows, 1).astype(F32)
+            turned = jnp.where((top - pair_ref[base + slot]) % 2 == 0, 1.0, -1.0).astype(F32)
+            last = s_buf[side, :, :, slot, :, top:].reshape(rows, 1).astype(F32) * end
             at = 4 * odd_slot * rows
-            lead_even, lead_odd, tail_even, tail_odd = (
+            north_lead, south_lead, north_tail, south_tail = (
                 total[pair, at + i * rows : at + (i + 1) * rows, :] for i in range(4)
             )
-            tail_even = tail_even + last * end
             found = (
-                (lead_even + lead_odd, lead_even - lead_odd),
-                (tail_even + tail_odd, (tail_even - tail_odd) * sign),
+                (north_lead, south_lead),
+                (north_tail + last, (south_tail + last) * turned),
             )
             for which, (north, south) in enumerate(found):
                 if odd_slot:
@@ -264,7 +262,7 @@
         grid_spec=pltpu.PrefetchScalarGridSpec(
             num_scalar_prefetch=2,
             grid=(units,),
-            in_specs=[here_spec, away, away],
+            in_specs=[pl.BlockSpec(owner.shape, lambda u, *_: (0, 0)), away, away],
             out_specs=[here_spec] * len(out),
             scratch_shapes=[
                 pltpu.VMEM((2, members, steps, slots, 2, length), BF16),
@@ -307,12 +305,63 @@
     return c, s
 
 
+def tables_kernel(lon, top, waves_ref, coef_ref, t_cos_h, t_cos_l, t_sin_h, t_sin_l, base_ref):
+    half, depth = t_cos_h.shape
+    coarse = half // NB
+    full = 8 * top
+    waves = waves_ref[...]
+    at = 0
+    for factor, shift_by, count in ((2 * NB, 0, coarse), (2, 1, NB)):
+        number = factor * iota((count, depth), 0) + shift_by
+        c, s = turns(number * waves % full, full)
+        base_ref[at : at + count, :] = c
+        base_ref[at + count : at + 2 * count, :] = s
+        at += 2 * count
+    c, s = turns((lon - 1) * waves % full, full)
+    rate = waves.astype(F32) * (1.0 / top)
+    scale = top ** (-0.5)
+    kind = iota((8, depth), 0)
+    turn = jnp.where(kind == 0, c * scale, jnp.where(kind == 1, s * scale, rate))
+    coef_ref[...] = turn.T
+
+    def fill(a, carry):
+        ca = base_ref[pl.ds(a, 1), :]
+        sa = base_ref[pl.ds(coarse + a, 1), :]
+        cb = base_ref[2 * coarse : 2 * coarse + NB, :]
+        sb = base_ref[2 * coarse + NB : 2 * coarse + 2 * NB, :]
+        at = pl.ds(pl.multiple_of(a * NB, NB), NB)
+        t_cos_h[at, :], t_cos_l[at, :] = split(ca * cb - sa * sb)
+        t_sin_h[at, :], t_sin_l[at, :] = split(sa * cb + ca * sb)
+        return carry
+
+    lax.fori_loop(0, coarse, fill, 0)
+
+
+def tables(waves, lon, top):
+    depth = waves.shape[1]
+    held = pl.BlockSpec(memory_space=pltpu.VMEM)
+    out = [jax.ShapeDtypeStruct((depth, 8), F32)]
+    out += [jax.ShapeDtypeStruct((lon // 2, depth), BF16)] * 4
+    return pl.pallas_call(
+        functools.partial(tables_kernel, lon, top),
+        in_specs=[held],
+        out_specs=[held] * 5,
+        out_shape=out,
+        scratch_shapes=[pltpu.VMEM((2 * (lon // 2 // NB + NB), depth), F32)],
+        compiler_params=pltpu.CompilerParams(vmem_limit_bytes=TABLES_VMEM),
+        cost_estimate=pl.CostEstimate(
+            flops=16 * lon * depth, bytes_accessed=4 * lon * depth, transcendentals=0
+        ),
+        name="tables",
+    )(waves)
+
+
 def synthesis_kernel(counts, fresh, closing, shape, *refs):
-    lon, top, regions, wide = shape
+    lon, regions, wide = shape
     refs = list(refs)
     if closing:
         starts_ref, here_ref = refs.pop(0), refs.pop(0)
-    waves_ref = refs.pop(0)
+    coef_ref, *table_refs = [refs.pop(0) for _ in range(5)]
     pieces = [refs.pop(0) for _ in counts]
     if not fresh:
         cos_in, sin_in = refs.pop(0), refs.pop(0)
@@ -320,32 +369,18 @@
         outs = [refs.pop(0) for _ in range(wide)]
     else:
         cos_out, sin_out = refs.pop(0), refs.pop(0)
-    base_ref, w_cos_h, w_cos_l, w_sin_h, w_sin_l, t_cos_h, t_cos_l, t_sin_h, t_sin_l = refs[:9]
+    w_cos_h, w_cos_l, w_sin_h, w_sin_l = refs[:4]
     step = pl.program_id(0)
-    block, depth = t_cos_h.shape
+    block = lon // 2 // pl.num_programs(0)
     width = pieces[0].shape[2]
-    coarse = lon // 2 // NB
-    full = 8 * top
+    here_rows = pl.ds(pl.multiple_of(step * block, block), block)
 
     @pl.when(step == 0)
     def _():
-        waves = waves_ref[...]
-        at = 0
-        for factor, shift_by, count in ((2 * NB, 0, coarse), (2, 1, NB)):
-            number = factor * iota((count, depth), 0) + shift_by
-            c, s = turns(number * waves % full, full)
-            base_ref[at : at + count, :] = c
-            base_ref[at + count : at + 2 * count, :] = s
-            at += 2 * count
-        c, s = turns((lon - 1) * waves % full, full)
-        rate = waves.astype(F32) * (1.0 / top)
-        scale = top ** (-0.5)
-        kind = iota((8, depth), 0)
-        turn = jnp.where(kind == 0, c * scale, jnp.where(kind == 1, s * scale, rate))
         at = 0
         for piece, count in zip(pieces, counts):
             span = slice(at, at + count)
-            coef = turn[:, span].T
+            coef = coef_ref[span, :]
             c, s, rate = coef[:, 0:1], coef[:, 1:2], coef[:, 2:3]
             real, imag = piece[0], piece[1]
             p0 = real * c - imag * s
@@ -358,18 +393,7 @@
                 w_sin_h[span, cols], w_sin_l[span, cols] = split(value)
             at += count
 
-    def fill(a, carry):
-        row = step * (block // NB) + a
-        ca = base_ref[pl.ds(row, 1), :]
-        sa = base_ref[pl.ds(coarse + row, 1), :]
-        cb = base_ref[2 * coarse : 2 * coarse + NB, :]
-        sb = base_ref[2 * coarse + NB : 2 * coarse + 2 * NB, :]
-        at = pl.ds(pl.multiple_of(a * NB, NB), NB)
-        t_cos_h[at, :], t_cos_l[at, :] = split(ca * cb - sa * sb)
-        t_sin_h[at, :], t_sin_l[at, :] = split(sa * cb + ca * sb)
-        return carry
-
-    lax.fori_loop(0, block // NB, fill, 0)
+    t_cos_h, t_cos_l, t_sin_h, t_sin_l = (table.at[here_rows, :] for table in table_refs)
 
     def product(table_h, table_l, weight_h, weight_l):
         dot = functools.partial(jnp.dot, preferred_element_type=F32)
@@ -381,7 +405,6 @@
 
     even = product(t_cos_h, t_cos_l, w_cos_h, w_cos_l)
     odd = product(t_sin_h, t_sin_l, w_sin_h, w_sin_l)
-    here_rows = pl.ds(pl.multiple_of(step * block, block), block)
     if not fresh:
         even = even + cos_in[here_rows, :]
         odd = odd + sin_in[here_rows, :]
@@ -390,7 +413,7 @@
         sin_out[here_rows, :] = odd
         return
 
-    value_ref, slope_ref, found_v, found_s = refs[9:]
+    value_ref, slope_ref, found_v, found_s = refs[4:]
     half = lon // 2
 
     def narrowed(x):
@@ -448,17 +471,16 @@
             outs[offset][...] = found_v[pl.ds(start, REG_DEV), :]
 
 
-def synthesis(waves, pieces, held, closing, lon, top, regions, wide, starts, here):
+def synthesis(made, pieces, held, closing, lon, regions, wide, starts, here):
     block = min(512, lon // 2)
-    depth = waves.shape[1]
+    depth = made[0].shape[0]
     counts = tuple(piece.shape[1] for piece in pieces)
     width = pieces[0].shape[2]
     fresh = held is None
     prefetch = (starts, here) if closing else ()
-    operands = [waves, *pieces] + ([] if fresh else list(held))
+    operands = [*made, *pieces] + ([] if fresh else list(held))
     in_specs = [pl.BlockSpec(memory_space=pltpu.VMEM)] * len(operands)
-    scratch = [pltpu.VMEM((2 * (lon // 2 // NB + NB), depth), F32)]
-    scratch += [pltpu.VMEM((depth, 2 * width), BF16)] * 4 + [pltpu.VMEM((block, depth), BF16)] * 4
+    scratch = [pltpu.VMEM((depth, 2 * width), BF16)] * 4
     if closing:
         out_shape = [jax.ShapeDtypeStruct((REG_DEV, LANES), F32)] * wide
         scratch += [pltpu.VMEM((lon, LANES), F32)] * 2 + [pltpu.VMEM((regions, LANES), F32)] * 2
@@ -467,7 +489,7 @@
     out_specs = [pl.BlockSpec(memory_space=pltpu.VMEM)] * len(out_shape)
     return pl.pallas_call(
         functools.partial(
-            synthesis_kernel, counts, fresh, closing, (lon, top, regions, wide)
+            synthesis_kernel, counts, fresh, closing, (lon, regions, wide)
         ),
         grid_spec=pltpu.PrefetchScalarGridSpec(
             num_scalar_prefetch=len(prefetch),
@@ -564,20 +586,19 @@
         for chunk in range(late + 1)
     ]
     stages = (
-        own[: late - 1] + swapped[:-2] + sum(across[: late - 1], []),
-        own[late - 1 :] + swapped[-2:-1] + across[late - 1],
+        own + swapped[:-1] + sum(across[:late], []),
         swapped[-1:] + across[late],
     )
     held = None
+    waves = [jnp.concatenate([w for _, found in stage for w in found]) for stage in stages]
+    made = [tables(w.reshape(1, -1), lon, top) for w in tied((*waves, kept[-1]))[:-1]]
     for number, stage in enumerate(stages):
-        waves = jnp.concatenate([w for _, found in stage for w in found])
         held = synthesis(
-            waves.reshape(1, -1),
+            made[number],
             [array for array, _ in stage],
             held,
             number == len(stages) - 1,
             lon,
-            top,
             regions,
             wide,
             starts,
@@ -586,7 +607,13 @@
 
     found = [held[0]] + [shift(held[i], "wide", wide, i) for i in range(1, wide)]
     out = jax.ShapeDtypeStruct((members, REG_DEV, LANES // 2 // members), F32)
-    peak, peak_slope = pl.pallas_call(final_kernel, out_shape=[out] * 2, name="final")(*found)
+    peak, peak_slope = pl.pallas_call(
+        final_kernel,
+        in_specs=[pl.BlockSpec(memory_space=pltpu.VMEM)] * wide,
+        out_shape=[out] * 2,
+        compiler_params=pltpu.CompilerParams(vmem_limit_bytes=TABLES_VMEM),
+        name="final",
+    )(*found)
     return jnp.transpose(peak, (0, 2, 1)), jnp.transpose(peak_slope, (0, 2, 1))
 
 

time: 97.5 us -> 86.2 us (0.88)
  Pallas kernels: 65.4 us -> 59.1 us
  starting transfers between devices: 22.7 us -> 19.1 us
  local copies, waits for them, and re-layouts: 4.33 us -> 3.05 us
    pallas_call x3 -> x2, Pallas kernels: 19 us -> 13.4 us  [synthesis(): pl.pallas_call(functools.partial(synthesis_kernel, counts, fresh, closing...]
    pallas_call x5 -> x4, Pallas kernels: 45 us -> 40.3 us  [legendre_sums(): pl.pallas_call(functools.partial(legendre_kernel, first_unit, units, part...]
    pallas_call x1 -> x3, Pallas kernels: 1.43 us -> 5.4 us  [the longest x2 4.72 us: tables(): pl.pallas_call(functools.partial(tables_kernel, lon, top), in_specs=[held...]
    ppermute x13 -> x10, starting transfers between devices: 17.1 us -> 13.9 us  [swap(): return lax.ppermute(x, axis, [(i, i ^ step) for i in range(count)])]
    unnamed x18 -> x8, local copies, waits for them, and re-layouts: 2.53 us -> 1.35 us
  transfers between devices with their start and end apart: 16 -> 13, of which waited for: 3 -> 3; matrix products, arithmetic and copies ran while one was open for 3% -> 3% of each run, Pallas kernels for 52% -> 54%
where the time goes in v2:
time: 86.2 us; the launch traced here: 86 us
  Pallas kernels  59.1 us (69%)
  starting transfers between devices  19.1 us (22%)
  local copies, waits for them, and re-layouts  3.05 us (4%)
  waiting for transfers between devices  2.89 us (3%)
  other arithmetic  1.02 us (1%)
    pallas_call x4, Pallas kernels, legendre_sums(): pl.pallas_call(functools.partial(legendre_kernel, first_unit, units, part...  40.3 us
    ppermute x10, starting transfers between devices, swap(): return lax.ppermute(x, axis, [(i, i ^ step) for i in range(count)])  13.9 us
    pallas_call x2, Pallas kernels, synthesis(): pl.pallas_call(functools.partial(synthesis_kernel, counts, fresh, closing...  13.4 us
    ppermute x3, starting transfers between devices, shift(): lax.ppermute(x, axis, [(i, (i + step) % count) for i in range(count)])  5.18 us
    pallas_call x2, Pallas kernels, tables(): pl.pallas_call(functools.partial(tables_kernel, lon, top), in_specs=[held...  4.72 us
    ppermute x3, waiting for transfers between devices, shift(): lax.ppermute(x, axis, [(i, (i + step) % count) for i in range(count)])  2.87 us
  transfers between devices with their start and end apart: 13, of which 3 were waited for; matrix products, arithmetic and copies ran while one was open for 3% of the time, Pallas kernels for 54%

profile of v2, /device:TPU:1, one launch (start us, length us, event | category | flops | bytes accessed | tf_op | source)
XLA Modules:
  0.0 86.0 jit_solution(469467314640706004)
XLA Ops:
  0.6 0.7 copy-done
  1.3 0.7 copy-done.2
  2.0 8.2 %legendre.4 = (f32[2,64,256]{2,1,0:T(8,128)S(1)}, f32[2,64,256]{2,1,0:T(8,128)S(1)}, f32[2,64,256]{2,1,0:T(8,128)S(1)}, f32[2,64,256]{2,1,0:T(8,128)}, s32[4,128]{1,0:T(4,128)S(1)}) custom-call(s32[640]{0:T(1024)S(1)} %copy-done, s32[1]{0:T(128)} %bitcast.here_ref, s32[1,128]{1,0:T(1,128)S(1)} %bitcast.42, bf16[2,4,160,2,1281]{4,3,2,1,0:T(2,128)(2,1)} %s_hbm.7, ...), custom_call_target="tpu_custom_call" | custom-call | flops 671612928 | bytes 6558720 | tf_op jit(solution)/shard_map/legendre/pallas_call | solution.py:260
  10.2 3.2 %collective-permute-start = (f32[2,64,256]{2,1,0:T(8,128)S(1)}, f32[2,64,256]{2,1,0:T(8,128)S(1)}, u32[]{:S(2)}, u32[]{:S(2)}) collective-permute-start(f32[2,64,256]{2,1,0:T(8,128)S(1)} %get-tuple-element.62), channel_id=1, source_target_pairs={{0,2},{1,3},{2,0},{3,1},{4,6},{5,7},{6,4},{7,5},{8,10},{9,11},{10,... | collective-permute-start | bytes 393224 | tf_op jit(solution)/shard_map/ppermute | solution.py:515
  13.4 1.1 %collective-permute-start.1 = (f32[2,64,256]{2,1,0:T(8,128)}, f32[2,64,256]{2,1,0:T(8,128)S(1)}, u32[]{:S(2)}, u32[]{:S(2)}) collective-permute-start(f32[2,64,256]{2,1,0:T(8,128)} %get-tuple-element.63), channel_id=1, source_target_pairs={{0,3},{1,2},{2,1},{3,0},{4,7},{5,6},{6,5},{7,4},{8,11},{9,10},{10,... | collective-permute-start | bytes 393224 | tf_op jit(solution)/shard_map/ppermute | solution.py:515
  14.5 11.6 %legendre.5 = (f32[2,96,256]{2,1,0:T(8,128)S(1)}, f32[2,96,256]{2,1,0:T(8,128)S(1)}, f32[2,96,256]{2,1,0:T(8,128)}, f32[2,96,256]{2,1,0:T(8,128)}) custom-call(s32[640]{0:T(1024)S(1)} %copy-done, s32[1]{0:T(128)} %bitcast.here_ref, s32[4,128]{1,0:T(4,128)S(1)} %get-tuple-element.56.owner_ref, bf16[2,4,160,2,1281]{4,3,2,1,0:T(2,128)(2,1)} %s_hbm.7, ...), custom_call_target="tpu_custom_call" | custom-call | flops 1007419392 | bytes 9838080 | tf_op jit(solution)/shard_map/legendre/pallas_call | solution.py:260
  26.1 1.4 %collective-permute-start.2 = (f32[2,96,256]{2,1,0:T(8,128)}, f32[2,96,256]{2,1,0:T(8,128)S(1)}, u32[]{:S(2)}, u32[]{:S(2)}) collective-permute-start(f32[2,96,256]{2,1,0:T(8,128)} %get-tuple-element.67), channel_id=1, source_target_pairs={{0,2},{1,3},{2,0},{3,1},{4,6},{5,7},{6,4},{7,5},{8,10},{9,11},{10,... | collective-permute-start | bytes 589832 | tf_op jit(solution)/shard_map/ppermute | solution.py:515
  27.5 0.9 %collective-permute-start.3 = (f32[2,96,256]{2,1,0:T(8,128)}, f32[2,96,256]{2,1,0:T(8,128)S(1)}, u32[]{:S(2)}, u32[]{:S(2)}) collective-permute-start(f32[2,96,256]{2,1,0:T(8,128)} %get-tuple-element.68), channel_id=1, source_target_pairs={{0,3},{1,2},{2,1},{3,0},{4,7},{5,6},{6,5},{7,4},{8,11},{9,10},{10,... | collective-permute-start | bytes 589832 | tf_op jit(solution)/shard_map/ppermute | solution.py:515
  28.5 0.2 copy.8
  28.7 0.2 reshape.42
  28.9 0.6 gather_fusion
  29.5 11.6 %legendre.6 = (f32[2,96,256]{2,1,0:T(8,128)S(1)}, f32[2,96,256]{2,1,0:T(8,128)S(1)}, f32[2,96,256]{2,1,0:T(8,128)}, f32[2,96,256]{2,1,0:T(8,128)}) custom-call(s32[640]{0:T(1024)S(1)} %copy-done.1, s32[1]{0:T(128)} %bitcast.here_ref, s32[4,128]{1,0:T(4,128)S(1)} %get-tuple-element.56.owner_ref, bf16[2,4,160,2,1281]{4,3,2,1,0:T(2,128)(2,1)} %s_hbm.7, ...), custom_call_target="tpu_custom_call" | custom-call | flops 1007419392 | bytes 9838080 | tf_op jit(solution)/shard_map/legendre/pallas_call | solution.py:260
  41.1 0.4 collective-permute-start.7
  41.7 0.6 slice.51
  42.4 2.3 %collective-permute-start.8 = (f32[2,96,256]{2,1,0:T(8,128)}, f32[2,96,256]{2,1,0:T(8,128)S(1)}, u32[]{:S(2)}, u32[]{:S(2)}) collective-permute-start(f32[2,96,256]{2,1,0:T(8,128)} %get-tuple-element.96), channel_id=1, source_target_pairs={{0,2},{1,3},{2,0},{3,1},{4,6},{5,7},{6,4},{7,5},{8,10},{9,11},{10,... | collective-permute-start | bytes 589832 | tf_op jit(solution)/shard_map/ppermute | solution.py:515
  44.7 0.9 %collective-permute-start.9 = (f32[2,96,256]{2,1,0:T(8,128)}, f32[2,96,256]{2,1,0:T(8,128)S(1)}, u32[]{:S(2)}, u32[]{:S(2)}) collective-permute-start(f32[2,96,256]{2,1,0:T(8,128)} %get-tuple-element.97), channel_id=1, source_target_pairs={{0,3},{1,2},{2,1},{3,0},{4,7},{5,6},{6,5},{7,4},{8,11},{9,10},{10,... | collective-permute-start | bytes 589832 | tf_op jit(solution)/shard_map/ppermute | solution.py:515
  45.6 0.7 pad_add_fusion.2.refs_0_
  46.5 8.9 %legendre.7 = (f32[2,64,256]{2,1,0:T(8,128)S(1)}, f32[2,64,256]{2,1,0:T(8,128)S(1)}, f32[2,64,256]{2,1,0:T(8,128)S(1)}, f32[2,64,256]{2,1,0:T(8,128)}) custom-call(s32[640]{0:T(1024)S(1)} %copy-done.1, s32[1]{0:T(128)} %bitcast.here_ref, s32[4,128]{1,0:T(4,128)S(1)} %get-tuple-element.56.owner_ref, bf16[2,4,160,2,1281]{4,3,2,1,0:T(2,128)(2,1)} %s_hbm.7, ...), custom_call_target="tpu_custom_call" | custom-call | flops 671612928 | bytes 6558720 | tf_op jit(solution)/shard_map/legendre/pallas_call | solution.py:260
  55.4 0.5 collective-permute-start.4
  55.9 2.2 %collective-permute-start.5 = (f32[2,64,256]{2,1,0:T(8,128)S(1)}, f32[2,64,256]{2,1,0:T(8,128)S(1)}, u32[]{:S(2)}, u32[]{:S(2)}) collective-permute-start(f32[2,64,256]{2,1,0:T(8,128)S(1)} %get-tuple-element.78), channel_id=1, source_target_pairs={{0,2},{1,3},{2,0},{3,1},{4,6},{5,7},{6,4},{7,5},{8,10},{9,11},{10,... | collective-permute-start | bytes 393224 | tf_op jit(solution)/shard_map/ppermute | solution.py:515
  58.1 1.1 %tables.2 = (f32[192,8]{1,0:T(8,128)S(1)}, bf16[1024,192]{1,0:T(8,128)(2,1)S(1)}, bf16[1024,192]{1,0:T(8,128)(2,1)S(1)}, bf16[1024,192]{1,0:T(8,128)(2,1)S(1)}, bf16[1024,192]{1,0:T(8,128)(2,1)S(1)}) custom-call(s32[1,192]{1,0:T(1,128)S(1)} %bitcast.41), custom_call_target="tpu_custom_call" | custom-call | flops 6291456 | bytes 1572864 | tf_op jit(solution)/shard_map/tables/pallas_call | solution.py:345
  59.2 3.6 %tables.3 = (f32[1088,8]{1,0:T(8,128)S(1)}, bf16[1024,1088]{1,0:T(8,128)(2,1)S(1)}, bf16[1024,1088]{1,0:T(8,128)(2,1)S(1)}, bf16[1024,1088]{1,0:T(8,128)(2,1)S(1)}, bf16[1024,1088]{1,0:T(8,128)(2,1)S(1)}) custom-call(s32[1,1088]{1,0:T(1,128)S(1)} %reshape.44.waves_ref), custom_call_target="tpu_custom_call" | custom-call | flops 35651584 | bytes 8912896 | tf_op jit(solution)/shard_map/tables/pallas_call | solution.py:345
  62.9 1.0 %collective-permute-start.6 = (f32[2,64,256]{2,1,0:T(8,128)}, f32[2,64,256]{2,1,0:T(8,128)S(1)}, u32[]{:S(2)}, u32[]{:S(2)}) collective-permute-start(f32[2,64,256]{2,1,0:T(8,128)} %get-tuple-element.79), channel_id=1, source_target_pairs={{0,3},{1,2},{2,1},{3,0},{4,7},{5,6},{6,5},{7,4},{8,11},{9,10},{10,... | collective-permute-start | bytes 393224 | tf_op jit(solution)/shard_map/ppermute | solution.py:515
  63.8 9.5 %synthesis.2 = (f32[1024,512]{1,0:T(8,128)S(1)}, f32[1024,512]{1,0:T(8,128)S(1)}) custom-call(f32[1088,8]{1,0:T(8,128)S(1)} %get-tuple-element.81.refs_0_, bf16[1024,1088]{1,0:T(8,128)(2,1)S(1)} %get-tuple-element.82.refs_1_, bf16[1024,1088]{1,0:T(8,128)(2,1)S(1)} %get-tuple-element.83.refs_2_, bf16[1024,1088]{1,0:T(8,128)(2,1)S(1)} %get-tuple-element.84.refs_3_, ...), custom_call_target="tpu_custom_call" | custom-call | flops 6845104128 | bytes 8388608 | tf_op jit(solution)/shard_map/synthesis/pallas_call | solution.py:490
  73.4 3.9 %synthesis.3 = (f32[16,128]{1,0:T(8,128)S(1)}, f32[16,128]{1,0:T(8,128)S(1)}, f32[16,128]{1,0:T(8,128)S(1)}, f32[16,128]{1,0:T(8,128)S(1)}) custom-call(s32[66]{0:T(128)S(1)} %pad_add_fusion.2.refs_0_, s32[1]{0:T(128)} %bitcast.3.refs_1_, f32[192,8]{1,0:T(8,128)S(1)} %get-tuple-element.72.refs_2_, bf16[1024,192]{1,0:T(8,128)(2,1)S(1)} %get-tuple-element.73.refs_3_, ...), custom_call_target="tpu_custom_call" | custom-call | flops 1207959552 | bytes 8388608 | tf_op jit(solution)/shard_map/synthesis/pallas_call | solution.py:490
  77.3 4.7 %collective-permute-start.10 = (f32[16,128]{1,0:T(8,128)S(1)}, f32[16,128]{1,0:T(8,128)S(1)}, u32[]{:S(2)}, u32[]{:S(2)}) collective-permute-start(f32[16,128]{1,0:T(8,128)S(1)} %get-tuple-element.101), channel_id=1, source_target_pairs={{0,4},{4,8},{8,12},{12,0},{1,5},{5,9},{9,13},{13,1},{2,6},{6,10},{... | collective-permute-start | bytes 24584 | tf_op jit(solution)/shard_map/ppermute | solution.py:511
  82.0 0.3 collective-permute-start.11
  82.2 0.2 collective-permute-start.12
  82.5 0.3 collective-permute-done.10.refs_1_
  82.8 1.7 %collective-permute-done.11.refs_2_ = f32[16,128]{1,0:T(8,128)S(1)} collective-permute-done((f32[16,128]{1,0:T(8,128)S(1)}, f32[16,128]{1,0:T(8,128)S(1)}, u32[]{:S(2)}, u32[]{:S(2)}) %collective-permute-start.11) | collective-permute-done | bytes 8224 | tf_op jit(solution)/shard_map/ppermute | solution.py:511
  84.5 0.8 collective-permute-done.12.refs_3_
  85.3 0.7 final.1
  (29 shorter events, 0.5 us)
Async XLA Ops:
  0.6 0.7 copy-start
  1.3 0.7 copy-start.2
  10.2 19.3 %collective-permute-start = (f32[2,64,256]{2,1,0:T(8,128)S(1)}, f32[2,64,256]{2,1,0:T(8,128)S(1)}, u32[]{:S(2)}, u32[]{:S(2)}) collective-permute-start(f32[2,64,256]{2,1,0:T(8,128)S(1)} %get-tuple-element.62), channel_id=1, source_target_pairs={{0,2},{1,3},{2,0},{3,1},{4,6},{5,7},{6,4},{7,5},{8,10},{9,11},{10,... | collective-permute-start | bytes 393224 | tf_op jit(solution)/shard_map/ppermute | solution.py:515
  13.4 16.1 %collective-permute-start.1 = (f32[2,64,256]{2,1,0:T(8,128)}, f32[2,64,256]{2,1,0:T(8,128)S(1)}, u32[]{:S(2)}, u32[]{:S(2)}) collective-permute-start(f32[2,64,256]{2,1,0:T(8,128)} %get-tuple-element.63), channel_id=1, source_target_pairs={{0,3},{1,2},{2,1},{3,0},{4,7},{5,6},{6,5},{7,4},{8,11},{9,10},{10,... | collective-permute-start | bytes 393224 | tf_op jit(solution)/shard_map/ppermute | solution.py:515
  14.5 15.0 %copy-start.1 = (s32[640]{0:T(1024)S(1)}, s32[640]{0:T(1024)}, u32[]{:S(2)}) copy-start(s32[640]{0:T(1024)} %pair_ref.7) | copy-start | bytes 7684
  26.1 20.4 %collective-permute-start.2 = (f32[2,96,256]{2,1,0:T(8,128)}, f32[2,96,256]{2,1,0:T(8,128)S(1)}, u32[]{:S(2)}, u32[]{:S(2)}) collective-permute-start(f32[2,96,256]{2,1,0:T(8,128)} %get-tuple-element.67), channel_id=1, source_target_pairs={{0,2},{1,3},{2,0},{3,1},{4,6},{5,7},{6,4},{7,5},{8,10},{9,11},{10,... | collective-permute-start | bytes 589832 | tf_op jit(solution)/shard_map/ppermute | solution.py:515
  27.5 18.9 %collective-permute-start.3 = (f32[2,96,256]{2,1,0:T(8,128)}, f32[2,96,256]{2,1,0:T(8,128)S(1)}, u32[]{:S(2)}, u32[]{:S(2)}) collective-permute-start(f32[2,96,256]{2,1,0:T(8,128)} %get-tuple-element.68), channel_id=1, source_target_pairs={{0,3},{1,2},{2,1},{3,0},{4,7},{5,6},{6,5},{7,4},{8,11},{9,10},{10,... | collective-permute-start | bytes 589832 | tf_op jit(solution)/shard_map/ppermute | solution.py:515
  29.5 12.1 %copy-start.3 = (s32[2048]{0:T(1024)S(1)}, s32[2048]{0:T(1024)}, u32[]{:S(2)}) copy-start(s32[2048]{0:T(1024)} %param.9) | copy-start | bytes 24580
  41.1 22.7 %collective-permute-start.7 = (f32[2,256,256]{2,1,0:T(8,128)S(1)}, f32[2,256,256]{2,1,0:T(8,128)S(1)}, u32[]{:S(2)}, u32[]{:S(2)}) collective-permute-start(f32[2,256,256]{2,1,0:T(8,128)S(1)} %pad_maximum_fusion), channel_id=1, source_target_pairs={{0,1},{1,0},{2,3},{3,2},{4,5},{5,4},{6,7},{7,6},{8,9},{9,8},{10,11... | collective-permute-start | bytes 1572872 | tf_op jit(solution)/shard_map/ppermute | solution.py:515
  42.4 20.5 %collective-permute-start.8 = (f32[2,96,256]{2,1,0:T(8,128)}, f32[2,96,256]{2,1,0:T(8,128)S(1)}, u32[]{:S(2)}, u32[]{:S(2)}) collective-permute-start(f32[2,96,256]{2,1,0:T(8,128)} %get-tuple-element.96), channel_id=1, source_target_pairs={{0,2},{1,3},{2,0},{3,1},{4,6},{5,7},{6,4},{7,5},{8,10},{9,11},{10,... | collective-permute-start | bytes 589832 | tf_op jit(solution)/shard_map/ppermute | solution.py:515
  44.7 19.2 %collective-permute-start.9 = (f32[2,96,256]{2,1,0:T(8,128)}, f32[2,96,256]{2,1,0:T(8,128)S(1)}, u32[]{:S(2)}, u32[]{:S(2)}) collective-permute-start(f32[2,96,256]{2,1,0:T(8,128)} %get-tuple-element.97), channel_id=1, source_target_pairs={{0,3},{1,2},{2,1},{3,0},{4,7},{5,6},{6,5},{7,4},{8,11},{9,10},{10,... | collective-permute-start | bytes 589832 | tf_op jit(solution)/shard_map/ppermute | solution.py:515
  55.4 18.0 %collective-permute-start.4 = (f32[2,64,256]{2,1,0:T(8,128)S(1)}, f32[2,64,256]{2,1,0:T(8,128)S(1)}, u32[]{:S(2)}, u32[]{:S(2)}) collective-permute-start(f32[2,64,256]{2,1,0:T(8,128)S(1)} %get-tuple-element.77), channel_id=1, source_target_pairs={{0,1},{1,0},{2,3},{3,2},{4,5},{5,4},{6,7},{7,6},{8,9},{9,8},{10,11... | collective-permute-start | bytes 393224 | tf_op jit(solution)/shard_map/ppermute | solution.py:515
  55.9 17.4 %collective-permute-start.5 = (f32[2,64,256]{2,1,0:T(8,128)S(1)}, f32[2,64,256]{2,1,0:T(8,128)S(1)}, u32[]{:S(2)}, u32[]{:S(2)}) collective-permute-start(f32[2,64,256]{2,1,0:T(8,128)S(1)} %get-tuple-element.78), channel_id=1, source_target_pairs={{0,2},{1,3},{2,0},{3,1},{4,6},{5,7},{6,4},{7,5},{8,10},{9,11},{10,... | collective-permute-start | bytes 393224 | tf_op jit(solution)/shard_map/ppermute | solution.py:515
  62.9 10.5 %collective-permute-start.6 = (f32[2,64,256]{2,1,0:T(8,128)}, f32[2,64,256]{2,1,0:T(8,128)S(1)}, u32[]{:S(2)}, u32[]{:S(2)}) collective-permute-start(f32[2,64,256]{2,1,0:T(8,128)} %get-tuple-element.79), channel_id=1, source_target_pairs={{0,3},{1,2},{2,1},{3,0},{4,7},{5,6},{6,5},{7,4},{8,11},{9,10},{10,... | collective-permute-start | bytes 393224 | tf_op jit(solution)/shard_map/ppermute | solution.py:515
  77.3 5.5 %collective-permute-start.10 = (f32[16,128]{1,0:T(8,128)S(1)}, f32[16,128]{1,0:T(8,128)S(1)}, u32[]{:S(2)}, u32[]{:S(2)}) collective-permute-start(f32[16,128]{1,0:T(8,128)S(1)} %get-tuple-element.101), channel_id=1, source_target_pairs={{0,4},{4,8},{8,12},{12,0},{1,5},{5,9},{9,13},{13,1},{2,6},{6,10},{... | collective-permute-start | bytes 24584 | tf_op jit(solution)/shard_map/ppermute | solution.py:511
  82.0 2.5 %collective-permute-start.11 = (f32[16,128]{1,0:T(8,128)S(1)}, f32[16,128]{1,0:T(8,128)S(1)}, u32[]{:S(2)}, u32[]{:S(2)}) collective-permute-start(f32[16,128]{1,0:T(8,128)S(1)} %get-tuple-element.102), channel_id=1, source_target_pairs={{0,8},{4,12},{8,0},{12,4},{1,9},{5,13},{9,1},{13,5},{2,10},{6,14},... | collective-permute-start | bytes 24584 | tf_op jit(solution)/shard_map/ppermute | solution.py:511
  82.2 3.1 %collective-permute-start.12 = (f32[16,128]{1,0:T(8,128)S(1)}, f32[16,128]{1,0:T(8,128)S(1)}, u32[]{:S(2)}, u32[]{:S(2)}) collective-permute-start(f32[16,128]{1,0:T(8,128)S(1)} %get-tuple-element.103), channel_id=1, source_target_pairs={{0,12},{4,0},{8,4},{12,8},{1,13},{5,1},{9,5},{13,9},{2,14},{6,2},{... | collective-permute-start | bytes 24584 | tf_op jit(solution)/shard_map/ppermute | solution.py:511

commit v3 on v2

--- a/solution.py
+++ b/solution.py
@@ -107,7 +107,7 @@
     return lax.broadcasted_iota(jnp.int32, shape, axis)
 
 
-def latitude_lanes(owner, here, parts):
+def latitude_lanes(owner, here, parts, members, steps):
     square = (LANES, LANES)
     row = jnp.broadcast_to(owner.astype(F32), square)
     column = row.T
@@ -118,12 +118,17 @@
     half = LANES // 2
     lane_of = jnp.where(first < half, first, half + LANES - 1 - first).astype(F32)
     share = LANES // parts
-    rows = []
+    shape = (2 * members * steps, LANES)
+    at = iota(shape, 0) // 2
+    at = at % steps * members + at // steps
+    relative = lax.bitwise_xor(iota(shape, 1) // share, at % parts)
+    lanes = jnp.zeros(shape, F32)
     for step in range(parts):
         owner_index = lax.bitwise_xor(here, jnp.int32(step))
         target = (owner_index * share + second % share).astype(F32)
-        rows.append(jnp.sum(jnp.where(place == target, lane_of, 0.0), axis=0, keepdims=True))
-    return jnp.concatenate(rows, axis=0).astype(jnp.int32)
+        found = jnp.sum(jnp.where(place == target, lane_of, 0.0), axis=0, keepdims=True)
+        lanes = jnp.where(relative == step, found, lanes)
+    return lanes.astype(jnp.int32)
 
 
 def legendre_kernel(first_unit, units, parts, known, pair_ref, here_ref, owner_ref, s_hbm, l_hbm, *refs):
@@ -144,12 +149,7 @@
 
     def copies(which):
         side = lax.rem(which, 2)
-        at = pl.multiple_of((first_unit + which) * slots, slots)
-        found = [
-            pltpu.make_async_copy(
-                s_hbm.at[:, :, pl.ds(at, slots)], s_buf.at[side], s_sem.at[side]
-            )
-        ]
+        found = []
         at = pl.multiple_of((first_unit + which) * pairs, pairs)
         for cut in range(cuts):
             span = pl.ds(cut * depth, depth if cut < cuts - 1 else length - cut * depth)
@@ -158,6 +158,12 @@
                     l_hbm.at[span, pl.ds(at, pairs)], l_buf.at[side, span], l_sem.at[side, cut]
                 )
             )
+        at = pl.multiple_of((first_unit + which) * slots, slots)
+        found.append(
+            pltpu.make_async_copy(
+                s_hbm.at[:, :, pl.ds(at, slots)], s_buf.at[side], s_sem.at[side]
+            )
+        )
         return found
 
     @pl.when(unit == 0)
@@ -165,7 +171,7 @@
         for copy in copies(jnp.int32(0)):
             copy.start()
         if not known:
-            lanes_ref[...] = latitude_lanes(owner_ref[...], here, parts)
+            lanes_ref[...] = latitude_lanes(owner_ref[...], here, parts, members, steps)
 
     @pl.when(unit + 1 < units)
     def _():
@@ -174,24 +180,24 @@
 
     side = lax.rem(unit, 2)
     arriving = copies(unit)
-    arriving[0].wait()
-
-    spot = iota((rows, top), 1)
-    sign = jnp.where(spot % 2 == 0, 1.0, -1.0).astype(BF16)
+
+    spot = iota((8, top), 1)
+    sign = jnp.where(iota((rows, top), 1) % 2 == 0, 1.0, -1.0).astype(BF16)
     base = here * (pair_ref.shape[0] // parts) + (first_unit + unit) * slots
     for cut in range(cuts):
-        arriving[1 + cut].wait()
+        arriving[cut].wait()
         for at in range(cut * depth, (cut + 1) * depth, TURN):
             table[:, at : at + TURN, :] = jnp.swapaxes(l_buf[side, at : at + TURN], 0, 1)
 
+    arriving[cuts].wait()
     for pair in range(pairs):
         masked = []
         for slot in (2 * pair, 2 * pair + 1):
             x = s_buf[side, :, :, slot].reshape(rows, length)[:, :top]
             first_len = top - pair_ref[base + slot]
-            lead = x * jnp.where(spot < first_len, 1.0, 0.0).astype(BF16)
-            tail = x - lead
-            masked += [lead, lead * sign, tail, tail * sign]
+            inside = jnp.where(spot < first_len, 1.0, 0.0)
+            lead = x * jnp.concatenate([inside] * (rows // 8), axis=0).astype(BF16)
+            masked += [lead, lead * sign, x, x * sign]
         total[pair] = jnp.dot(
             jnp.concatenate(masked, axis=0), table[pair], preferred_element_type=F32
         )
@@ -199,6 +205,7 @@
     low = iota((rows, LANES), 1) < LANES // 2
 
     ends[...] = l_buf[side, top].astype(F32)
+    lanes = lanes_ref[...]
 
     def combine(pair, carry):
         end = ends[pl.ds(pair, 1), :]
@@ -207,12 +214,12 @@
             turned = jnp.where((top - pair_ref[base + slot]) % 2 == 0, 1.0, -1.0).astype(F32)
             last = s_buf[side, :, :, slot, :, top:].reshape(rows, 1).astype(F32) * end
             at = 4 * odd_slot * rows
-            north_lead, south_lead, north_tail, south_tail = (
+            north_lead, south_lead, north, south = (
                 total[pair, at + i * rows : at + (i + 1) * rows, :] for i in range(4)
             )
             found = (
                 (north_lead, south_lead),
-                (north_tail + last, (south_tail + last) * turned),
+                (north - north_lead + last, (south - south_lead + last) * turned),
             )
             for which, (north, south) in enumerate(found):
                 if odd_slot:
@@ -220,7 +227,9 @@
                 else:
                     both = jnp.where(low, north, pltpu.roll(south, LANES // 2, 1))
                 at = pl.multiple_of((2 * slot + which) * rows, rows)
-                sums[pl.ds(at, rows), :] = both
+                sums[pl.ds(at, rows), :] = jnp.take_along_axis(
+                    both, lanes, axis=1, mode="promise_in_bounds"
+                )
         return carry
 
     [combine(i, 0) for i in range(pairs)]
@@ -230,18 +239,17 @@
     per = LANES // share
     group = iota((waves, LANES), 1) // share
     mine = pl.ds(pl.multiple_of(unit * waves, waves), waves)
-    for step in range(parts):
-        index = jnp.broadcast_to(lanes_ref[step : step + 1, :], (waves, LANES))
-        for part in range(2):
-            for block in range(times // per):
-                built = None
-                for place in range(per):
-                    at = block * per + place
-                    step_of, member = at // members, at % members
-                    row = (member * steps + step_of) * 2 + part
-                    source = sums[pl.ds(row, waves, stride=rows), :]
-                    moved = jnp.take_along_axis(source, index, axis=1, mode="promise_in_bounds")
-                    built = moved if place == 0 else jnp.where(group == place, moved, built)
+    for part in range(2):
+        for block in range(times // per):
+            sources = []
+            for place in range(per):
+                step_of, member = (block * per + place) // members, (block * per + place) % members
+                row = (member * steps + step_of) * 2 + part
+                sources.append(sums[pl.ds(row, waves, stride=rows), :])
+            for step in range(parts):
+                built = sources[step]
+                for place in range(1, per):
+                    built = jnp.where(group == place, sources[place ^ step], built)
                 outs[step][part, mine, block * LANES : (block + 1) * LANES] = built
 
 
@@ -254,7 +262,7 @@
     known = first_unit > 0
     out = [jax.ShapeDtypeStruct((2, units * waves, width), F32)] * parts
     if not known:
-        out = out + [jax.ShapeDtypeStruct((parts, LANES), jnp.int32)]
+        out = out + [jax.ShapeDtypeStruct((2 * times, LANES), jnp.int32)]
     here_spec = pl.BlockSpec(memory_space=pltpu.VMEM)
     away = pl.BlockSpec(memory_space=pltpu.HBM)
     return pl.pallas_call(
@@ -305,6 +313,20 @@
     return c, s
 
 
+def regrouped(x, step, share):
+    if step == 0:
+        return x
+    shape = (x.shape[0], LANES)
+    index = lax.bitwise_xor(iota(shape, 1), jnp.int32(step * share))
+    return jnp.concatenate(
+        [
+            jnp.take_along_axis(x[:, i : i + LANES], index, axis=1, mode="promise_in_bounds")
+            for i in range(0, x.shape[1], LANES)
+        ],
+        axis=1,
+    )
+
+
 def tables_kernel(lon, top, waves_ref, coef_ref, t_cos_h, t_cos_l, t_sin_h, t_sin_l, base_ref):
     half, depth = t_cos_h.shape
     coarse = half // NB
@@ -357,7 +379,7 @@
 
 
 def synthesis_kernel(counts, fresh, closing, shape, *refs):
-    lon, regions, wide = shape
+    lon, regions, wide, share = shape
     refs = list(refs)
     if closing:
         starts_ref, here_ref = refs.pop(0), refs.pop(0)
@@ -378,11 +400,11 @@
     @pl.when(step == 0)
     def _():
         at = 0
-        for piece, count in zip(pieces, counts):
+        for piece, (count, step_of) in zip(pieces, counts):
             span = slice(at, at + count)
             coef = coef_ref[span, :]
             c, s, rate = coef[:, 0:1], coef[:, 1:2], coef[:, 2:3]
-            real, imag = piece[0], piece[1]
+            real, imag = (regrouped(piece[i], step_of, share) for i in range(2))
             p0 = real * c - imag * s
             p1 = real * s + imag * c
             for index, value in enumerate((p0, rate * p1)):
@@ -471,10 +493,10 @@
             outs[offset][...] = found_v[pl.ds(start, REG_DEV), :]
 
 
-def synthesis(made, pieces, held, closing, lon, regions, wide, starts, here):
+def synthesis(made, pieces, sources, held, closing, lon, regions, wide, share, starts, here):
     block = min(512, lon // 2)
     depth = made[0].shape[0]
-    counts = tuple(piece.shape[1] for piece in pieces)
+    counts = tuple((piece.shape[1], source) for piece, source in zip(pieces, sources))
     width = pieces[0].shape[2]
     fresh = held is None
     prefetch = (starts, here) if closing else ()
@@ -489,7 +511,7 @@
     out_specs = [pl.BlockSpec(memory_space=pltpu.VMEM)] * len(out_shape)
     return pl.pallas_call(
         functools.partial(
-            synthesis_kernel, counts, fresh, closing, (lon, regions, wide)
+            synthesis_kernel, counts, fresh, closing, (lon, regions, wide, share)
         ),
         grid_spec=pltpu.PrefetchScalarGridSpec(
             num_scalar_prefetch=len(prefetch),
@@ -576,7 +598,7 @@
         bounds.append(bounds[-1] + units * per_unit)
 
     def piece(array, source, chunks):
-        return array, [waves_of[source, bounds[i] : bounds[i + 1]] for i in chunks]
+        return array, source, [waves_of[source, bounds[i] : bounds[i + 1]] for i in chunks]
 
     late = len(CHUNKS) - 1
     own = [piece(kept[i], 0, (i,)) for i in range(late + 1)]
@@ -590,17 +612,19 @@
         swapped[-1:] + across[late],
     )
     held = None
-    waves = [jnp.concatenate([w for _, found in stage for w in found]) for stage in stages]
+    waves = [jnp.concatenate([w for _, _, found in stage for w in found]) for stage in stages]
     made = [tables(w.reshape(1, -1), lon, top) for w in tied((*waves, kept[-1]))[:-1]]
     for number, stage in enumerate(stages):
         held = synthesis(
             made[number],
-            [array for array, _ in stage],
+            [array for array, _, _ in stage],
+            [source for _, source, _ in stage],
             held,
             number == len(stages) - 1,
             lon,
             regions,
             wide,
+            LANES // parts,
             starts,
             here_wide.reshape(1),
         )

time: 86.2 us -> 82.1 us (0.952)
  Pallas kernels: 59.1 us -> 53.4 us
  starting transfers between devices: 19.1 us -> 20.2 us
    pallas_call x4, Pallas kernels: 40.3 us -> 34.4 us  [legendre_sums(): pl.pallas_call(functools.partial(legendre_kernel, first_unit, units, part...]
  transfers between devices with their start and end apart: 13 -> 13, of which waited for: 3 -> 4; matrix products, arithmetic and copies ran while one was open for 3% -> 3% of each run, Pallas kernels for 54% -> 51%
where the time goes in v3:
time: 82.1 us; the launch traced here: 81.9 us
  Pallas kernels  53.4 us (65%)
  starting transfers between devices  20.2 us (25%)
  waiting for transfers between devices  3.37 us (4%)
  local copies, waits for them, and re-layouts  3.05 us (4%)
  other arithmetic  1.02 us (1%)
    pallas_call x4, Pallas kernels, legendre_sums(): pl.pallas_call(functools.partial(legendre_kernel, first_unit, units, part...  34.4 us
    ppermute x10, starting transfers between devices, swap(): return lax.ppermute(x, axis, [(i, i ^ step) for i in range(count)])  14.7 us
    pallas_call x2, Pallas kernels, synthesis(): pl.pallas_call(functools.partial(synthesis_kernel, counts, fresh, closing...  13.8 us
    ppermute x3, starting transfers between devices, shift(): lax.ppermute(x, axis, [(i, (i + step) % count) for i in range(count)])  5.53 us
    pallas_call x2, Pallas kernels, tables(): pl.pallas_call(functools.partial(tables_kernel, lon, top), in_specs=[held...  4.54 us
    ppermute x3, waiting for transfers between devices, shift(): lax.ppermute(x, axis, [(i, (i + step) % count) for i in range(count)])  2.87 us
  transfers between devices with their start and end apart: 13, of which 4 were waited for; matrix products, arithmetic and copies ran while one was open for 3% of the time, Pallas kernels for 51%

profile of v3, /device:TPU:1, one launch (start us, length us, event | category | flops | bytes accessed | tf_op | source)
XLA Modules:
  0.0 81.9 jit_solution(7245851201577462450)
XLA Ops:
  0.6 0.7 copy-done
  1.3 0.7 copy-done.2
  2.0 7.0 %legendre.4 = (f32[2,64,256]{2,1,0:T(8,128)S(1)}, f32[2,64,256]{2,1,0:T(8,128)S(1)}, f32[2,64,256]{2,1,0:T(8,128)S(1)}, f32[2,64,256]{2,1,0:T(8,128)}, s32[16,128]{1,0:T(8,128)S(1)}) custom-call(s32[640]{0:T(1024)S(1)} %copy-done, s32[1]{0:T(128)} %bitcast.here_ref, s32[1,128]{1,0:T(1,128)S(1)} %bitcast.42, bf16[2,4,160,2,1281]{4,3,2,1,0:T(2,128)(2,1)} %s_hbm.7, ...), custom_call_target="tpu_custom_call" | custom-call | flops 671612928 | bytes 6558720 | tf_op jit(solution)/shard_map/legendre/pallas_call | solution.py:268
  9.0 3.2 %collective-permute-start = (f32[2,64,256]{2,1,0:T(8,128)S(1)}, f32[2,64,256]{2,1,0:T(8,128)S(1)}, u32[]{:S(2)}, u32[]{:S(2)}) collective-permute-start(f32[2,64,256]{2,1,0:T(8,128)S(1)} %get-tuple-element.62), channel_id=1, source_target_pairs={{0,2},{1,3},{2,0},{3,1},{4,6},{5,7},{6,4},{7,5},{8,10},{9,11},{10,... | collective-permute-start | bytes 393224 | tf_op jit(solution)/shard_map/ppermute | solution.py:537
  12.2 1.1 %collective-permute-start.1 = (f32[2,64,256]{2,1,0:T(8,128)}, f32[2,64,256]{2,1,0:T(8,128)S(1)}, u32[]{:S(2)}, u32[]{:S(2)}) collective-permute-start(f32[2,64,256]{2,1,0:T(8,128)} %get-tuple-element.63), channel_id=1, source_target_pairs={{0,3},{1,2},{2,1},{3,0},{4,7},{5,6},{6,5},{7,4},{8,11},{9,10},{10,... | collective-permute-start | bytes 393224 | tf_op jit(solution)/shard_map/ppermute | solution.py:537
  13.3 9.9 %legendre.5 = (f32[2,96,256]{2,1,0:T(8,128)S(1)}, f32[2,96,256]{2,1,0:T(8,128)S(1)}, f32[2,96,256]{2,1,0:T(8,128)}, f32[2,96,256]{2,1,0:T(8,128)}) custom-call(s32[640]{0:T(1024)S(1)} %copy-done, s32[1]{0:T(128)} %bitcast.here_ref, s32[16,128]{1,0:T(8,128)S(1)} %get-tuple-element.56.owner_ref, bf16[2,4,160,2,1281]{4,3,2,1,0:T(2,128)(2,1)} %s_hbm.7, ...), custom_call_target="tpu_custom_call" | custom-call | flops 1007419392 | bytes 9838080 | tf_op jit(solution)/shard_map/legendre/pallas_call | solution.py:268
  23.2 1.4 %collective-permute-start.2 = (f32[2,96,256]{2,1,0:T(8,128)}, f32[2,96,256]{2,1,0:T(8,128)S(1)}, u32[]{:S(2)}, u32[]{:S(2)}) collective-permute-start(f32[2,96,256]{2,1,0:T(8,128)} %get-tuple-element.67), channel_id=1, source_target_pairs={{0,2},{1,3},{2,0},{3,1},{4,6},{5,7},{6,4},{7,5},{8,10},{9,11},{10,... | collective-permute-start | bytes 589832 | tf_op jit(solution)/shard_map/ppermute | solution.py:537
  24.7 0.9 %collective-permute-start.3 = (f32[2,96,256]{2,1,0:T(8,128)}, f32[2,96,256]{2,1,0:T(8,128)S(1)}, u32[]{:S(2)}, u32[]{:S(2)}) collective-permute-start(f32[2,96,256]{2,1,0:T(8,128)} %get-tuple-element.68), channel_id=1, source_target_pairs={{0,3},{1,2},{2,1},{3,0},{4,7},{5,6},{6,5},{7,4},{8,11},{9,10},{10,... | collective-permute-start | bytes 589832 | tf_op jit(solution)/shard_map/ppermute | solution.py:537
  25.8 0.2 reshape.42
  26.0 0.6 gather_fusion
  26.6 9.9 %legendre.6 = (f32[2,96,256]{2,1,0:T(8,128)S(1)}, f32[2,96,256]{2,1,0:T(8,128)S(1)}, f32[2,96,256]{2,1,0:T(8,128)}, f32[2,96,256]{2,1,0:T(8,128)}) custom-call(s32[640]{0:T(1024)S(1)} %copy-done.1, s32[1]{0:T(128)} %bitcast.here_ref, s32[16,128]{1,0:T(8,128)S(1)} %get-tuple-element.56.owner_ref, bf16[2,4,160,2,1281]{4,3,2,1,0:T(2,128)(2,1)} %s_hbm.7, ...), custom_call_target="tpu_custom_call" | custom-call | flops 1007419392 | bytes 9838080 | tf_op jit(solution)/shard_map/legendre/pallas_call | solution.py:268
  36.6 0.4 collective-permute-start.7
  37.2 0.6 slice.51
  37.8 2.3 %collective-permute-start.8 = (f32[2,96,256]{2,1,0:T(8,128)}, f32[2,96,256]{2,1,0:T(8,128)S(1)}, u32[]{:S(2)}, u32[]{:S(2)}) collective-permute-start(f32[2,96,256]{2,1,0:T(8,128)} %get-tuple-element.96), channel_id=1, source_target_pairs={{0,2},{1,3},{2,0},{3,1},{4,6},{5,7},{6,4},{7,5},{8,10},{9,11},{10,... | collective-permute-start | bytes 589832 | tf_op jit(solution)/shard_map/ppermute | solution.py:537
  40.1 0.9 %collective-permute-start.9 = (f32[2,96,256]{2,1,0:T(8,128)}, f32[2,96,256]{2,1,0:T(8,128)S(1)}, u32[]{:S(2)}, u32[]{:S(2)}) collective-permute-start(f32[2,96,256]{2,1,0:T(8,128)} %get-tuple-element.97), channel_id=1, source_target_pairs={{0,3},{1,2},{2,1},{3,0},{4,7},{5,6},{6,5},{7,4},{8,11},{9,10},{10,... | collective-permute-start | bytes 589832 | tf_op jit(solution)/shard_map/ppermute | solution.py:537
  41.0 0.7 pad_add_fusion.2.refs_0_
  41.9 7.5 %legendre.7 = (f32[2,64,256]{2,1,0:T(8,128)S(1)}, f32[2,64,256]{2,1,0:T(8,128)S(1)}, f32[2,64,256]{2,1,0:T(8,128)S(1)}, f32[2,64,256]{2,1,0:T(8,128)}) custom-call(s32[640]{0:T(1024)S(1)} %copy-done.1, s32[1]{0:T(128)} %bitcast.here_ref, s32[16,128]{1,0:T(8,128)S(1)} %get-tuple-element.56.owner_ref, bf16[2,4,160,2,1281]{4,3,2,1,0:T(2,128)(2,1)} %s_hbm.7, ...), custom_call_target="tpu_custom_call" | custom-call | flops 671612928 | bytes 6558720 | tf_op jit(solution)/shard_map/legendre/pallas_call | solution.py:268
  49.5 2.2 %collective-permute-start.4 = (f32[2,64,256]{2,1,0:T(8,128)S(1)}, f32[2,64,256]{2,1,0:T(8,128)S(1)}, u32[]{:S(2)}, u32[]{:S(2)}) collective-permute-start(f32[2,64,256]{2,1,0:T(8,128)S(1)} %get-tuple-element.77), channel_id=1, source_target_pairs={{0,1},{1,0},{2,3},{3,2},{4,5},{5,4},{6,7},{7,6},{8,9},{9,8},{10,11... | collective-permute-start | bytes 393224 | tf_op jit(solution)/shard_map/ppermute | solution.py:537
  51.7 1.0 %collective-permute-start.5 = (f32[2,64,256]{2,1,0:T(8,128)S(1)}, f32[2,64,256]{2,1,0:T(8,128)S(1)}, u32[]{:S(2)}, u32[]{:S(2)}) collective-permute-start(f32[2,64,256]{2,1,0:T(8,128)S(1)} %get-tuple-element.78), channel_id=1, source_target_pairs={{0,2},{1,3},{2,0},{3,1},{4,6},{5,7},{6,4},{7,5},{8,10},{9,11},{10,... | collective-permute-start | bytes 393224 | tf_op jit(solution)/shard_map/ppermute | solution.py:537
  52.7 0.9 %tables.2 = (f32[192,8]{1,0:T(8,128)S(1)}, bf16[1024,192]{1,0:T(8,128)(2,1)S(1)}, bf16[1024,192]{1,0:T(8,128)(2,1)S(1)}, bf16[1024,192]{1,0:T(8,128)(2,1)S(1)}, bf16[1024,192]{1,0:T(8,128)(2,1)S(1)}) custom-call(s32[1,192]{1,0:T(1,128)S(1)} %bitcast.41), custom_call_target="tpu_custom_call" | custom-call | flops 6291456 | bytes 1572864 | tf_op jit(solution)/shard_map/tables/pallas_call | solution.py:367
  53.6 3.6 %tables.3 = (f32[1088,8]{1,0:T(8,128)S(1)}, bf16[1024,1088]{1,0:T(8,128)(2,1)S(1)}, bf16[1024,1088]{1,0:T(8,128)(2,1)S(1)}, bf16[1024,1088]{1,0:T(8,128)(2,1)S(1)}, bf16[1024,1088]{1,0:T(8,128)(2,1)S(1)}) custom-call(s32[1,1088]{1,0:T(1,128)S(1)} %reshape.44.waves_ref), custom_call_target="tpu_custom_call" | custom-call | flops 35651584 | bytes 8912896 | tf_op jit(solution)/shard_map/tables/pallas_call | solution.py:367
  57.3 1.2 %collective-permute-start.6 = (f32[2,64,256]{2,1,0:T(8,128)}, f32[2,64,256]{2,1,0:T(8,128)S(1)}, u32[]{:S(2)}, u32[]{:S(2)}) collective-permute-start(f32[2,64,256]{2,1,0:T(8,128)} %get-tuple-element.79), channel_id=1, source_target_pairs={{0,3},{1,2},{2,1},{3,0},{4,7},{5,6},{6,5},{7,4},{8,11},{9,10},{10,... | collective-permute-start | bytes 393224 | tf_op jit(solution)/shard_map/ppermute | solution.py:537
  58.5 9.9 %synthesis.2 = (f32[1024,512]{1,0:T(8,128)S(1)}, f32[1024,512]{1,0:T(8,128)S(1)}) custom-call(f32[1088,8]{1,0:T(8,128)S(1)} %get-tuple-element.81.refs_0_, bf16[1024,1088]{1,0:T(8,128)(2,1)S(1)} %get-tuple-element.82.refs_1_, bf16[1024,1088]{1,0:T(8,128)(2,1)S(1)} %get-tuple-element.83.refs_2_, bf16[1024,1088]{1,0:T(8,128)(2,1)S(1)} %get-tuple-element.84.refs_3_, ...), custom_call_target="tpu_custom_call" | custom-call | flops 6845104128 | bytes 8388608 | tf_op jit(solution)/shard_map/synthesis/pallas_call | solution.py:512
  68.4 0.5 collective-permute-done.5.refs_8_
  68.8 3.9 %synthesis.3 = (f32[16,128]{1,0:T(8,128)S(1)}, f32[16,128]{1,0:T(8,128)S(1)}, f32[16,128]{1,0:T(8,128)S(1)}, f32[16,128]{1,0:T(8,128)S(1)}) custom-call(s32[66]{0:T(128)S(1)} %pad_add_fusion.2.refs_0_, s32[1]{0:T(128)} %bitcast.3.refs_1_, f32[192,8]{1,0:T(8,128)S(1)} %get-tuple-element.72.refs_2_, bf16[1024,192]{1,0:T(8,128)(2,1)S(1)} %get-tuple-element.73.refs_3_, ...), custom_call_target="tpu_custom_call" | custom-call | flops 1207959552 | bytes 8388608 | tf_op jit(solution)/shard_map/synthesis/pallas_call | solution.py:512
  72.8 5.1 %collective-permute-start.10 = (f32[16,128]{1,0:T(8,128)S(1)}, f32[16,128]{1,0:T(8,128)S(1)}, u32[]{:S(2)}, u32[]{:S(2)}) collective-permute-start(f32[16,128]{1,0:T(8,128)S(1)} %get-tuple-element.101), channel_id=1, source_target_pairs={{0,4},{4,8},{8,12},{12,0},{1,5},{5,9},{9,13},{13,1},{2,6},{6,10},{... | collective-permute-start | bytes 24584 | tf_op jit(solution)/shard_map/ppermute | solution.py:533
  77.8 0.3 collective-permute-start.11
  78.1 0.2 collective-permute-start.12
  78.3 0.3 collective-permute-done.10.refs_1_
  78.6 1.7 %collective-permute-done.11.refs_2_ = f32[16,128]{1,0:T(8,128)S(1)} collective-permute-done((f32[16,128]{1,0:T(8,128)S(1)}, f32[16,128]{1,0:T(8,128)S(1)}, u32[]{:S(2)}, u32[]{:S(2)}) %collective-permute-start.11) | collective-permute-done | bytes 8224 | tf_op jit(solution)/shard_map/ppermute | solution.py:533
  80.3 0.8 %collective-permute-done.12.refs_3_ = f32[16,128]{1,0:T(8,128)S(1)} collective-permute-done((f32[16,128]{1,0:T(8,128)S(1)}, f32[16,128]{1,0:T(8,128)S(1)}, u32[]{:S(2)}, u32[]{:S(2)}) %collective-permute-start.12) | collective-permute-done | bytes 8224 | tf_op jit(solution)/shard_map/ppermute | solution.py:533
  81.2 0.7 final.1
  (29 shorter events, 0.7 us)
Async XLA Ops:
  0.6 0.7 copy-start
  1.3 0.7 copy-start.2
  9.0 17.6 %collective-permute-start = (f32[2,64,256]{2,1,0:T(8,128)S(1)}, f32[2,64,256]{2,1,0:T(8,128)S(1)}, u32[]{:S(2)}, u32[]{:S(2)}) collective-permute-start(f32[2,64,256]{2,1,0:T(8,128)S(1)} %get-tuple-element.62), channel_id=1, source_target_pairs={{0,2},{1,3},{2,0},{3,1},{4,6},{5,7},{6,4},{7,5},{8,10},{9,11},{10,... | collective-permute-start | bytes 393224 | tf_op jit(solution)/shard_map/ppermute | solution.py:537
  12.2 14.4 %collective-permute-start.1 = (f32[2,64,256]{2,1,0:T(8,128)}, f32[2,64,256]{2,1,0:T(8,128)S(1)}, u32[]{:S(2)}, u32[]{:S(2)}) collective-permute-start(f32[2,64,256]{2,1,0:T(8,128)} %get-tuple-element.63), channel_id=1, source_target_pairs={{0,3},{1,2},{2,1},{3,0},{4,7},{5,6},{6,5},{7,4},{8,11},{9,10},{10,... | collective-permute-start | bytes 393224 | tf_op jit(solution)/shard_map/ppermute | solution.py:537
  13.3 13.3 %copy-start.1 = (s32[640]{0:T(1024)S(1)}, s32[640]{0:T(1024)}, u32[]{:S(2)}) copy-start(s32[640]{0:T(1024)} %pair_ref.7) | copy-start | bytes 7684
  23.2 18.7 %collective-permute-start.2 = (f32[2,96,256]{2,1,0:T(8,128)}, f32[2,96,256]{2,1,0:T(8,128)S(1)}, u32[]{:S(2)}, u32[]{:S(2)}) collective-permute-start(f32[2,96,256]{2,1,0:T(8,128)} %get-tuple-element.67), channel_id=1, source_target_pairs={{0,2},{1,3},{2,0},{3,1},{4,6},{5,7},{6,4},{7,5},{8,10},{9,11},{10,... | collective-permute-start | bytes 589832 | tf_op jit(solution)/shard_map/ppermute | solution.py:537
  24.7 17.2 %collective-permute-start.3 = (f32[2,96,256]{2,1,0:T(8,128)}, f32[2,96,256]{2,1,0:T(8,128)S(1)}, u32[]{:S(2)}, u32[]{:S(2)}) collective-permute-start(f32[2,96,256]{2,1,0:T(8,128)} %get-tuple-element.68), channel_id=1, source_target_pairs={{0,3},{1,2},{2,1},{3,0},{4,7},{5,6},{6,5},{7,4},{8,11},{9,10},{10,... | collective-permute-start | bytes 589832 | tf_op jit(solution)/shard_map/ppermute | solution.py:537
  26.6 10.4 %copy-start.3 = (s32[2048]{0:T(1024)S(1)}, s32[2048]{0:T(1024)}, u32[]{:S(2)}) copy-start(s32[2048]{0:T(1024)} %param.9) | copy-start | bytes 24580
  36.6 21.9 %collective-permute-start.7 = (f32[2,256,256]{2,1,0:T(8,128)S(1)}, f32[2,256,256]{2,1,0:T(8,128)S(1)}, u32[]{:S(2)}, u32[]{:S(2)}) collective-permute-start(f32[2,256,256]{2,1,0:T(8,128)S(1)} %pad_maximum_fusion), channel_id=1, source_target_pairs={{0,1},{1,0},{2,3},{3,2},{4,5},{5,4},{6,7},{7,6},{8,9},{9,8},{10,11... | collective-permute-start | bytes 1572872 | tf_op jit(solution)/shard_map/ppermute | solution.py:537
  37.8 19.4 %collective-permute-start.8 = (f32[2,96,256]{2,1,0:T(8,128)}, f32[2,96,256]{2,1,0:T(8,128)S(1)}, u32[]{:S(2)}, u32[]{:S(2)}) collective-permute-start(f32[2,96,256]{2,1,0:T(8,128)} %get-tuple-element.96), channel_id=1, source_target_pairs={{0,2},{1,3},{2,0},{3,1},{4,6},{5,7},{6,4},{7,5},{8,10},{9,11},{10,... | collective-permute-start | bytes 589832 | tf_op jit(solution)/shard_map/ppermute | solution.py:537
  40.1 18.4 %collective-permute-start.9 = (f32[2,96,256]{2,1,0:T(8,128)}, f32[2,96,256]{2,1,0:T(8,128)S(1)}, u32[]{:S(2)}, u32[]{:S(2)}) collective-permute-start(f32[2,96,256]{2,1,0:T(8,128)} %get-tuple-element.97), channel_id=1, source_target_pairs={{0,3},{1,2},{2,1},{3,0},{4,7},{5,6},{6,5},{7,4},{8,11},{9,10},{10,... | collective-permute-start | bytes 589832 | tf_op jit(solution)/shard_map/ppermute | solution.py:537
  49.5 18.9 %collective-permute-start.4 = (f32[2,64,256]{2,1,0:T(8,128)S(1)}, f32[2,64,256]{2,1,0:T(8,128)S(1)}, u32[]{:S(2)}, u32[]{:S(2)}) collective-permute-start(f32[2,64,256]{2,1,0:T(8,128)S(1)} %get-tuple-element.77), channel_id=1, source_target_pairs={{0,1},{1,0},{2,3},{3,2},{4,5},{5,4},{6,7},{7,6},{8,9},{9,8},{10,11... | collective-permute-start | bytes 393224 | tf_op jit(solution)/shard_map/ppermute | solution.py:537
  51.7 17.1 %collective-permute-start.5 = (f32[2,64,256]{2,1,0:T(8,128)S(1)}, f32[2,64,256]{2,1,0:T(8,128)S(1)}, u32[]{:S(2)}, u32[]{:S(2)}) collective-permute-start(f32[2,64,256]{2,1,0:T(8,128)S(1)} %get-tuple-element.78), channel_id=1, source_target_pairs={{0,2},{1,3},{2,0},{3,1},{4,6},{5,7},{6,4},{7,5},{8,10},{9,11},{10,... | collective-permute-start | bytes 393224 | tf_op jit(solution)/shard_map/ppermute | solution.py:537
  57.3 11.6 %collective-permute-start.6 = (f32[2,64,256]{2,1,0:T(8,128)}, f32[2,64,256]{2,1,0:T(8,128)S(1)}, u32[]{:S(2)}, u32[]{:S(2)}) collective-permute-start(f32[2,64,256]{2,1,0:T(8,128)} %get-tuple-element.79), channel_id=1, source_target_pairs={{0,3},{1,2},{2,1},{3,0},{4,7},{5,6},{6,5},{7,4},{8,11},{9,10},{10,... | collective-permute-start | bytes 393224 | tf_op jit(solution)/shard_map/ppermute | solution.py:537
  72.8 5.8 %collective-permute-start.10 = (f32[16,128]{1,0:T(8,128)S(1)}, f32[16,128]{1,0:T(8,128)S(1)}, u32[]{:S(2)}, u32[]{:S(2)}) collective-permute-start(f32[16,128]{1,0:T(8,128)S(1)} %get-tuple-element.101), channel_id=1, source_target_pairs={{0,4},{4,8},{8,12},{12,0},{1,5},{5,9},{9,13},{13,1},{2,6},{6,10},{... | collective-permute-start | bytes 24584 | tf_op jit(solution)/shard_map/ppermute | solution.py:533
  77.8 2.5 %collective-permute-start.11 = (f32[16,128]{1,0:T(8,128)S(1)}, f32[16,128]{1,0:T(8,128)S(1)}, u32[]{:S(2)}, u32[]{:S(2)}) collective-permute-start(f32[16,128]{1,0:T(8,128)S(1)} %get-tuple-element.102), channel_id=1, source_target_pairs={{0,8},{4,12},{8,0},{12,4},{1,9},{5,13},{9,1},{13,5},{2,10},{6,14},... | collective-permute-start | bytes 24584 | tf_op jit(solution)/shard_map/ppermute | solution.py:533
  78.1 3.1 %collective-permute-start.12 = (f32[16,128]{1,0:T(8,128)S(1)}, f32[16,128]{1,0:T(8,128)S(1)}, u32[]{:S(2)}, u32[]{:S(2)}) collective-permute-start(f32[16,128]{1,0:T(8,128)S(1)} %get-tuple-element.103), channel_id=1, source_target_pairs={{0,12},{4,0},{8,4},{12,8},{1,13},{5,1},{9,5},{13,9},{2,14},{6,2},{... | collective-permute-start | bytes 24584 | tf_op jit(solution)/shard_map/ppermute | solution.py:533

commit v4 on v3

--- a/solution.py
+++ b/solution.py
@@ -494,7 +494,7 @@
 
 
 def synthesis(made, pieces, sources, held, closing, lon, regions, wide, share, starts, here):
-    block = min(512, lon // 2)
+    block = min(1024, lon // 2)
     depth = made[0].shape[0]
     counts = tuple((piece.shape[1], source) for piece, source in zip(pieces, sources))
     width = pieces[0].shape[2]
@@ -608,8 +608,8 @@
         for chunk in range(late + 1)
     ]
     stages = (
-        own + swapped[:-1] + sum(across[:late], []),
-        swapped[-1:] + across[late],
+        own[:late] + swapped[:-1] + sum(across[:late], []),
+        own[late:] + swapped[-1:] + across[late],
     )
     held = None
     waves = [jnp.concatenate([w for _, _, found in stage for w in found]) for stage in stages]

time: 82.1 us -> 79.8 us (0.972)
  Pallas kernels: 53.4 us -> 50.3 us
  waiting for transfers between devices: 3.37 us -> 6.27 us
  starting transfers between devices: 20.2 us -> 17.6 us
    ppermute x10, waiting for transfers between devices: 0.51 us -> 3.41 us  [swap(): return lax.ppermute(x, axis, [(i, i ^ step) for i in range(count)])]
    pallas_call x2, Pallas kernels: 13.8 us -> 11 us  [synthesis(): pl.pallas_call(functools.partial(synthesis_kernel, counts, fresh, closing...]
    ppermute x3, starting transfers between devices: 5.53 us -> 2.87 us  [shift(): lax.ppermute(x, axis, [(i, (i + step) % count) for i in range(count)])]
  transfers between devices with their start and end apart: 13 -> 13, of which waited for: 4 -> 4; matrix products, arithmetic and copies ran while one was open for 3% -> 3% of each run, Pallas kernels for 51% -> 49%
where the time goes in v4:
time: 79.8 us; the launch traced here: 79.1 us
  Pallas kernels  50.3 us (63%)
  starting transfers between devices  17.6 us (22%)
  waiting for transfers between devices  6.27 us (8%)
  local copies, waits for them, and re-layouts  3.05 us (4%)
  other arithmetic  1.02 us (1%)
  between operations  0.81 us (1%)
    pallas_call x4, Pallas kernels, legendre_sums(): pl.pallas_call(functools.partial(legendre_kernel, first_unit, units, part...  34.4 us
    ppermute x10, starting transfers between devices, swap(): return lax.ppermute(x, axis, [(i, i ^ step) for i in range(count)])  14.7 us
    pallas_call x2, Pallas kernels, synthesis(): pl.pallas_call(functools.partial(synthesis_kernel, counts, fresh, closing...  11 us
    pallas_call x2, Pallas kernels, tables(): pl.pallas_call(functools.partial(tables_kernel, lon, top), in_specs=[held...  4.31 us
    ppermute x10, waiting for transfers between devices, swap(): return lax.ppermute(x, axis, [(i, i ^ step) for i in range(count)])  3.41 us
    ppermute x3, starting transfers between devices, shift(): lax.ppermute(x, axis, [(i, (i + step) % count) for i in range(count)])  2.87 us
    ppermute x3, waiting for transfers between devices, shift(): lax.ppermute(x, axis, [(i, (i + step) % count) for i in range(count)])  2.86 us
  transfers between devices with their start and end apart: 13, of which 4 were waited for; matrix products, arithmetic and copies ran while one was open for 3% of the time, Pallas kernels for 49%

profile of v4, /device:TPU:1, one launch (start us, length us, event | category | flops | bytes accessed | tf_op | source)
XLA Modules:
  0.0 79.1 jit_solution(12415855968707682061)
XLA Ops:
  0.6 0.7 copy-done
  1.3 0.7 copy-done.2
  2.0 7.0 %legendre.4 = (f32[2,64,256]{2,1,0:T(8,128)S(1)}, f32[2,64,256]{2,1,0:T(8,128)S(1)}, f32[2,64,256]{2,1,0:T(8,128)S(1)}, f32[2,64,256]{2,1,0:T(8,128)}, s32[16,128]{1,0:T(8,128)S(1)}) custom-call(s32[640]{0:T(1024)S(1)} %copy-done, s32[1]{0:T(128)} %bitcast.here_ref, s32[1,128]{1,0:T(1,128)S(1)} %bitcast.44, bf16[2,4,160,2,1281]{4,3,2,1,0:T(2,128)(2,1)} %s_hbm.7, ...), custom_call_target="tpu_custom_call" | custom-call | flops 671612928 | bytes 6558720 | tf_op jit(solution)/shard_map/legendre/pallas_call | solution.py:268
  9.0 3.2 %collective-permute-start = (f32[2,64,256]{2,1,0:T(8,128)S(1)}, f32[2,64,256]{2,1,0:T(8,128)S(1)}, u32[]{:S(2)}, u32[]{:S(2)}) collective-permute-start(f32[2,64,256]{2,1,0:T(8,128)S(1)} %get-tuple-element.62), channel_id=1, source_target_pairs={{0,2},{1,3},{2,0},{3,1},{4,6},{5,7},{6,4},{7,5},{8,10},{9,11},{10,... | collective-permute-start | bytes 393224 | tf_op jit(solution)/shard_map/ppermute | solution.py:537
  12.2 1.1 %collective-permute-start.1 = (f32[2,64,256]{2,1,0:T(8,128)}, f32[2,64,256]{2,1,0:T(8,128)S(1)}, u32[]{:S(2)}, u32[]{:S(2)}) collective-permute-start(f32[2,64,256]{2,1,0:T(8,128)} %get-tuple-element.63), channel_id=1, source_target_pairs={{0,3},{1,2},{2,1},{3,0},{4,7},{5,6},{6,5},{7,4},{8,11},{9,10},{10,... | collective-permute-start | bytes 393224 | tf_op jit(solution)/shard_map/ppermute | solution.py:537
  13.3 9.9 %legendre.5 = (f32[2,96,256]{2,1,0:T(8,128)S(1)}, f32[2,96,256]{2,1,0:T(8,128)S(1)}, f32[2,96,256]{2,1,0:T(8,128)}, f32[2,96,256]{2,1,0:T(8,128)}) custom-call(s32[640]{0:T(1024)S(1)} %copy-done, s32[1]{0:T(128)} %bitcast.here_ref, s32[16,128]{1,0:T(8,128)S(1)} %get-tuple-element.56.owner_ref, bf16[2,4,160,2,1281]{4,3,2,1,0:T(2,128)(2,1)} %s_hbm.7, ...), custom_call_target="tpu_custom_call" | custom-call | flops 1007419392 | bytes 9838080 | tf_op jit(solution)/shard_map/legendre/pallas_call | solution.py:268
  23.2 1.4 %collective-permute-start.2 = (f32[2,96,256]{2,1,0:T(8,128)}, f32[2,96,256]{2,1,0:T(8,128)S(1)}, u32[]{:S(2)}, u32[]{:S(2)}) collective-permute-start(f32[2,96,256]{2,1,0:T(8,128)} %get-tuple-element.67), channel_id=1, source_target_pairs={{0,2},{1,3},{2,0},{3,1},{4,6},{5,7},{6,4},{7,5},{8,10},{9,11},{10,... | collective-permute-start | bytes 589832 | tf_op jit(solution)/shard_map/ppermute | solution.py:537
  24.7 0.9 %collective-permute-start.3 = (f32[2,96,256]{2,1,0:T(8,128)}, f32[2,96,256]{2,1,0:T(8,128)S(1)}, u32[]{:S(2)}, u32[]{:S(2)}) collective-permute-start(f32[2,96,256]{2,1,0:T(8,128)} %get-tuple-element.68), channel_id=1, source_target_pairs={{0,3},{1,2},{2,1},{3,0},{4,7},{5,6},{6,5},{7,4},{8,11},{9,10},{10,... | collective-permute-start | bytes 589832 | tf_op jit(solution)/shard_map/ppermute | solution.py:537
  25.8 0.2 reshape.42
  26.0 0.6 gather_fusion
  26.6 9.9 %legendre.6 = (f32[2,96,256]{2,1,0:T(8,128)S(1)}, f32[2,96,256]{2,1,0:T(8,128)S(1)}, f32[2,96,256]{2,1,0:T(8,128)}, f32[2,96,256]{2,1,0:T(8,128)}) custom-call(s32[640]{0:T(1024)S(1)} %copy-done.1, s32[1]{0:T(128)} %bitcast.here_ref, s32[16,128]{1,0:T(8,128)S(1)} %get-tuple-element.56.owner_ref, bf16[2,4,160,2,1281]{4,3,2,1,0:T(2,128)(2,1)} %s_hbm.7, ...), custom_call_target="tpu_custom_call" | custom-call | flops 1007419392 | bytes 9838080 | tf_op jit(solution)/shard_map/legendre/pallas_call | solution.py:268
  36.6 0.4 collective-permute-start.7
  37.2 0.6 slice.51
  37.8 2.3 %collective-permute-start.8 = (f32[2,96,256]{2,1,0:T(8,128)}, f32[2,96,256]{2,1,0:T(8,128)S(1)}, u32[]{:S(2)}, u32[]{:S(2)}) collective-permute-start(f32[2,96,256]{2,1,0:T(8,128)} %get-tuple-element.96), channel_id=1, source_target_pairs={{0,2},{1,3},{2,0},{3,1},{4,6},{5,7},{6,4},{7,5},{8,10},{9,11},{10,... | collective-permute-start | bytes 589832 | tf_op jit(solution)/shard_map/ppermute | solution.py:537
  40.1 0.9 %collective-permute-start.9 = (f32[2,96,256]{2,1,0:T(8,128)}, f32[2,96,256]{2,1,0:T(8,128)S(1)}, u32[]{:S(2)}, u32[]{:S(2)}) collective-permute-start(f32[2,96,256]{2,1,0:T(8,128)} %get-tuple-element.97), channel_id=1, source_target_pairs={{0,3},{1,2},{2,1},{3,0},{4,7},{5,6},{6,5},{7,4},{8,11},{9,10},{10,... | collective-permute-start | bytes 589832 | tf_op jit(solution)/shard_map/ppermute | solution.py:537
  41.0 0.7 pad_add_fusion.2.refs_0_
  41.9 7.6 %legendre.7 = (f32[2,64,256]{2,1,0:T(8,128)S(1)}, f32[2,64,256]{2,1,0:T(8,128)S(1)}, f32[2,64,256]{2,1,0:T(8,128)S(1)}, f32[2,64,256]{2,1,0:T(8,128)}) custom-call(s32[640]{0:T(1024)S(1)} %copy-done.1, s32[1]{0:T(128)} %bitcast.here_ref, s32[16,128]{1,0:T(8,128)S(1)} %get-tuple-element.56.owner_ref, bf16[2,4,160,2,1281]{4,3,2,1,0:T(2,128)(2,1)} %s_hbm.7, ...), custom_call_target="tpu_custom_call" | custom-call | flops 671612928 | bytes 6558720 | tf_op jit(solution)/shard_map/legendre/pallas_call | solution.py:268
  49.5 2.2 %collective-permute-start.4 = (f32[2,64,256]{2,1,0:T(8,128)S(1)}, f32[2,64,256]{2,1,0:T(8,128)S(1)}, u32[]{:S(2)}, u32[]{:S(2)}) collective-permute-start(f32[2,64,256]{2,1,0:T(8,128)S(1)} %get-tuple-element.77), channel_id=1, source_target_pairs={{0,1},{1,0},{2,3},{3,2},{4,5},{5,4},{6,7},{7,6},{8,9},{9,8},{10,11... | collective-permute-start | bytes 393224 | tf_op jit(solution)/shard_map/ppermute | solution.py:537
  51.7 1.0 %collective-permute-start.5 = (f32[2,64,256]{2,1,0:T(8,128)S(1)}, f32[2,64,256]{2,1,0:T(8,128)S(1)}, u32[]{:S(2)}, u32[]{:S(2)}) collective-permute-start(f32[2,64,256]{2,1,0:T(8,128)S(1)} %get-tuple-element.78), channel_id=1, source_target_pairs={{0,2},{1,3},{2,0},{3,1},{4,6},{5,7},{6,4},{7,5},{8,10},{9,11},{10,... | collective-permute-start | bytes 393224 | tf_op jit(solution)/shard_map/ppermute | solution.py:537
  52.7 0.9 %tables.2 = (f32[256,8]{1,0:T(8,128)S(1)}, bf16[1024,256]{1,0:T(8,128)(2,1)S(1)}, bf16[1024,256]{1,0:T(8,128)(2,1)S(1)}, bf16[1024,256]{1,0:T(8,128)(2,1)S(1)}, bf16[1024,256]{1,0:T(8,128)(2,1)S(1)}) custom-call(s32[1,256]{1,0:T(1,128)S(1)} %bitcast.43), custom_call_target="tpu_custom_call" | custom-call | flops 8388608 | bytes 2097152 | tf_op jit(solution)/shard_map/tables/pallas_call | solution.py:367
  53.6 3.4 %tables.3 = (f32[1024,8]{1,0:T(8,128)S(1)}, bf16[1024,1024]{1,0:T(8,128)(2,1)S(1)}, bf16[1024,1024]{1,0:T(8,128)(2,1)S(1)}, bf16[1024,1024]{1,0:T(8,128)(2,1)S(1)}, bf16[1024,1024]{1,0:T(8,128)(2,1)S(1)}) custom-call(s32[1,1024]{1,0:T(1,128)S(1)} %bitcast.42), custom_call_target="tpu_custom_call" | custom-call | flops 33554432 | bytes 8388608 | tf_op jit(solution)/shard_map/tables/pallas_call | solution.py:367
  57.0 1.2 %collective-permute-start.6 = (f32[2,64,256]{2,1,0:T(8,128)}, f32[2,64,256]{2,1,0:T(8,128)S(1)}, u32[]{:S(2)}, u32[]{:S(2)}) collective-permute-start(f32[2,64,256]{2,1,0:T(8,128)} %get-tuple-element.79), channel_id=1, source_target_pairs={{0,3},{1,2},{2,1},{3,0},{4,7},{5,6},{6,5},{7,4},{8,11},{9,10},{10,... | collective-permute-start | bytes 393224 | tf_op jit(solution)/shard_map/ppermute | solution.py:537
  58.2 7.2 %synthesis.2 = (f32[1024,512]{1,0:T(8,128)S(1)}, f32[1024,512]{1,0:T(8,128)S(1)}) custom-call(f32[1024,8]{1,0:T(8,128)S(1)} %get-tuple-element.81.refs_0_, bf16[1024,1024]{1,0:T(8,128)(2,1)S(1)} %get-tuple-element.82.refs_1_, bf16[1024,1024]{1,0:T(8,128)(2,1)S(1)} %get-tuple-element.83.refs_2_, bf16[1024,1024]{1,0:T(8,128)(2,1)S(1)} %get-tuple-element.84.refs_3_, ...), custom_call_target="tpu_custom_call" | custom-call | flops 6442450944 | bytes 8388608 | tf_op jit(solution)/shard_map/synthesis/pallas_call | solution.py:512
  65.5 3.4 %collective-permute-done.5.refs_9_ = f32[2,64,256]{2,1,0:T(8,128)S(1)} collective-permute-done((f32[2,64,256]{2,1,0:T(8,128)S(1)}, f32[2,64,256]{2,1,0:T(8,128)S(1)}, u32[]{:S(2)}, u32[]{:S(2)}) %collective-permute-start.5) | collective-permute-done | bytes 131104 | tf_op jit(solution)/shard_map/ppermute | solution.py:537
  68.8 3.8 %synthesis.3 = (f32[16,128]{1,0:T(8,128)S(1)}, f32[16,128]{1,0:T(8,128)S(1)}, f32[16,128]{1,0:T(8,128)S(1)}, f32[16,128]{1,0:T(8,128)S(1)}) custom-call(s32[66]{0:T(128)S(1)} %pad_add_fusion.2.refs_0_, s32[1]{0:T(128)} %bitcast.3.refs_1_, f32[256,8]{1,0:T(8,128)S(1)} %get-tuple-element.72.refs_2_, bf16[1024,256]{1,0:T(8,128)(2,1)S(1)} %get-tuple-element.73.refs_3_, ...), custom_call_target="tpu_custom_call" | custom-call | flops 1610612736 | bytes 8388608 | tf_op jit(solution)/shard_map/synthesis/pallas_call | solution.py:512
  72.6 2.4 %collective-permute-start.10 = (f32[16,128]{1,0:T(8,128)S(1)}, f32[16,128]{1,0:T(8,128)S(1)}, u32[]{:S(2)}, u32[]{:S(2)}) collective-permute-start(f32[16,128]{1,0:T(8,128)S(1)} %get-tuple-element.101), channel_id=1, source_target_pairs={{0,4},{4,8},{8,12},{12,0},{1,5},{5,9},{9,13},{13,1},{2,6},{6,10},{... | collective-permute-start | bytes 24584 | tf_op jit(solution)/shard_map/ppermute | solution.py:533
  75.0 0.3 collective-permute-start.11
  75.3 0.2 collective-permute-start.12
  75.5 0.3 collective-permute-done.10.refs_1_
  75.8 1.7 %collective-permute-done.11.refs_2_ = f32[16,128]{1,0:T(8,128)S(1)} collective-permute-done((f32[16,128]{1,0:T(8,128)S(1)}, f32[16,128]{1,0:T(8,128)S(1)}, u32[]{:S(2)}, u32[]{:S(2)}) %collective-permute-start.11) | collective-permute-done | bytes 8224 | tf_op jit(solution)/shard_map/ppermute | solution.py:533
  77.5 0.8 %collective-permute-done.12.refs_3_ = f32[16,128]{1,0:T(8,128)S(1)} collective-permute-done((f32[16,128]{1,0:T(8,128)S(1)}, f32[16,128]{1,0:T(8,128)S(1)}, u32[]{:S(2)}, u32[]{:S(2)}) %collective-permute-start.12) | collective-permute-done | bytes 8224 | tf_op jit(solution)/shard_map/ppermute | solution.py:533
  78.4 0.7 final.1
  (28 shorter events, 0.7 us)
Async XLA Ops:
  0.6 0.7 copy-start
  1.3 0.7 copy-start.2
  9.0 17.6 %collective-permute-start = (f32[2,64,256]{2,1,0:T(8,128)S(1)}, f32[2,64,256]{2,1,0:T(8,128)S(1)}, u32[]{:S(2)}, u32[]{:S(2)}) collective-permute-start(f32[2,64,256]{2,1,0:T(8,128)S(1)} %get-tuple-element.62), channel_id=1, source_target_pairs={{0,2},{1,3},{2,0},{3,1},{4,6},{5,7},{6,4},{7,5},{8,10},{9,11},{10,... | collective-permute-start | bytes 393224 | tf_op jit(solution)/shard_map/ppermute | solution.py:537
  12.2 14.4 %collective-permute-start.1 = (f32[2,64,256]{2,1,0:T(8,128)}, f32[2,64,256]{2,1,0:T(8,128)S(1)}, u32[]{:S(2)}, u32[]{:S(2)}) collective-permute-start(f32[2,64,256]{2,1,0:T(8,128)} %get-tuple-element.63), channel_id=1, source_target_pairs={{0,3},{1,2},{2,1},{3,0},{4,7},{5,6},{6,5},{7,4},{8,11},{9,10},{10,... | collective-permute-start | bytes 393224 | tf_op jit(solution)/shard_map/ppermute | solution.py:537
  13.3 13.3 %copy-start.1 = (s32[640]{0:T(1024)S(1)}, s32[640]{0:T(1024)}, u32[]{:S(2)}) copy-start(s32[640]{0:T(1024)} %pair_ref.7) | copy-start | bytes 7684
  23.2 18.7 %collective-permute-start.2 = (f32[2,96,256]{2,1,0:T(8,128)}, f32[2,96,256]{2,1,0:T(8,128)S(1)}, u32[]{:S(2)}, u32[]{:S(2)}) collective-permute-start(f32[2,96,256]{2,1,0:T(8,128)} %get-tuple-element.67), channel_id=1, source_target_pairs={{0,2},{1,3},{2,0},{3,1},{4,6},{5,7},{6,4},{7,5},{8,10},{9,11},{10,... | collective-permute-start | bytes 589832 | tf_op jit(solution)/shard_map/ppermute | solution.py:537
  24.7 17.2 %collective-permute-start.3 = (f32[2,96,256]{2,1,0:T(8,128)}, f32[2,96,256]{2,1,0:T(8,128)S(1)}, u32[]{:S(2)}, u32[]{:S(2)}) collective-permute-start(f32[2,96,256]{2,1,0:T(8,128)} %get-tuple-element.68), channel_id=1, source_target_pairs={{0,3},{1,2},{2,1},{3,0},{4,7},{5,6},{6,5},{7,4},{8,11},{9,10},{10,... | collective-permute-start | bytes 589832 | tf_op jit(solution)/shard_map/ppermute | solution.py:537
  26.6 10.4 %copy-start.3 = (s32[2048]{0:T(1024)S(1)}, s32[2048]{0:T(1024)}, u32[]{:S(2)}) copy-start(s32[2048]{0:T(1024)} %param.9) | copy-start | bytes 24580
  36.6 21.7 %collective-permute-start.7 = (f32[2,256,256]{2,1,0:T(8,128)S(1)}, f32[2,256,256]{2,1,0:T(8,128)S(1)}, u32[]{:S(2)}, u32[]{:S(2)}) collective-permute-start(f32[2,256,256]{2,1,0:T(8,128)S(1)} %pad_maximum_fusion), channel_id=1, source_target_pairs={{0,1},{1,0},{2,3},{3,2},{4,5},{5,4},{6,7},{7,6},{8,9},{9,8},{10,11... | collective-permute-start | bytes 1572872 | tf_op jit(solution)/shard_map/ppermute | solution.py:537
  37.8 19.2 %collective-permute-start.8 = (f32[2,96,256]{2,1,0:T(8,128)}, f32[2,96,256]{2,1,0:T(8,128)S(1)}, u32[]{:S(2)}, u32[]{:S(2)}) collective-permute-start(f32[2,96,256]{2,1,0:T(8,128)} %get-tuple-element.96), channel_id=1, source_target_pairs={{0,2},{1,3},{2,0},{3,1},{4,6},{5,7},{6,4},{7,5},{8,10},{9,11},{10,... | collective-permute-start | bytes 589832 | tf_op jit(solution)/shard_map/ppermute | solution.py:537
  40.1 18.1 %collective-permute-start.9 = (f32[2,96,256]{2,1,0:T(8,128)}, f32[2,96,256]{2,1,0:T(8,128)S(1)}, u32[]{:S(2)}, u32[]{:S(2)}) collective-permute-start(f32[2,96,256]{2,1,0:T(8,128)} %get-tuple-element.97), channel_id=1, source_target_pairs={{0,3},{1,2},{2,1},{3,0},{4,7},{5,6},{6,5},{7,4},{8,11},{9,10},{10,... | collective-permute-start | bytes 589832 | tf_op jit(solution)/shard_map/ppermute | solution.py:537
  49.5 16.0 %collective-permute-start.4 = (f32[2,64,256]{2,1,0:T(8,128)S(1)}, f32[2,64,256]{2,1,0:T(8,128)S(1)}, u32[]{:S(2)}, u32[]{:S(2)}) collective-permute-start(f32[2,64,256]{2,1,0:T(8,128)S(1)} %get-tuple-element.77), channel_id=1, source_target_pairs={{0,1},{1,0},{2,3},{3,2},{4,5},{5,4},{6,7},{7,6},{8,9},{9,8},{10,11... | collective-permute-start | bytes 393224 | tf_op jit(solution)/shard_map/ppermute | solution.py:537
  51.7 17.2 %collective-permute-start.5 = (f32[2,64,256]{2,1,0:T(8,128)S(1)}, f32[2,64,256]{2,1,0:T(8,128)S(1)}, u32[]{:S(2)}, u32[]{:S(2)}) collective-permute-start(f32[2,64,256]{2,1,0:T(8,128)S(1)} %get-tuple-element.78), channel_id=1, source_target_pairs={{0,2},{1,3},{2,0},{3,1},{4,6},{5,7},{6,4},{7,5},{8,10},{9,11},{10,... | collective-permute-start | bytes 393224 | tf_op jit(solution)/shard_map/ppermute | solution.py:537
  57.0 11.8 %collective-permute-start.6 = (f32[2,64,256]{2,1,0:T(8,128)}, f32[2,64,256]{2,1,0:T(8,128)S(1)}, u32[]{:S(2)}, u32[]{:S(2)}) collective-permute-start(f32[2,64,256]{2,1,0:T(8,128)} %get-tuple-element.79), channel_id=1, source_target_pairs={{0,3},{1,2},{2,1},{3,0},{4,7},{5,6},{6,5},{7,4},{8,11},{9,10},{10,... | collective-permute-start | bytes 393224 | tf_op jit(solution)/shard_map/ppermute | solution.py:537
  72.6 3.2 %collective-permute-start.10 = (f32[16,128]{1,0:T(8,128)S(1)}, f32[16,128]{1,0:T(8,128)S(1)}, u32[]{:S(2)}, u32[]{:S(2)}) collective-permute-start(f32[16,128]{1,0:T(8,128)S(1)} %get-tuple-element.101), channel_id=1, source_target_pairs={{0,4},{4,8},{8,12},{12,0},{1,5},{5,9},{9,13},{13,1},{2,6},{6,10},{... | collective-permute-start | bytes 24584 | tf_op jit(solution)/shard_map/ppermute | solution.py:533
  75.0 2.5 %collective-permute-start.11 = (f32[16,128]{1,0:T(8,128)S(1)}, f32[16,128]{1,0:T(8,128)S(1)}, u32[]{:S(2)}, u32[]{:S(2)}) collective-permute-start(f32[16,128]{1,0:T(8,128)S(1)} %get-tuple-element.102), channel_id=1, source_target_pairs={{0,8},{4,12},{8,0},{12,4},{1,9},{5,13},{9,1},{13,5},{2,10},{6,14},... | collective-permute-start | bytes 24584 | tf_op jit(solution)/shard_map/ppermute | solution.py:533
  75.3 3.1 %collective-permute-start.12 = (f32[16,128]{1,0:T(8,128)S(1)}, f32[16,128]{1,0:T(8,128)S(1)}, u32[]{:S(2)}, u32[]{:S(2)}) collective-permute-start(f32[16,128]{1,0:T(8,128)S(1)} %get-tuple-element.103), channel_id=1, source_target_pairs={{0,12},{4,0},{8,4},{12,8},{1,13},{5,1},{9,5},{13,9},{2,14},{6,2},{... | collective-permute-start | bytes 24584 | tf_op jit(solution)/shard_map/ppermute | solution.py:533
